TPU v7x, 256 devices: a whole 4x4x8 slice. The times are simulated.
256 devices in a mesh: lat: 8 (over y, x_hi), lon: 32 (over z, x_lo, core).
Axes of the slice: x: 4 (x_hi: 2, x_lo: 2; x = x_hi * 2 + x_lo), y: 4, z: 8, core: 2. Of those that a mesh axis runs over, the one named last changes fastest.
Arguments:
- checkpoint: float32 [4, 8, 256, 2048], P(None, None, 'lon', 'lat'), may hold values from -6 to 6
- courant_lon: float32 [8, 256, 2048], P(None, 'lon', 'lat'), may hold values from -0.6 to 0.6
- courant_lat: float32 [8, 256, 2048], P(None, 'lon', 'lat'), may hold values from -0.6 to 0.6
- mixing: float32 [8, 256, 2048], P(None, 'lon', 'lat'), may hold values from 0.05 to 5
- limiter_flags: int32 [4, 4, 8, 256, 2048], P(None, None, None, 'lon', 'lat'), may hold values from 0 to 8
- column_weights: float32 [8], replicated, may hold values from 0.1 to 1
- observations: float32 [4, 4, 256, 2048], P(None, None, 'lon', 'lat'), may hold values from -12 to 12
- misfit_weight: float32 [4, 256, 2048], P(None, 'lon', 'lat'), may hold values from 0.2 to 2
Outputs:
- final_state: float32 [4, 8, 256, 2048], P(None, None, 'lon', 'lat')
- gradient: float32 [4, 8, 256, 2048], P(None, None, 'lon', 'lat')
Inputs may be any that keep to these rules, and one draw needn't show every extreme that they name: `limiter_flags`: each value holds the longitude branch as its remainder by 3 and the latitude branch as its quotient by 3.
All inputs are finite; a program needn't handle non-finite values.
Results may differ from a plain program's by a relative error of at most 0.0003.
Values sent between devices are 32-bit elements; how exact they have to be, the bound alone decides.
No kernel may reach another device: no remote copies, remote signals or barrier semaphores. Data moves between devices by JAX's collectives and lax.ppermute only.
A program may use at most 64 MiB of HBM per device.

v0:
```python
import jax
import jax.numpy as jnp
from jax import lax
from jax.experimental import pallas as pl
from jax.experimental.pallas import tpu as pltpu
from jax.sharding import PartitionSpec as P

TRACERS, LEVELS, SUBSTEPS = 4, 8, 4
COLS, ROWS, EDGE, LANES = 8, 256, 16, 128
WIDE = ROWS + LANES
STATE = TRACERS * LEVELS
LIMIT = 50 * 1024 * 1024
CORNER = 23


def lane_ids():
    return lax.broadcasted_iota(jnp.int32, (COLS, LANES), 1)


def col_ids(lanes=LANES):
    return lax.broadcasted_iota(jnp.int32, (COLS, lanes), 0)


def pack(ck, cl, ct, mx, fl, obs, mw, to_right, to_left, to_north, to_south):
    lane, col = (lane_ids(), col_ids(ROWS))
    to_right[0:STATE] = ck[...]
    to_left[0:STATE] = ck[...]
    for place, field in ((32, cl), (40, ct), (48, mx)):
        to_right[place : place + LEVELS] = field[...]
        to_left[place : place + LEVELS] = field[...]

    def flags(substep, row):
        return fl[substep * STATE + row].astype(jnp.float32)

    @pl.loop(0, TRACERS)
    def _(tracer):
        for level in range(LEVELS):
            row = tracer * LEVELS + level
            one, two, three, four = [flags(s, row) for s in range(SUBSTEPS)]
            to_right[56 + row] = jnp.where(col >= 1, one, pltpu.roll(four, 1, 0))
            to_right[88 + row] = jnp.where(col >= 3, two, pltpu.roll(three, 3, 0))
            to_left[56 + row] = jnp.where(col < 6, one, pltpu.roll(three, 6, 0))
            if level < 4:
                other = flags(1, row + 4)
                to_left[88 + tracer * 4 + level] = jnp.where(col < 4, two, pltpu.roll(other, 4, 0))

    def strips(place, read, count):
        north = jnp.zeros((COLS, LANES), jnp.float32)
        south = north
        for k in range(count):
            here = (lane >= EDGE * k) & (lane < EDGE * (k + 1))
            whole = read(k)
            north = jnp.where(here, pltpu.roll(whole[:, LANES:], (EDGE * (k + 1)) % LANES, 1), north)
            south = jnp.where(here, pltpu.roll(whole[:, :LANES], EDGE * k, 1), south)
        to_north[place] = north
        to_south[place] = south

    @pl.loop(0, TRACERS)
    def _(tracer):
        strips(tracer, lambda k: ck[tracer * LEVELS + k], LEVELS)

    for place, field in ((4, cl), (5, ct), (6, mx)):
        strips(place, lambda k, field=field: field[k], LEVELS)

    @pl.loop(0, SUBSTEPS * TRACERS)
    def _(block):
        strips(7 + block, lambda k: fl[block * LEVELS + k].astype(jnp.float32), LEVELS)

    for half in range(2):
        strips(23 + half, lambda k, half=half: obs[half * 8 + k], 8)
    strips(25, lambda k: mw[k], TRACERS)


def behind(value, axis):
    return pltpu.roll(value, 1, axis)


def ahead(value, axis):
    return pltpu.roll(value, value.shape[axis] - 1, axis)


def weights(branch, low, high, c_minus, c_both, slope):
    first = jnp.where(branch >= high, c_minus, jnp.where(branch >= low, c_both, c_minus))
    return first, jnp.where(branch >= high, slope, 0.0)


def sweep(value, courant, first, second, axis):
    step = ahead(value, axis) - value
    farther = jnp.where(courant >= 0.0, behind(step, axis), ahead(step, axis))
    flux = courant * value + first * step + second * farther
    return value - flux + behind(flux, axis)


def sweep_back(value, courant, first, second, axis):
    step = ahead(value, axis) - value
    reach = second * step
    forward = jnp.where(courant >= 0.0, reach, 0.0)
    total = first * step + ahead(forward, axis) + behind(reach - forward, axis)
    return value + courant * step + behind(total, axis) - total


def slopes(courant):
    c_minus = jnp.minimum(courant, 0.0)
    size = jnp.abs(courant)
    slope = 0.5 * size * (1.0 - size)
    return c_minus, c_minus + slope, slope


def window(
    ck, cl, ct, mx, fl, obs, mw, cw, from_left, from_right, north, south, left_corner, right_corner,
    final, grad, grad_left, grad_right,
    q, temp, lon_code, lat_code, cx, cy, cy_minus, cy_both, cy_slope, inv, elim, ratio, obs_w, mw_w, force,
):
    lane, col = (lane_ids(), col_ids())
    col_w = col_ids(WIDE)

    def tail(n_tile, s_tile, k):
        n_part = pltpu.roll(n_tile, (LANES - EDGE * k) % LANES, 1)
        s_part = pltpu.roll(s_tile, (LANES - EDGE - EDGE * k) % LANES, 1)
        return jnp.where(lane < EDGE, n_part, jnp.where(lane >= LANES - EDGE, s_part, 0.0))

    def own_tail(place, k):
        return tail(north[place], south[place], k)

    def left_tail(place, k):
        return tail(left_corner[place], left_corner[CORNER + place], k)

    def right_tail(place, k):
        return tail(right_corner[place], right_corner[CORNER + place], k)

    def wide(main, end):
        return jnp.concatenate([main, end], axis=1)

    def squeeze(right, left):
        return jnp.where(col_w < 4, right, left)

    @pl.loop(0, TRACERS)
    def _(tracer):
        for level in range(LEVELS):
            row = tracer * LEVELS + level
            q[row, 0] = wide(ck[row], own_tail(tracer, level))
            q[row, 1] = wide(from_right[row], right_tail(tracer, level))
            q[row, 2] = wide(from_left[row], left_tail(tracer, level))

    lane_w = lax.broadcasted_iota(jnp.int32, (COLS, WIDE), 1)
    last = lax.axis_index("lat") == lax.axis_size("lat") - 1
    pole = (lane_w == ROWS - 1) & last
    carry = [None] * 4
    for level in range(LEVELS):
        def blocks(field, place):
            at = 32 + 8 * (place - 4) + level
            own = wide(field[level], own_tail(place, level))
            right = wide(from_right[at], right_tail(place, level))
            left = wide(from_left[at], left_tail(place, level))
            return [own, right, left, squeeze(right, left)]

        for k, value in enumerate(blocks(cl, 4)):
            cx[level, k] = value
        for k, value in enumerate(blocks(ct, 5)):
            value = jnp.where(pole, 0.0, value)
            c_minus, c_both, slope = slopes(value)
            cy[level, k] = value
            cy_minus[level, k] = c_minus
            cy_both[level, k] = c_both
            cy_slope[level, k] = slope
        for k, value in enumerate(blocks(mx, 6)):
            coupling = value if level < LEVELS - 1 else jnp.zeros_like(value)
            pivot = 1.0 + coupling
            if level > 0:
                above, above_ratio = carry[k]
                pivot = pivot + above - above * above_ratio
            inverse = 1.0 / pivot
            inv[level, k] = inverse
            ratio[level, k] = coupling * inverse
            elim[level, k] = above * inverse if level > 0 else jnp.zeros_like(value)
            carry[k] = (coupling, coupling * inverse)

    for k in range(SUBSTEPS * TRACERS):
        obs_w[k] = wide(obs[k], own_tail(23 + k // 8, k % 8))
    for k in range(TRACERS):
        mw_w[k] = wide(mw[k], own_tail(25, k))

    def put_codes(substep, row, blocks, lat_blocks):
        for k, value in enumerate(blocks):
            lon_code[substep, row, k] = value - jnp.where(value >= 6.0, 6.0, jnp.where(value >= 3.0, 3.0, 0.0))
        for k, value in enumerate(lat_blocks):
            lat_code[substep, row, k] = value

    @pl.loop(0, TRACERS)
    def _(tracer):
        for level in range(LEVELS):
            row = tracer * LEVELS + level
            own = [
                wide(fl[s * STATE + row].astype(jnp.float32), own_tail(7 + s * TRACERS + tracer, level))
                for s in range(SUBSTEPS)
            ]
            r_tail = [right_tail(7 + s * TRACERS + tracer, level) for s in range(3)]
            l_tail = [left_tail(7 + s * TRACERS + tracer, level) for s in range(SUBSTEPS)]
            l_a, l_b = (from_left[56 + row], from_left[88 + row])
            r_a = from_right[56 + row]
            r_b = from_right[88 + tracer * 4 + level % 4]
            if level >= 4:
                r_b = pltpu.roll(r_b, 4, 0)
            one = [own[0], wide(r_a, r_tail[0]), wide(l_a, l_tail[0])]
            put_codes(0, row, one, one)
            two = [own[1], wide(r_b, r_tail[1]), wide(l_b, l_tail[1])]
            put_codes(1, row, two, [own[1], squeeze(two[1], two[2])])
            three = [
                own[2],
                squeeze(wide(pltpu.roll(r_a, 2, 0), r_tail[2]), wide(pltpu.roll(l_b, 5, 0), l_tail[2])),
            ]
            put_codes(2, row, three, three)
            four = [own[3], wide(pltpu.roll(l_a, 7, 0), l_tail[3])]
            put_codes(3, row, four, [own[3]])

    def lon_pass(substep, source, target, slots, back, chunks=3):
        code_slots = slots if len(slots) == 3 else (0, 1)

        @pl.loop(0, LEVELS)
        def _(level):
            for chunk in range(chunks):
                at = slice(chunk * LANES, (chunk + 1) * LANES)
                c = jnp.concatenate([cx[level, k, :, at] for k in slots], axis=0)
                c_minus, c_both, slope = slopes(c)
                for tracer in range(TRACERS):
                    row = tracer * LEVELS + level
                    value = jnp.concatenate([source[row, k, :, at] for k in slots], axis=0)
                    code = jnp.concatenate([lon_code[substep, row, k, :, at] for k in code_slots], axis=0)
                    first, second = weights(code, 1.0, 2.0, c_minus, c_both, slope)
                    out = (sweep_back if back else sweep)(value, c, first, second, 0)
                    for n, k in enumerate(slots):
                        target(row, k, at, out[n * COLS : (n + 1) * COLS])

    def to_temp(row, k, at, value):
        temp[row, k, :, at] = value

    def to_q(row, k, at, value):
        q[row, k, :, at] = value

    def to_grad(row, k, at, value):
        (grad, grad_right, grad_left)[k][row, :, at] = value

    def lat_weights(substep, row, level, code_slot, slot):
        return weights(
            lat_code[substep, row, code_slot], 3.0, 6.0, cy_minus[level, slot], cy_both[level, slot], cy_slope[level, slot]
        )

    def solve(read, slot):
        forward = []
        for level in range(LEVELS):
            running = read(level) * inv[level, slot]
            if level > 0:
                running = running + elim[level, slot] * forward[-1]
            forward.append(running)
        results = [forward[-1]]
        for level in range(LEVELS - 2, -1, -1):
            results.append(forward[level] + ratio[level, slot] * results[-1])
        return results[::-1]

    def lat_and_mix(substep, slots):
        @pl.loop(0, TRACERS)
        def _(tracer):
            for slot in slots:
                code_slot = 1 if slot == 3 else slot

                def read(level):
                    row = tracer * LEVELS + level
                    if slot == 3 and substep == 1:
                        value = squeeze(temp[row, 1], temp[row, 2])
                    else:
                        value = temp[row, slot]
                    first, second = lat_weights(substep, row, level, code_slot, slot)
                    return sweep(value, cy[level, slot], first, second, 1)

                results = solve(read, slot)
                if slot == 0:
                    column = cw[0] * results[0]
                    for level in range(1, LEVELS):
                        column = column + cw[level] * results[level]
                    at = substep * TRACERS + tracer
                    force[at] = mw_w[tracer] * (column - obs_w[at])
                for level in range(LEVELS):
                    row = tracer * LEVELS + level
                    if substep == SUBSTEPS - 1:
                        final[row] = results[level][:, :ROWS]
                    else:
                        q[row, slot] = results[level]

    def mix_and_lat(substep, slots):
        @pl.loop(0, TRACERS)
        def _(tracer):
            for slot in slots:
                code_slot = 1 if slot == 3 else slot

                def read(level):
                    row = tracer * LEVELS + level
                    if slot != 0:
                        return q[row, slot]
                    added = cw[level] * force[substep * TRACERS + tracer]
                    return added if substep == SUBSTEPS - 1 else q[row, slot] + added

                results = solve(read, slot)
                for level in range(LEVELS):
                    row = tracer * LEVELS + level
                    first, second = lat_weights(substep, row, level, code_slot, slot)
                    out = sweep_back(results[level], cy[level, slot], first, second, 1)
                    if slot == 3 and substep == 1:
                        temp[row, 1] = jnp.where(col_w < 4, out, 0.0)
                        temp[row, 2] = jnp.where(col_w < 4, 0.0, out)
                    else:
                        temp[row, slot] = out
                    if substep == SUBSTEPS - 1:
                        temp[row, 3] = jnp.zeros_like(out)

    three, two = ((0, 1, 2), (0, 3))
    lon_pass(0, q, to_temp, three, False)
    lat_and_mix(0, three)
    lon_pass(1, q, to_temp, three, False)
    lat_and_mix(1, two)
    lon_pass(2, q, to_temp, two, False)
    lat_and_mix(2, two)
    lon_pass(3, q, to_temp, two, False)
    lat_and_mix(3, (0,))
    mix_and_lat(3, (0,))
    lon_pass(3, temp, to_q, two, True)
    mix_and_lat(2, two)
    lon_pass(2, temp, to_q, two, True)
    mix_and_lat(1, two)
    lon_pass(1, temp, to_q, three, True)
    mix_and_lat(0, three)
    lon_pass(0, temp, to_grad, three, True, 2)


def whole_spec(count):
    return [pl.BlockSpec(memory_space=pltpu.VMEM)] * count


def shards(
    checkpoint, courant_lon, courant_lat, mixing, limiter_flags, column_weights, observations, misfit_weight
):
    f32 = jnp.float32
    lat, lon = (lax.axis_size("lat"), lax.axis_size("lon"))
    east = [(i, (i + 1) % lon) for i in range(lon)]
    west = [(j, i) for i, j in east]
    up = [(i, i + 1) for i in range(lat - 1)]
    down = [(j, i) for i, j in up]
    own = (
        checkpoint.reshape((STATE, COLS, ROWS)),
        courant_lon,
        courant_lat,
        mixing,
        limiter_flags.reshape((SUBSTEPS * STATE, COLS, ROWS)),
        observations.reshape((SUBSTEPS * TRACERS, COLS, ROWS)),
        misfit_weight,
    )
    params = pltpu.CompilerParams(vmem_limit_bytes=LIMIT)
    to_right, to_left, to_north, to_south = pl.pallas_call(
        pack,
        out_shape=(
            jax.ShapeDtypeStruct((120, COLS, ROWS), f32),
            jax.ShapeDtypeStruct((104, COLS, ROWS), f32),
            jax.ShapeDtypeStruct((26, COLS, LANES), f32),
            jax.ShapeDtypeStruct((26, COLS, LANES), f32),
        ),
        in_specs=whole_spec(7),
        out_specs=tuple(whole_spec(4)),
        compiler_params=params,
        name="pack",
    )(*own)
    from_left = lax.ppermute(to_right, "lon", east)
    from_right = lax.ppermute(to_left, "lon", west)
    south = lax.ppermute(to_north, "lat", up)
    north = lax.ppermute(to_south, "lat", down)
    corner = jnp.concatenate([north[:CORNER], south[:CORNER]], axis=0)
    left_corner = lax.ppermute(corner, "lon", east)
    right_corner = lax.ppermute(corner, "lon", west)
    small = pltpu.VMEM((LEVELS, 4, COLS, WIDE), f32)
    block = jax.ShapeDtypeStruct((STATE, COLS, ROWS), f32)
    final, grad, grad_left, grad_right = pl.pallas_call(
        window,
        out_shape=(block,) * 4,
        in_specs=whole_spec(7) + [pl.BlockSpec(memory_space=pltpu.SMEM)] + whole_spec(6),
        out_specs=tuple(whole_spec(4)),
        scratch_shapes=[
            pltpu.VMEM((STATE, 4, COLS, WIDE), f32),
            pltpu.VMEM((STATE, 4, COLS, WIDE), f32),
            pltpu.VMEM((SUBSTEPS, STATE, 3, COLS, WIDE), f32),
            pltpu.VMEM((SUBSTEPS, STATE, 3, COLS, WIDE), f32),
        ]
        + [small] * 8
        + [
            pltpu.VMEM((SUBSTEPS * TRACERS, COLS, WIDE), f32),
            pltpu.VMEM((TRACERS, COLS, WIDE), f32),
            pltpu.VMEM((SUBSTEPS * TRACERS, COLS, WIDE), f32),
        ],
        compiler_params=params,
        name="window",
    )(*own, column_weights, from_left, from_right, north, south, left_corner, right_corner)
    grad = grad + lax.ppermute(grad_left, "lon", west) + lax.ppermute(grad_right, "lon", east)
    return (final.reshape(checkpoint.shape), grad.reshape(checkpoint.shape))


def solution(mesh):
    return jax.shard_map(
        shards,
        mesh=mesh,
        in_specs=(
            P(None, None, "lon", "lat"),
            P(None, "lon", "lat"),
            P(None, "lon", "lat"),
            P(None, "lon", "lat"),
            P(None, None, None, "lon", "lat"),
            P(),
            P(None, None, "lon", "lat"),
            P(None, "lon", "lat"),
        ),
        out_specs=(P(None, None, "lon", "lat"), P(None, None, "lon", "lat")),
        check_vma=False,
    )
```

profile of v0, /device:TPU:24, one launch (start us, length us, event | category | flops | bytes accessed | tf_op | source)
XLA Modules:
  0.0 85.2 jit_solution(4215245258875664818)
XLA Ops:
  0.6 0.0 copy-start
  0.6 1.2 %copy-done = s32[4,4,8,8,256]{4,3,2,1,0:T(8,128)S(1)} copy-done((s32[4,4,8,8,256]{4,3,2,1,0:T(8,128)S(1)}, s32[4,4,8,8,256]{4,3,2,1,0:T(8,128)}, u32[]{:S(2)}) %copy-start) | copy-done | bytes 1048600
  1.9 0.0 copy-start.1
  1.9 0.9 %copy-done.1 = f32[4,8,8,256]{3,2,1,0:T(8,128)S(1)} copy-done((f32[4,8,8,256]{3,2,1,0:T(8,128)S(1)}, f32[4,8,8,256]{3,2,1,0:T(8,128)}, u32[]{:S(2)}) %copy-start.1) | copy-done | bytes 262168
  2.8 0.0 copy-start.2
  2.8 0.9 %copy-done.2 = f32[4,4,8,256]{3,2,1,0:T(8,128)S(1)} copy-done((f32[4,4,8,256]{3,2,1,0:T(8,128)S(1)}, f32[4,4,8,256]{3,2,1,0:T(8,128)}, u32[]{:S(2)}) %copy-start.2) | copy-done | bytes 131096
  3.7 0.0 copy-start.5
  3.7 0.8 copy-done.5
  4.6 0.0 copy-start.6
  4.6 0.8 copy-done.6
  5.4 0.0 copy-start.7
  5.4 0.8 copy-done.7
  6.2 0.0 copy-start.8
  6.2 0.8 copy-done.8
  7.0 2.0 %pack.1 = (f32[120,8,256]{2,1,0:T(8,128)S(1)}, f32[104,8,256]{2,1,0:T(8,128)S(1)}, f32[26,8,128]{2,1,0:T(8,128)S(1)}, f32[26,8,128]{2,1,0:T(8,128)S(1)}) custom-call(f32[32,8,256]{2,1,0:T(8,128)S(1)} %bitcast.7, f32[8,8,256]{2,1,0:T(8,128)S(1)} %copy-done.5, f32[8,8,256]{2,1,0:T(8,128)S(1)} %copy-done.6, f32[8,8,256]{2,1,0:T(8,128)S(1)} %copy-done.7, ...), custom_call_target="tpu_custom_call" | custom-call | tf_op jit(solution)/shard_map/pack/pallas_call | solution.py:357
  9.0 0.1 collective-permute-start
  9.1 6.3 %collective-permute-start.1 = (f32[104,8,256]{2,1,0:T(8,128)S(1)}, f32[104,8,256]{2,1,0:T(8,128)S(1)}, u32[]{:S(2)}, u32[]{:S(2)}) collective-permute-start(f32[104,8,256]{2,1,0:T(8,128)S(1)} %get-tuple-element.11), channel_id=1, source_target_pairs={{1,0},{2,1},{3,2},{4,3},{5,4},{6,5},{7,6},{8,7},{9,8},{10,9},{11,1... | collective-permute-start | bytes 2555912 | tf_op jit(solution)/shard_map/ppermute | solution.py:371
  15.4 4.8 %collective-permute-start.2 = (f32[26,8,128]{2,1,0:T(8,128)S(1)}, f32[26,8,128]{2,1,0:T(8,128)S(1)}, u32[]{:S(2)}, u32[]{:S(2)}) collective-permute-start(f32[26,8,128]{2,1,0:T(8,128)S(1)} %get-tuple-element.12), channel_id=1, source_target_pairs={{32,0},{64,32},{96,64},{128,96},{160,128},{192,160},{224,192},{33,... | collective-permute-start | bytes 319496 | tf_op jit(solution)/shard_map/ppermute | solution.py:373
  20.2 2.5 %collective-permute-start.3 = (f32[26,8,128]{2,1,0:T(8,128)S(1)}, f32[26,8,128]{2,1,0:T(8,128)S(1)}, u32[]{:S(2)}, u32[]{:S(2)}) collective-permute-start(f32[26,8,128]{2,1,0:T(8,128)S(1)} %get-tuple-element.13), channel_id=1, source_target_pairs={{0,32},{32,64},{64,96},{96,128},{128,160},{160,192},{192,224},{1,3... | collective-permute-start | bytes 319496 | tf_op jit(solution)/shard_map/ppermute | solution.py:372
  22.7 6.5 %collective-permute-done.2.north = f32[26,8,128]{2,1,0:T(8,128)S(1)} collective-permute-done((f32[26,8,128]{2,1,0:T(8,128)S(1)}, f32[26,8,128]{2,1,0:T(8,128)S(1)}, u32[]{:S(2)}, u32[]{:S(2)}) %collective-permute-start.2) | collective-permute-done | bytes 106528 | tf_op jit(solution)/shard_map/ppermute | solution.py:373
  29.2 0.0 copy-start.3
  29.2 0.6 copy-done.3
  29.8 1.8 %collective-permute-done.3.south = f32[26,8,128]{2,1,0:T(8,128)S(1)} collective-permute-done((f32[26,8,128]{2,1,0:T(8,128)S(1)}, f32[26,8,128]{2,1,0:T(8,128)S(1)}, u32[]{:S(2)}, u32[]{:S(2)}) %collective-permute-start.3) | collective-permute-done | bytes 106528 | tf_op jit(solution)/shard_map/ppermute | solution.py:372
  31.6 0.0 slice-start
  31.7 0.9 %slice-done = f32[23,8,128]{2,1,0:T(8,128)S(1)} async-done(((f32[26,8,128]{2,1,0:T(8,128)}), f32[23,8,128]{2,1,0:T(8,128)S(1)}, s32[]{:S(2)}) %slice-start) | async-done | bytes 94232 | tf_op jit(solution)/shard_map/slice | solution.py:374
  32.5 0.0 copy-start.4
  32.5 0.0 copy-start.9
  32.5 0.0 copy-start.10
  32.6 3.9 %collective-permute-start.5 = (f32[46,8,128]{2,1,0:T(8,128)S(1)}, f32[46,8,128]{2,1,0:T(8,128)S(1)}, u32[]{:S(2)}, u32[]{:S(2)}) collective-permute-start(f32[46,8,128]{2,1,0:T(8,128)S(1)} %pad_maximum_fusion), channel_id=1, source_target_pairs={{1,0},{2,1},{3,2},{4,3},{5,4},{6,5},{7,6},{8,7},{9,8},{10,9},{11,1... | collective-permute-start | bytes 565256 | tf_op jit(solution)/shard_map/ppermute | solution.py:376
  36.4 3.1 %collective-permute-start.4 = (f32[46,8,128]{2,1,0:T(8,128)S(1)}, f32[46,8,128]{2,1,0:T(8,128)S(1)}, u32[]{:S(2)}, u32[]{:S(2)}) collective-permute-start(f32[46,8,128]{2,1,0:T(8,128)S(1)} %pad_maximum_fusion), channel_id=1, source_target_pairs={{0,1},{1,2},{2,3},{3,4},{4,5},{5,6},{6,7},{7,8},{8,9},{9,10},{10,1... | collective-permute-start | bytes 565256 | tf_op jit(solution)/shard_map/ppermute | solution.py:375
  39.5 0.8 collective-permute-done.5.right_corner
  40.4 9.0 %collective-permute-done.4.left_corner = f32[46,8,128]{2,1,0:T(8,128)S(1)} collective-permute-done((f32[46,8,128]{2,1,0:T(8,128)S(1)}, f32[46,8,128]{2,1,0:T(8,128)S(1)}, u32[]{:S(2)}, u32[]{:S(2)}) %collective-permute-start.4) | collective-permute-done | bytes 188448 | tf_op jit(solution)/shard_map/ppermute | solution.py:375
  49.4 0.0 collective-permute-done.1.from_right
  49.4 0.0 collective-permute-done.from_left
  49.4 0.0 copy-done.4
  49.4 0.0 copy-done.9
  49.4 0.0 copy-done.10
  49.5 26.9 %window.1 = (f32[32,8,256]{2,1,0:T(8,128)}, f32[32,8,256]{2,1,0:T(8,128)S(1)}, f32[32,8,256]{2,1,0:T(8,128)S(1)}, f32[32,8,256]{2,1,0:T(8,128)S(1)}) custom-call(f32[32,8,256]{2,1,0:T(8,128)S(1)} %bitcast.8, f32[8,8,256]{2,1,0:T(8,128)S(1)} %copy-done.5, f32[8,8,256]{2,1,0:T(8,128)S(1)} %copy-done.6, f32[8,8,256]{2,1,0:T(8,128)S(1)} %copy-done.7, ...), custom_call_target="tpu_custom_call" | custom-call | tf_op jit(solution)/shard_map/window/pallas_call | solution.py:379
  76.3 0.0 collective-permute-start.6
  76.3 0.5 collective-permute-start.7
  76.8 3.4 %collective-permute-done.6 = f32[32,8,256]{2,1,0:T(8,128)S(1)} collective-permute-done((f32[32,8,256]{2,1,0:T(8,128)S(1)}, f32[32,8,256]{2,1,0:T(8,128)S(1)}, u32[]{:S(2)}, u32[]{:S(2)}) %collective-permute-start.6) | collective-permute-done | bytes 262176 | tf_op jit(solution)/shard_map/ppermute | solution.py:399
  80.2 4.2 %collective-permute-done.7 = f32[32,8,256]{2,1,0:T(8,128)S(1)} collective-permute-done((f32[32,8,256]{2,1,0:T(8,128)S(1)}, f32[32,8,256]{2,1,0:T(8,128)S(1)}, u32[]{:S(2)}, u32[]{:S(2)}) %collective-permute-start.7) | collective-permute-done | bytes 262176 | tf_op jit(solution)/shard_map/ppermute | solution.py:399
  84.5 0.8 add_add_fusion
  (2 shorter events, 0.0 us)
Async XLA Ops:
  0.6 1.2 %copy-start = (s32[4,4,8,8,256]{4,3,2,1,0:T(8,128)S(1)}, s32[4,4,8,8,256]{4,3,2,1,0:T(8,128)}, u32[]{:S(2)}) copy-start(s32[4,4,8,8,256]{4,3,2,1,0:T(8,128)} %param.12) | copy-start | bytes 3145732
  1.9 0.9 %copy-start.1 = (f32[4,8,8,256]{3,2,1,0:T(8,128)S(1)}, f32[4,8,8,256]{3,2,1,0:T(8,128)}, u32[]{:S(2)}) copy-start(f32[4,8,8,256]{3,2,1,0:T(8,128)} %param.8) | copy-start | bytes 786436
  2.8 0.9 %copy-start.2 = (f32[4,4,8,256]{3,2,1,0:T(8,128)S(1)}, f32[4,4,8,256]{3,2,1,0:T(8,128)}, u32[]{:S(2)}) copy-start(f32[4,4,8,256]{3,2,1,0:T(8,128)} %param.14) | copy-start | bytes 393220
  3.7 0.8 copy-start.5
  4.6 0.8 copy-start.6
  5.4 0.8 copy-start.7
  6.2 0.8 copy-start.8
  9.0 40.5 %collective-permute-start = (f32[120,8,256]{2,1,0:T(8,128)S(1)}, f32[120,8,256]{2,1,0:T(8,128)S(1)}, u32[]{:S(2)}, u32[]{:S(2)}) collective-permute-start(f32[120,8,256]{2,1,0:T(8,128)S(1)} %get-tuple-element.10), channel_id=1, source_target_pairs={{0,1},{1,2},{2,3},{3,4},{4,5},{5,6},{6,7},{7,8},{8,9},{9,10},{10,1... | collective-permute-start | bytes 2949128 | tf_op jit(solution)/shard_map/ppermute | solution.py:370
  9.1 40.4 %collective-permute-start.1 = (f32[104,8,256]{2,1,0:T(8,128)S(1)}, f32[104,8,256]{2,1,0:T(8,128)S(1)}, u32[]{:S(2)}, u32[]{:S(2)}) collective-permute-start(f32[104,8,256]{2,1,0:T(8,128)S(1)} %get-tuple-element.11), channel_id=1, source_target_pairs={{1,0},{2,1},{3,2},{4,3},{5,4},{6,5},{7,6},{8,7},{9,8},{10,9},{11,1... | collective-permute-start | bytes 2555912 | tf_op jit(solution)/shard_map/ppermute | solution.py:371
  15.4 13.8 %collective-permute-start.2 = (f32[26,8,128]{2,1,0:T(8,128)S(1)}, f32[26,8,128]{2,1,0:T(8,128)S(1)}, u32[]{:S(2)}, u32[]{:S(2)}) collective-permute-start(f32[26,8,128]{2,1,0:T(8,128)S(1)} %get-tuple-element.12), channel_id=1, source_target_pairs={{32,0},{64,32},{96,64},{128,96},{160,128},{192,160},{224,192},{33,... | collective-permute-start | bytes 319496 | tf_op jit(solution)/shard_map/ppermute | solution.py:373
  20.2 11.5 %collective-permute-start.3 = (f32[26,8,128]{2,1,0:T(8,128)S(1)}, f32[26,8,128]{2,1,0:T(8,128)S(1)}, u32[]{:S(2)}, u32[]{:S(2)}) collective-permute-start(f32[26,8,128]{2,1,0:T(8,128)S(1)} %get-tuple-element.13), channel_id=1, source_target_pairs={{0,32},{32,64},{64,96},{96,128},{128,160},{160,192},{192,224},{1,3... | collective-permute-start | bytes 319496 | tf_op jit(solution)/shard_map/ppermute | solution.py:372
  29.2 0.6 copy-start.3
  31.6 0.9 %slice-start = ((f32[26,8,128]{2,1,0:T(8,128)}), f32[23,8,128]{2,1,0:T(8,128)S(1)}, s32[]{:S(2)}) async-start(f32[26,8,128]{2,1,0:T(8,128)} %copy-done.3), calls=%async_computation | async-start | bytes 188416 | tf_op jit(solution)/shard_map/slice | solution.py:374
  32.5 16.9 %copy-start.4 = (f32[26,8,128]{2,1,0:T(8,128)S(1)}, f32[26,8,128]{2,1,0:T(8,128)}, u32[]{:S(2)}) copy-start(f32[26,8,128]{2,1,0:T(8,128)} %copy-done.3) | copy-start | bytes 319492
  32.5 16.9 %copy-start.9 = (f32[4,8,256]{2,1,0:T(8,128)S(1)}, f32[4,8,256]{2,1,0:T(8,128)}, u32[]{:S(2)}) copy-start(f32[4,8,256]{2,1,0:T(8,128)} %mw.3) | copy-start | bytes 98308
  32.5 16.9 %copy-start.10 = (f32[8]{0:T(128)S(1)}, f32[8]{0:T(128)}, u32[]{:S(2)}) copy-start(f32[8]{0:T(128)} %cw.1) | copy-start | bytes 100
  32.6 7.8 %collective-permute-start.5 = (f32[46,8,128]{2,1,0:T(8,128)S(1)}, f32[46,8,128]{2,1,0:T(8,128)S(1)}, u32[]{:S(2)}, u32[]{:S(2)}) collective-permute-start(f32[46,8,128]{2,1,0:T(8,128)S(1)} %pad_maximum_fusion), channel_id=1, source_target_pairs={{1,0},{2,1},{3,2},{4,3},{5,4},{6,5},{7,6},{8,7},{9,8},{10,9},{11,1... | collective-permute-start | bytes 565256 | tf_op jit(solution)/shard_map/ppermute | solution.py:376
  36.4 13.0 %collective-permute-start.4 = (f32[46,8,128]{2,1,0:T(8,128)S(1)}, f32[46,8,128]{2,1,0:T(8,128)S(1)}, u32[]{:S(2)}, u32[]{:S(2)}) collective-permute-start(f32[46,8,128]{2,1,0:T(8,128)S(1)} %pad_maximum_fusion), channel_id=1, source_target_pairs={{0,1},{1,2},{2,3},{3,4},{4,5},{5,6},{6,7},{7,8},{8,9},{9,10},{10,1... | collective-permute-start | bytes 565256 | tf_op jit(solution)/shard_map/ppermute | solution.py:375
  76.3 3.9 %collective-permute-start.6 = (f32[32,8,256]{2,1,0:T(8,128)S(1)}, f32[32,8,256]{2,1,0:T(8,128)S(1)}, u32[]{:S(2)}, u32[]{:S(2)}) collective-permute-start(f32[32,8,256]{2,1,0:T(8,128)S(1)} %get-tuple-element.16), channel_id=1, source_target_pairs={{1,0},{2,1},{3,2},{4,3},{5,4},{6,5},{7,6},{8,7},{9,8},{10,9},{11,1... | collective-permute-start | bytes 786440 | tf_op jit(solution)/shard_map/ppermute | solution.py:399
  76.3 8.1 %collective-permute-start.7 = (f32[32,8,256]{2,1,0:T(8,128)S(1)}, f32[32,8,256]{2,1,0:T(8,128)S(1)}, u32[]{:S(2)}, u32[]{:S(2)}) collective-permute-start(f32[32,8,256]{2,1,0:T(8,128)S(1)} %get-tuple-element.17), channel_id=1, source_target_pairs={{0,1},{1,2},{2,3},{3,4},{4,5},{5,6},{6,7},{7,8},{8,9},{9,10},{10,1... | collective-permute-start | bytes 786440 | tf_op jit(solution)/shard_map/ppermute | solution.py:399
where the time goes:
time: 85.7 us; the launch traced here: 85.2 us
  Pallas kernels  28.8 us (34%)
  waiting for transfers between devices  25.8 us (30%)
  starting transfers between devices  21.2 us (25%)
  local copies, waits for them, and re-layouts  7.89 us (9%)
    pallas_call x1, Pallas kernels, shards(): pl.pallas_call(window, out_shape=(block,) * 4, in_specs=whole_spec(7) + [...  26.9 us
    ppermute x1, waiting for transfers between devices, shards(): left_corner = lax.ppermute(corner, 'lon', east)  9.05 us
    unnamed x22, local copies, waits for them, and re-layouts  7 us
    ppermute x1, waiting for transfers between devices, shards(): north = lax.ppermute(to_south, 'lat', down)  6.47 us
    ppermute x1, starting transfers between devices, shards(): from_right = lax.ppermute(to_left, 'lon', west)  6.3 us
    ppermute x1, starting transfers between devices, shards(): north = lax.ppermute(to_south, 'lat', down)  4.81 us
    ppermute x1, waiting for transfers between devices, shards(): lax.ppermute(grad_right, 'lon', east)  4.25 us
    ppermute x1, starting transfers between devices, shards(): right_corner = lax.ppermute(corner, 'lon', west)  3.87 us
  transfers between devices with their start and end apart: 8, of which 6 were waited for; matrix products, arithmetic and copies ran while one was open for 0% of the time, Pallas kernels for 0%

commit v1 on v0

v1 whole, which is shorter than its diff:
```python
import jax
import jax.numpy as jnp
from jax import lax
from jax.experimental import pallas as pl
from jax.experimental.pallas import tpu as pltpu
from jax.sharding import PartitionSpec as P

TRACERS, LEVELS, SUBSTEPS = 4, 8, 4
PAIR = 2
COLS, ROWS, EDGE, LANES = 8, 256, 16, 128
STATE = TRACERS * LEVELS
HALF = PAIR * LEVELS
LIMIT = 40 * 1024 * 1024
CORNER = 23


def lane_ids():
    return lax.broadcasted_iota(jnp.int32, (COLS, LANES), 1)


def col_ids(lanes=LANES):
    return lax.broadcasted_iota(jnp.int32, (COLS, lanes), 0)


def pack(*refs):
    hbm, (right_a, right_b, left_a, left_b, to_north, to_south), own, sems = (refs[:7], refs[7:13], refs[13:20], refs[20])
    copies = [pltpu.make_async_copy(hbm[k], own[k], sems.at[k]) for k in range(7)]
    for copy in copies:
        copy.start()
    for copy in copies:
        copy.wait()
    ck, cl, ct, mx, fl, obs, mw = own
    lane, col = (lane_ids(), col_ids(ROWS))
    for half, (to_right, to_left) in enumerate(((right_a, left_a), (right_b, left_b))):
        to_right[0:HALF] = ck[half * HALF : (half + 1) * HALF]
        to_left[0:HALF] = ck[half * HALF : (half + 1) * HALF]

        @pl.loop(0, PAIR)
        def _(tracer):
            for level in range(LEVELS):
                row = tracer * LEVELS + level
                one, two, three, four = [
                    fl[s * STATE + half * HALF + row].astype(jnp.float32) for s in range(SUBSTEPS)
                ]
                to_right[HALF + row] = jnp.where(col >= 1, one, pltpu.roll(four, 1, 0))
                to_right[2 * HALF + row] = jnp.where(col >= 3, two, pltpu.roll(three, 3, 0))
                to_left[HALF + row] = jnp.where(col < 6, one, pltpu.roll(three, 6, 0))
                if level < 4:
                    other = fl[STATE + half * HALF + row + 4].astype(jnp.float32)
                    to_left[2 * HALF + tracer * 4 + level] = jnp.where(col < 4, two, pltpu.roll(other, 4, 0))

    for k, field in enumerate((cl, ct, mx)):
        right_a[3 * HALF + 8 * k : 3 * HALF + 8 * k + 8] = field[...]
        left_a[40 + 8 * k : 48 + 8 * k] = field[...]

    def strips(place, read, count):
        north = jnp.zeros((COLS, LANES), jnp.float32)
        south = north
        for k in range(count):
            here = (lane >= EDGE * k) & (lane < EDGE * (k + 1))
            whole = read(k)
            north = jnp.where(here, pltpu.roll(whole[:, LANES:], (EDGE * (k + 1)) % LANES, 1), north)
            south = jnp.where(here, pltpu.roll(whole[:, :LANES], EDGE * k, 1), south)
        to_north[place] = north
        to_south[place] = south

    @pl.loop(0, TRACERS)
    def _(tracer):
        strips(tracer, lambda k: ck[tracer * LEVELS + k], LEVELS)

    for place, field in ((4, cl), (5, ct), (6, mx)):
        strips(place, lambda k, field=field: field[k], LEVELS)

    @pl.loop(0, SUBSTEPS * TRACERS)
    def _(block):
        strips(7 + block, lambda k: fl[block * LEVELS + k].astype(jnp.float32), LEVELS)

    for half in range(2):
        strips(23 + half, lambda k, half=half: obs[half * 8 + k], 8)
    strips(25, lambda k: mw[k], TRACERS)


def behind(value, axis):
    return pltpu.roll(value, 1, axis)


def ahead(value, axis):
    return pltpu.roll(value, value.shape[axis] - 1, axis)


def weights(branch, low, high, c_minus, c_both, slope):
    first = jnp.where(branch >= high, c_minus, jnp.where(branch >= low, c_both, c_minus))
    return first, jnp.where(branch >= high, slope, 0.0)


def sweep(value, courant, first, second, axis):
    step = ahead(value, axis) - value
    farther = jnp.where(courant >= 0.0, behind(step, axis), ahead(step, axis))
    flux = courant * value + first * step + second * farther
    return value - flux + behind(flux, axis)


def sweep_back(value, courant, first, second, axis):
    step = ahead(value, axis) - value
    reach = second * step
    forward = jnp.where(courant >= 0.0, reach, 0.0)
    total = first * step + ahead(forward, axis) + behind(reach - forward, axis)
    return value + courant * step + behind(total, axis) - total


def slopes(courant):
    c_minus = jnp.minimum(courant, 0.0)
    size = jnp.abs(courant)
    slope = 0.5 * size * (1.0 - size)
    return c_minus, c_minus + slope, slope


def window(width, groups, own, edges, outs, scratch):
    ck, cl, ct, mx, fl, obs, mw, cw = own
    final, grad, grad_left, grad_right = outs
    (
        q, temp, lon_code, lat_code, cx, cx_minus, cx_both, cx_slope, cy, cy_minus, cy_both, cy_slope,
        inv, elim, ratio, obs_w, mw_w, force,
    ) = scratch
    lane, col_w = (lane_ids(), col_ids(width))
    count_w = width // LANES
    tracers = PAIR * len(groups)
    offset = groups[0][0]
    static_left, static_right = groups[0][3:5]

    def spread(value, which, place, k):
        if edges is None:
            return value
        north, south = edges[which]
        n_part = pltpu.roll(north[place], (32 + LANES - EDGE * k) % LANES, 1)
        s_part = pltpu.roll(south(place), (64 + LANES - EDGE * k) % LANES, 1)
        top = pltpu.roll(value[:, LANES:], 32, 1)
        low = pltpu.roll(value[:, :LANES], 80, 1)
        outer = jnp.where(lane < 48, n_part, jnp.where(lane < 64, 0.0, s_part))
        inner = jnp.where((lane >= 80) & (lane < 112), low, jnp.where(lane < 112, outer, 0.0))
        return jnp.where(lane < 32, top, inner)

    def squeeze(right, left):
        return jnp.where(col_w < 4, right, left)

    lane_w = lax.broadcasted_iota(jnp.int32, (COLS, width), 1)
    last = lax.axis_index("lat") == lax.axis_size("lat") - 1
    pole = (lane_w == (ROWS - 1 if edges is None else 31)) & last
    carry = [None] * 4
    for level in range(LEVELS):
        def blocks(field, k):
            own_block = spread(field[level], 0, 4 + k, level)
            right = spread(static_right[40 + 8 * k + level], 2, 4 + k, level)
            left = spread(static_left[48 + 8 * k + level], 1, 4 + k, level)
            return [own_block, right, left, squeeze(right, left)]

        for k, value in enumerate(blocks(cl, 0)):
            cx[level, k] = value
            cx_minus[level, k], cx_both[level, k], cx_slope[level, k] = slopes(value)
        for k, value in enumerate(blocks(ct, 1)):
            value = jnp.where(pole, 0.0, value)
            cy[level, k] = value
            cy_minus[level, k], cy_both[level, k], cy_slope[level, k] = slopes(value)
        for k, value in enumerate(blocks(mx, 2)):
            coupling = value if level < LEVELS - 1 else jnp.zeros_like(value)
            pivot = 1.0 + coupling
            if level > 0:
                above, above_ratio = carry[k]
                pivot = pivot + above - above * above_ratio
            inverse = 1.0 / pivot
            inv[level, k] = inverse
            ratio[level, k] = coupling * inverse
            elim[level, k] = above * inverse if level > 0 else jnp.zeros_like(value)
            carry[k] = (coupling, coupling * inverse)

    for substep in range(SUBSTEPS):
        for tracer in range(tracers):
            k = substep * TRACERS + offset + tracer
            obs_w[substep * tracers + tracer] = spread(obs[k], 0, 23 + k // 8, k % 8)
    for tracer in range(tracers):
        mw_w[tracer] = spread(mw[offset + tracer], 0, 25, offset + tracer)

    def put_codes(substep, row, blocks, lat_blocks):
        for k, value in enumerate(blocks):
            lon_code[substep, row, k] = value - jnp.where(value >= 6.0, 6.0, jnp.where(value >= 3.0, 3.0, 0.0))
        for k, value in enumerate(lat_blocks):
            lat_code[substep, row, k] = value

    for first, from_left, from_right, _, _ in groups:
        @pl.loop(0, PAIR)
        def _(within):
            for level in range(LEVELS):
                part = within * LEVELS + level
                row = (first - offset) * LEVELS + part
                whole = first * LEVELS + part
                place = first + within
                q[row, 0] = spread(ck[whole], 0, place, level)
                q[row, 1] = spread(from_right[part], 2, place, level)
                q[row, 2] = spread(from_left[part], 1, place, level)

                def tail(value, which, s):
                    return spread(value, which, 7 + s * TRACERS + place, level)

                mine = [tail(fl[s * STATE + whole].astype(jnp.float32), 0, s) for s in range(SUBSTEPS)]
                l_a, l_b = (from_left[HALF + part], from_left[2 * HALF + part])
                r_a = from_right[HALF + part]
                r_b = from_right[2 * HALF + within * 4 + level % 4]
                if level >= 4:
                    r_b = pltpu.roll(r_b, 4, 0)
                one = [mine[0], tail(r_a, 2, 0), tail(l_a, 1, 0)]
                put_codes(0, row, one, one)
                two = [mine[1], tail(r_b, 2, 1), tail(l_b, 1, 1)]
                put_codes(1, row, two, [mine[1], squeeze(two[1], two[2])])
                three = [
                    mine[2], squeeze(tail(pltpu.roll(r_a, 2, 0), 2, 2), tail(pltpu.roll(l_b, 5, 0), 1, 2))
                ]
                put_codes(2, row, three, three)
                four = [mine[3], tail(pltpu.roll(l_a, 7, 0), 1, 3)]
                put_codes(3, row, four, [mine[3]])

    def ring(slots, read):
        return jnp.concatenate([read(k) for k in slots], axis=0)

    def lon_sweep(substep, row, level, slots, pieces, back):
        code_slots = slots if len(slots) == 3 else (0, 1)
        out = []
        for chunk in range(len(pieces)):
            at = slice(chunk * LANES, (chunk + 1) * LANES)
            value = jnp.concatenate(pieces[chunk], axis=0)
            code = ring(code_slots, lambda k: lon_code[substep, row, k, :, at])
            c, c_minus, c_both, slope = [ring(slots, lambda k: f[level, k, :, at]) for f in (cx, cx_minus, cx_both, cx_slope)]
            first, second = weights(code, 1.0, 2.0, c_minus, c_both, slope)
            value = (sweep_back if back else sweep)(value, c, first, second, 0)
            out.append([value[n * COLS : (n + 1) * COLS] for n in range(len(slots))])
        return out

    def lat_weights(substep, row, level, code_slot, slot):
        return weights(
            lat_code[substep, row, code_slot], 3.0, 6.0, cy_minus[level, slot], cy_both[level, slot], cy_slope[level, slot]
        )

    def forward(substep, slots, out_slots):
        @pl.loop(0, tracers)
        def _(tracer):
            above = {}
            for level in range(LEVELS):
                row = tracer * LEVELS + level
                pieces = [
                    [q[row, k, :, chunk * LANES : (chunk + 1) * LANES] for k in slots] for chunk in range(count_w)
                ]
                pieces = lon_sweep(substep, row, level, slots, pieces, False)
                blocks = {k: jnp.concatenate([piece[n] for piece in pieces], axis=1) for n, k in enumerate(slots)}
                if substep == 1:
                    blocks[3] = squeeze(blocks[1], blocks[2])
                for slot in out_slots:
                    code_slot = 1 if slot == 3 else slot
                    first, second = lat_weights(substep, row, level, code_slot, slot)
                    value = sweep(blocks[slot], cy[level, slot], first, second, 1)
                    value = value * inv[level, slot]
                    if level > 0:
                        value = value + elim[level, slot] * above[slot]
                    above[slot] = value
                    temp[row, slot] = value
            for slot in out_slots:
                value = above[slot]
                column = cw[LEVELS - 1] * value
                for level in range(LEVELS - 1, -1, -1):
                    row = tracer * LEVELS + level
                    if level < LEVELS - 1:
                        value = temp[row, slot] + ratio[level, slot] * value
                        column = column + cw[level] * value
                    if substep == SUBSTEPS - 1:
                        final[row] = value
                    else:
                        q[row, slot] = value
                if slot == 0:
                    at = substep * tracers + tracer
                    force[at] = mw_w[tracer] * (column - obs_w[at])

    def backward(substep, slots, out_slots):
        @pl.loop(0, tracers)
        def _(tracer):
            for slot in slots:
                for level in range(LEVELS):
                    row = tracer * LEVELS + level
                    if slot == 0:
                        value = cw[level] * force[substep * tracers + tracer]
                        if substep < SUBSTEPS - 1:
                            value = value + q[row, slot]
                    else:
                        value = q[row, slot]
                    value = value * inv[level, slot]
                    if level > 0:
                        value = value + elim[level, slot] * above
                    above = value
                    temp[row, slot] = value
            below = {}
            for level in range(LEVELS - 1, -1, -1):
                row = tracer * LEVELS + level
                blocks = {}
                for slot in slots:
                    code_slot = 1 if slot == 3 else slot
                    value = temp[row, slot]
                    if level < LEVELS - 1:
                        value = value + ratio[level, slot] * below[slot]
                    below[slot] = value
                    first, second = lat_weights(substep, row, level, code_slot, slot)
                    blocks[slot] = sweep_back(value, cy[level, slot], first, second, 1)
                if substep == SUBSTEPS - 1:
                    blocks[3] = jnp.zeros_like(blocks[0])
                if substep == 1:
                    blocks[1] = jnp.where(col_w < 4, blocks[3], 0.0)
                    blocks[2] = jnp.where(col_w < 4, 0.0, blocks[3])
                pieces = [
                    [blocks[k][:, chunk * LANES : (chunk + 1) * LANES] for k in out_slots] for chunk in range(count_w)
                ]
                pieces = lon_sweep(substep, row, level, out_slots, pieces, True)
                for chunk in range(count_w):
                    at = slice(chunk * LANES, (chunk + 1) * LANES)
                    for n, k in enumerate(out_slots):
                        if substep == 0:
                            (grad, grad_right, grad_left)[k][row, :, at] = pieces[chunk][n]
                        else:
                            q[row, k, :, at] = pieces[chunk][n]

    three, two = ((0, 1, 2), (0, 3))
    forward(0, three, three)
    forward(1, three, two)
    forward(2, two, two)
    forward(3, two, (0,))
    backward(3, (0,), two)
    backward(2, two, two)
    backward(1, two, three)
    backward(0, three, three)


def keep_inner(value):
    lane = lax.broadcasted_iota(jnp.int32, (COLS, ROWS), 1)
    return jnp.where((lane >= EDGE) & (lane < ROWS - EDGE), value, 0.0)


def main_first(*refs):
    own, (left_a, right_a), outs, scratch = (refs[:8], refs[8:10], refs[10:14], refs[14:])
    window(ROWS, [(0, left_a, right_a, left_a, right_a)], own, None, outs, scratch)
    for ref in outs[2:]:
        @pl.loop(0, HALF)
        def _(row):
            ref[row] = keep_inner(ref[row])


def main_second(*refs):
    own, (left_a, right_a, left_b, right_b), before, outs, scratch = (
        refs[:8], refs[8:12], refs[12:16], refs[16:20], refs[20:]
    )
    parts = [ref.at[HALF:STATE] for ref in outs]
    for ref, old in zip(outs, before):
        ref[0:HALF] = old[...]
    window(ROWS, [(PAIR, left_b, right_b, left_a, right_a)], own, None, parts, scratch)
    for ref in outs[2:]:
        @pl.loop(HALF, STATE)
        def _(row):
            ref[row] = keep_inner(ref[row])


def strip(*refs):
    own, (left_a, right_a, left_b, right_b, north, south, corner_l, corner_r), (main_final, main_grad) = (
        refs[:8], refs[8:16], refs[16:18]
    )
    final, grad, pack_left, pack_right = refs[18:22]
    outs, scratch = (refs[22:26], refs[26:])
    edges = (
        (north, lambda k: south[k]),
        (corner_l, lambda k: corner_l[CORNER + k]),
        (corner_r, lambda k: corner_r[CORNER + k]),
    )
    groups = [(0, left_a, right_a, left_a, right_a), (PAIR, left_b, right_b, left_a, right_a)]
    window(LANES, groups, own, edges, outs, scratch)
    lane = lane_ids()

    @pl.loop(0, STATE)
    def _(row):
        for target, source, value in ((final, main_final, outs[0][row]), (grad, main_grad, outs[1][row])):
            low = pltpu.roll(value, 48, 1)
            top = pltpu.roll(value, 96, 1)
            target[row, :, :LANES] = jnp.where(lane < EDGE, low, source[row, :, :LANES])
            target[row, :, LANES:] = jnp.where(lane >= LANES - EDGE, top, source[row, :, LANES:])

    for level in range(LEVELS):
        for target, source in ((pack_left, outs[2]), (pack_right, outs[3])):
            packed = jnp.zeros((COLS, LANES), jnp.float32)
            for tracer in range(TRACERS):
                value = source[tracer * LEVELS + level]
                start = 32 * tracer
                top = pltpu.roll(value, (start + LANES - 16) % LANES, 1)
                low = pltpu.roll(value, (start + 16 + LANES - 80) % LANES, 1)
                packed = jnp.where(lane >= start, jnp.where(lane < start + 16, top, low), packed)
            target[level] = packed


def finish(grad, from_right, from_left, edge_right, edge_left, out):
    lane = lane_ids()
    for level in range(LEVELS):
        packed = edge_right[level] + edge_left[level]
        for tracer in range(TRACERS):
            row = tracer * LEVELS + level
            start = 32 * tracer
            top = pltpu.roll(packed, (2 * LANES - 16 - start) % LANES, 1)
            low = pltpu.roll(packed, (2 * LANES - 16 - start) % LANES, 1)
            total = grad[row] + from_right[row] + from_left[row]
            out[row, :, :LANES] = total[:, :LANES] + jnp.where(lane < EDGE, low, 0.0)
            out[row, :, LANES:] = total[:, LANES:] + jnp.where(lane >= LANES - EDGE, top, 0.0)


def spec(count, space=pltpu.VMEM):
    return [pl.BlockSpec(memory_space=space)] * count


def scratch_for(width, tracers):
    rows = tracers * LEVELS
    sizes = [(rows, 4)] * 2 + [(SUBSTEPS, rows, 3)] * 2 + [(LEVELS, 4)] * 11 + [(SUBSTEPS * tracers,), (tracers,), (SUBSTEPS * tracers,)]
    return [pltpu.VMEM(size + (COLS, width), jnp.float32) for size in sizes]


def shards(
    checkpoint, courant_lon, courant_lat, mixing, limiter_flags, column_weights, observations, misfit_weight
):
    def block(rows, lanes=ROWS):
        return jax.ShapeDtypeStruct((rows, COLS, lanes), jnp.float32)

    def call(kernel, name, outs, in_specs, operands, scratch=(), cost=0):
        return pl.pallas_call(
            kernel,
            out_shape=tuple(outs),
            in_specs=in_specs,
            out_specs=tuple(spec(len(outs))),
            scratch_shapes=list(scratch),
            compiler_params=pltpu.CompilerParams(vmem_limit_bytes=LIMIT),
            name=name,
        )(*operands)

    lat, lon = (lax.axis_size("lat"), lax.axis_size("lon"))
    east = [(i, (i + 1) % lon) for i in range(lon)]
    west = [(j, i) for i, j in east]
    up = [(i, i + 1) for i in range(lat - 1)]
    down = [(j, i) for i, j in up]
    own = (
        checkpoint.reshape((STATE, COLS, ROWS)),
        courant_lon,
        courant_lat,
        mixing,
        limiter_flags.reshape((SUBSTEPS * STATE, COLS, ROWS)),
        observations.reshape((SUBSTEPS * TRACERS, COLS, ROWS)),
        misfit_weight,
    )
    copies = [pltpu.VMEM(value.shape, value.dtype) for value in own]
    right_a, right_b, left_a, left_b, to_north, to_south = call(
        pack,
        "pack",
        (block(72), block(48), block(64), block(40), block(26, LANES), block(26, LANES)),
        spec(7, pltpu.HBM),
        own,
        copies + [pltpu.SemaphoreType.DMA((7,))],
    )
    from_left_a = lax.ppermute(right_a, "lon", east)
    from_right_a = lax.ppermute(left_a, "lon", west)
    south = lax.ppermute(to_north, "lat", up)
    north = lax.ppermute(to_south, "lat", down)
    from_left_b = lax.ppermute(right_b, "lon", east)
    from_right_b = lax.ppermute(left_b, "lon", west)
    corner = jnp.concatenate([north[:CORNER], south[:CORNER]], axis=0)
    corner_l = lax.ppermute(corner, "lon", east)
    corner_r = lax.ppermute(corner, "lon", west)
    smem = spec(1, pltpu.SMEM)
    owned = own + (column_weights,)
    first = call(
        main_first, "main_first", [block(HALF)] * 4, spec(7) + smem + spec(2),
        owned + (from_left_a, from_right_a), scratch_for(ROWS, PAIR),
    )
    main_final, main_grad, grad_left, grad_right = call(
        main_second, "main_second", [block(STATE)] * 4, spec(7) + smem + spec(8),
        owned + (from_left_a, from_right_a, from_left_b, from_right_b) + tuple(first), scratch_for(ROWS, PAIR),
    )
    from_right = lax.ppermute(grad_left, "lon", west)
    from_left = lax.ppermute(grad_right, "lon", east)
    narrow = [pltpu.VMEM((STATE, COLS, LANES), jnp.float32)] * 4
    final, grad, pack_left, pack_right = call(
        strip, "strip", [block(STATE)] * 2 + [block(LEVELS, LANES)] * 2, spec(7) + smem + spec(10),
        owned + (from_left_a, from_right_a, from_left_b, from_right_b, north, south, corner_l, corner_r, main_final, main_grad),
        narrow + scratch_for(LANES, TRACERS),
    )
    edge_right = lax.ppermute(pack_left, "lon", west)
    edge_left = lax.ppermute(pack_right, "lon", east)
    (grad,) = call(finish, "finish", [block(STATE)], spec(5), (grad, from_right, from_left, edge_right, edge_left))
    return (final.reshape(checkpoint.shape), grad.reshape(checkpoint.shape))


def solution(mesh):
    return jax.shard_map(
        shards,
        mesh=mesh,
        in_specs=(
            P(None, None, "lon", "lat"),
            P(None, "lon", "lat"),
            P(None, "lon", "lat"),
            P(None, "lon", "lat"),
            P(None, None, None, "lon", "lat"),
            P(),
            P(None, None, "lon", "lat"),
            P(None, "lon", "lat"),
        ),
        out_specs=(P(None, None, "lon", "lat"), P(None, None, "lon", "lat")),
        check_vma=False,
    )
```

time: 85.7 us -> 98.8 us (1.15); the launches traced: 85.2 us -> 97.3 us
  starting transfers between devices: 21.2 us -> 31.3 us
  Pallas kernels: 28.8 us -> 33.7 us
  waiting for transfers between devices: 25.8 us -> 24.4 us
    ppermute x6 -> x10, starting transfers between devices: 13.9 us -> 24.6 us  [the longest x1 8.02 us: shards(): corner_r = lax.ppermute(corner, 'lon', west)]
    ppermute x6 -> x10, waiting for transfers between devices: 17.5 us -> 12.2 us  [the longest x1 4.02 us: shards(): corner_l = lax.ppermute(corner, 'lon', east)]
    ppermute x1, waiting for transfers between devices: 1.82 us -> 7.05 us  [shards(): south = lax.ppermute(to_north, 'lat', up)]
    pallas_call x2 -> x5, Pallas kernels: 28.8 us -> 33.7 us  [call(): pl.pallas_call(kernel, out_shape=tuple(outs), in_specs=in_specs, out_spec...]
    ppermute x1, waiting for transfers between devices: 6.47 us -> 5.15 us  [shards(): north = lax.ppermute(to_south, 'lat', down)]
    unnamed x22 -> x24, local copies, waits for them, and re-layouts: 7 us -> 7.01 us
  transfers between devices with their start and end apart: 8 -> 12, of which waited for: 6 -> 6; matrix products, arithmetic and copies ran while one was open for 0% -> 0% of each run, Pallas kernels for 0% -> 24%
where the time goes in v1:
time: 98.8 us; the launch traced here: 97.3 us
  Pallas kernels  33.7 us (34%)
  starting transfers between devices  31.3 us (32%)
  waiting for transfers between devices  24.4 us (25%)
  local copies, waits for them, and re-layouts  7.02 us (7%)
    pallas_call x5, Pallas kernels, call(): pl.pallas_call(kernel, out_shape=tuple(outs), in_specs=in_specs, out_spec...  33.7 us
    ppermute x1, starting transfers between devices, shards(): corner_r = lax.ppermute(corner, 'lon', west)  8.02 us
    ppermute x1, waiting for transfers between devices, shards(): south = lax.ppermute(to_north, 'lat', up)  7.05 us
    unnamed x24, local copies, waits for them, and re-layouts  7.01 us
    ppermute x1, starting transfers between devices, shards(): from_right_a = lax.ppermute(left_a, 'lon', west)  6.3 us
    ppermute x1, waiting for transfers between devices, shards(): north = lax.ppermute(to_south, 'lat', down)  5.15 us
    ppermute x1, starting transfers between devices, shards(): north = lax.ppermute(to_south, 'lat', down)  4.81 us
    ppermute x1, waiting for transfers between devices, shards(): corner_l = lax.ppermute(corner, 'lon', east)  4.02 us
  transfers between devices with their start and end apart: 12, of which 6 were waited for; matrix products, arithmetic and copies ran while one was open for 0% of the time, Pallas kernels for 24%

profile of v1, /device:TPU:24, one launch (start us, length us, event | category | flops | bytes accessed | tf_op | source)
XLA Modules:
  0.0 97.3 jit_solution(6228428371466590994)
XLA Ops:
  0.6 0.0 copy-start
  0.6 1.2 %copy-done = s32[4,4,8,8,256]{4,3,2,1,0:T(8,128)S(1)} copy-done((s32[4,4,8,8,256]{4,3,2,1,0:T(8,128)S(1)}, s32[4,4,8,8,256]{4,3,2,1,0:T(8,128)}, u32[]{:S(2)}) %copy-start) | copy-done | bytes 1048600
  1.9 0.0 copy-start.1
  1.9 0.9 copy-done.1
  2.8 0.0 copy-start.2
  2.8 0.9 copy-done.2
  3.7 0.0 copy-start.3
  3.7 0.8 copy-done.3
  4.6 0.0 copy-start.4
  4.6 0.8 copy-done.4
  5.4 0.0 copy-start.5
  5.4 0.8 copy-done.5
  6.2 0.0 copy-start.6
  6.2 0.8 copy-done.6
  7.0 2.6 %pack.1 = (f32[72,8,256]{2,1,0:T(8,128)S(1)}, f32[48,8,256]{2,1,0:T(8,128)S(1)}, f32[64,8,256]{2,1,0:T(8,128)S(1)}, f32[40,8,256]{2,1,0:T(8,128)S(1)}, f32[26,8,...) custom-call(f32[32,8,256]{2,1,0:T(8,128)S(1)} %bitcast.9, f32[8,8,256]{2,1,0:T(8,128)S(1)} %copy-done.3, ...), custom_call_target="tpu_custom_call" | custom-call | tf_op jit(solution)/shard_map/pack/pallas_call | solution.py:431
  9.6 0.1 collective-permute-start
  9.7 6.3 %collective-permute-start.1 = (f32[64,8,256]{2,1,0:T(8,128)S(1)}, f32[64,8,256]{2,1,0:T(8,128)S(1)}, u32[]{:S(2)}, u32[]{:S(2)}) collective-permute-start(f32[64,8,256]{2,1,0:T(8,128)S(1)} %get-tuple-element.21), channel_id=1, source_target_pairs={{1,0},{2,1},{3,2},{4,3},{5,4},{6,5},{7,6},{8,7},{9,8},{10,9},{11,1... | collective-permute-start | bytes 1572872 | tf_op jit(solution)/shard_map/ppermute | solution.py:465
  16.0 0.0 collective-permute-start.2
  16.0 3.9 %collective-permute-start.3 = (f32[40,8,256]{2,1,0:T(8,128)S(1)}, f32[40,8,256]{2,1,0:T(8,128)S(1)}, u32[]{:S(2)}, u32[]{:S(2)}) collective-permute-start(f32[40,8,256]{2,1,0:T(8,128)S(1)} %get-tuple-element.23), channel_id=1, source_target_pairs={{1,0},{2,1},{3,2},{4,3},{5,4},{6,5},{7,6},{8,7},{9,8},{10,9},{11,1... | collective-permute-start | bytes 983048 | tf_op jit(solution)/shard_map/ppermute | solution.py:469
  19.8 4.8 %collective-permute-start.4 = (f32[26,8,128]{2,1,0:T(8,128)S(1)}, f32[26,8,128]{2,1,0:T(8,128)S(1)}, u32[]{:S(2)}, u32[]{:S(2)}) collective-permute-start(f32[26,8,128]{2,1,0:T(8,128)S(1)} %get-tuple-element.24), channel_id=1, source_target_pairs={{32,0},{64,32},{96,64},{128,96},{160,128},{192,160},{224,192},{33,... | collective-permute-start | bytes 319496 | tf_op jit(solution)/shard_map/ppermute | solution.py:467
  24.6 5.2 %collective-permute-done.4.refs_12_ = f32[26,8,128]{2,1,0:T(8,128)S(1)} collective-permute-done((f32[26,8,128]{2,1,0:T(8,128)S(1)}, f32[26,8,128]{2,1,0:T(8,128)S(1)}, u32[]{:S(2)}, u32[]{:S(2)}) %collective-permute-start.4) | collective-permute-done | bytes 106528 | tf_op jit(solution)/shard_map/ppermute | solution.py:467
  29.8 0.0 copy-start.7
  29.8 1.9 %collective-permute-start.5 = (f32[26,8,128]{2,1,0:T(8,128)S(1)}, f32[26,8,128]{2,1,0:T(8,128)S(1)}, u32[]{:S(2)}, u32[]{:S(2)}) collective-permute-start(f32[26,8,128]{2,1,0:T(8,128)S(1)} %get-tuple-element.25), channel_id=1, source_target_pairs={{0,32},{32,64},{64,96},{96,128},{128,160},{160,192},{192,224},{1,3... | collective-permute-start | bytes 319496 | tf_op jit(solution)/shard_map/ppermute | solution.py:466
  31.7 0.0 copy-done.7
  31.7 0.0 copy-start.11
  31.7 7.1 %collective-permute-done.5.refs_13_ = f32[26,8,128]{2,1,0:T(8,128)S(1)} collective-permute-done((f32[26,8,128]{2,1,0:T(8,128)S(1)}, f32[26,8,128]{2,1,0:T(8,128)S(1)}, u32[]{:S(2)}, u32[]{:S(2)}) %collective-permute-start.5) | collective-permute-done | bytes 106528 | tf_op jit(solution)/shard_map/ppermute | solution.py:466
  38.8 0.0 copy-start.9
  38.8 0.6 copy-done.9
  39.4 0.0 collective-permute-done.1.refs_9_
  39.4 0.0 collective-permute-done.refs_8_
  39.4 0.0 copy-done.11
  39.4 7.4 %main_first.1 = (f32[16,8,256]{2,1,0:T(8,128)S(1)}, f32[16,8,256]{2,1,0:T(8,128)S(1)}, f32[16,8,256]{2,1,0:T(8,128)S(1)}, f32[16,8,256]{2,1,0:T(8,128)S(1)}) custom-call(f32[32,8,256]{2,1,0:T(8,128)S(1)} %bitcast.10, f32[8,8,256]{2,1,0:T(8,128)S(1)} %copy-done.3, f32[8,8,256]{2,1,0:T(8,128)S(1)} %copy-done.4, f32[8,8,256]{2,1,0:T(8,128)S(1)} %copy-done.5, ...), custom_call_target="tpu_custom_call" | custom-call | tf_op jit(solution)/shard_map/main_first/pallas_call | solution.py:431
  46.8 0.0 collective-permute-done.3.refs_11_
  46.8 0.0 collective-permute-done.2.refs_10_
  46.8 0.0 slice-start
  46.9 0.0 slice-start.1
  46.9 7.4 %main_second.1 = (f32[32,8,256]{2,1,0:T(8,128)S(1)}, f32[32,8,256]{2,1,0:T(8,128)S(1)}, f32[32,8,256]{2,1,0:T(8,128)S(1)}, f32[32,8,256]{2,1,0:T(8,128)S(1)}) custom-call(f32[32,8,256]{2,1,0:T(8,128)S(1)} %bitcast.11, f32[8,8,256]{2,1,0:T(8,128)S(1)} %copy-done.3, f32[8,8,256]{2,1,0:T(8,128)S(1)} %copy-done.4, f32[8,8,256]{2,1,0:T(8,128)S(1)} %copy-done.5, ...), custom_call_target="tpu_custom_call" | custom-call | tf_op jit(solution)/shard_map/main_second/pallas_call | solution.py:431
  54.3 3.9 %collective-permute-start.8 = (f32[32,8,256]{2,1,0:T(8,128)S(1)}, f32[32,8,256]{2,1,0:T(8,128)S(1)}, u32[]{:S(2)}, u32[]{:S(2)}) collective-permute-start(f32[32,8,256]{2,1,0:T(8,128)S(1)} %get-tuple-element.34), channel_id=1, source_target_pairs={{1,0},{2,1},{3,2},{4,3},{5,4},{6,5},{7,6},{8,7},{9,8},{10,9},{11,1... | collective-permute-start | bytes 786440 | tf_op jit(solution)/shard_map/ppermute | solution.py:483
  58.2 0.0 copy-start.8
  58.2 0.0 copy-start.10
  58.2 1.9 %collective-permute-start.9 = (f32[32,8,256]{2,1,0:T(8,128)S(1)}, f32[32,8,256]{2,1,0:T(8,128)S(1)}, u32[]{:S(2)}, u32[]{:S(2)}) collective-permute-start(f32[32,8,256]{2,1,0:T(8,128)S(1)} %get-tuple-element.35), channel_id=1, source_target_pairs={{0,1},{1,2},{2,3},{3,4},{4,5},{5,6},{6,7},{7,8},{8,9},{9,10},{10,1... | collective-permute-start | bytes 786440 | tf_op jit(solution)/shard_map/ppermute | solution.py:484
  60.1 0.0 slice-done
  60.1 0.0 slice-done.1
  60.2 8.0 %collective-permute-start.7 = (f32[46,8,128]{2,1,0:T(8,128)S(1)}, f32[46,8,128]{2,1,0:T(8,128)S(1)}, u32[]{:S(2)}, u32[]{:S(2)}) collective-permute-start(f32[46,8,128]{2,1,0:T(8,128)S(1)} %pad_maximum_fusion), channel_id=1, source_target_pairs={{1,0},{2,1},{3,2},{4,3},{5,4},{6,5},{7,6},{8,7},{9,8},{10,9},{11,1... | collective-permute-start | bytes 565256 | tf_op jit(solution)/shard_map/ppermute | solution.py:472
  68.2 0.0 collective-permute-start.6
  68.2 3.1 %collective-permute-done.7.refs_15_ = f32[46,8,128]{2,1,0:T(8,128)S(1)} collective-permute-done((f32[46,8,128]{2,1,0:T(8,128)S(1)}, f32[46,8,128]{2,1,0:T(8,128)S(1)}, u32[]{:S(2)}, u32[]{:S(2)}) %collective-permute-start.7) | collective-permute-done | bytes 188448 | tf_op jit(solution)/shard_map/ppermute | solution.py:472
  71.3 4.0 %collective-permute-done.6.refs_14_ = f32[46,8,128]{2,1,0:T(8,128)S(1)} collective-permute-done((f32[46,8,128]{2,1,0:T(8,128)S(1)}, f32[46,8,128]{2,1,0:T(8,128)S(1)}, u32[]{:S(2)}, u32[]{:S(2)}) %collective-permute-start.6) | collective-permute-done | bytes 188448 | tf_op jit(solution)/shard_map/ppermute | solution.py:471
  75.3 0.0 copy-done.8
  75.3 0.0 copy-done.10
  75.3 15.6 %strip.1 = (f32[32,8,256]{2,1,0:T(8,128)}, f32[32,8,256]{2,1,0:T(8,128)S(1)}, f32[8,8,128]{2,1,0:T(8,128)S(1)}, f32[8,8,128]{2,1,0:T(8,128)S(1)}) custom-call(f32[32,8,256]{2,1,0:T(8,128)S(1)} %bitcast.12, f32[8,8,256]{2,1,0:T(8,128)S(1)} %copy-done.3, f32[8,8,256]{2,1,0:T(8,128)S(1)} %copy-done.4, f32[8,8,256]{2,1,0:T(8,128)S(1)} %copy-done.5, ...), custom_call_target="tpu_custom_call" | custom-call | tf_op jit(solution)/shard_map/strip/pallas_call | solution.py:431
  90.9 0.1 collective-permute-start.10
  91.0 0.4 collective-permute-start.11
  91.4 1.2 %collective-permute-done.10.edge_right = f32[8,8,128]{2,1,0:T(8,128)S(1)} collective-permute-done((f32[8,8,128]{2,1,0:T(8,128)S(1)}, f32[8,8,128]{2,1,0:T(8,128)S(1)}, u32[]{:S(2)}, u32[]{:S(2)}) %collective-permute-start.10) | collective-permute-done | bytes 32800 | tf_op jit(solution)/shard_map/ppermute | solution.py:491
  92.6 3.9 %collective-permute-done.11.edge_left = f32[8,8,128]{2,1,0:T(8,128)S(1)} collective-permute-done((f32[8,8,128]{2,1,0:T(8,128)S(1)}, f32[8,8,128]{2,1,0:T(8,128)S(1)}, u32[]{:S(2)}, u32[]{:S(2)}) %collective-permute-start.11) | collective-permute-done | bytes 32800 | tf_op jit(solution)/shard_map/ppermute | solution.py:492
  96.4 0.0 collective-permute-done.8.from_right
  96.5 0.0 collective-permute-done.9.from_left
  96.5 0.8 finish.1
  (1 shorter events, 0.0 us)
Async XLA Ops:
  0.6 1.2 %copy-start = (s32[4,4,8,8,256]{4,3,2,1,0:T(8,128)S(1)}, s32[4,4,8,8,256]{4,3,2,1,0:T(8,128)}, u32[]{:S(2)}) copy-start(s32[4,4,8,8,256]{4,3,2,1,0:T(8,128)} %param.12) | copy-start | bytes 3145732
  1.9 0.9 copy-start.1
  2.8 0.9 copy-start.2
  3.7 0.8 copy-start.3
  4.6 0.8 copy-start.4
  5.4 0.8 copy-start.5
  6.2 0.8 copy-start.6
  9.6 29.9 %collective-permute-start = (f32[72,8,256]{2,1,0:T(8,128)S(1)}, f32[72,8,256]{2,1,0:T(8,128)S(1)}, u32[]{:S(2)}, u32[]{:S(2)}) collective-permute-start(f32[72,8,256]{2,1,0:T(8,128)S(1)} %get-tuple-element.20), channel_id=1, source_target_pairs={{0,1},{1,2},{2,3},{3,4},{4,5},{5,6},{6,7},{7,8},{8,9},{9,10},{10,1... | collective-permute-start | bytes 1769480 | tf_op jit(solution)/shard_map/ppermute | solution.py:464
  9.7 29.8 %collective-permute-start.1 = (f32[64,8,256]{2,1,0:T(8,128)S(1)}, f32[64,8,256]{2,1,0:T(8,128)S(1)}, u32[]{:S(2)}, u32[]{:S(2)}) collective-permute-start(f32[64,8,256]{2,1,0:T(8,128)S(1)} %get-tuple-element.21), channel_id=1, source_target_pairs={{1,0},{2,1},{3,2},{4,3},{5,4},{6,5},{7,6},{8,7},{9,8},{10,9},{11,1... | collective-permute-start | bytes 1572872 | tf_op jit(solution)/shard_map/ppermute | solution.py:465
  16.0 30.9 %collective-permute-start.2 = (f32[48,8,256]{2,1,0:T(8,128)S(1)}, f32[48,8,256]{2,1,0:T(8,128)S(1)}, u32[]{:S(2)}, u32[]{:S(2)}) collective-permute-start(f32[48,8,256]{2,1,0:T(8,128)S(1)} %get-tuple-element.22), channel_id=1, source_target_pairs={{0,1},{1,2},{2,3},{3,4},{4,5},{5,6},{6,7},{7,8},{8,9},{9,10},{10,1... | collective-permute-start | bytes 1179656 | tf_op jit(solution)/shard_map/ppermute | solution.py:468
  16.0 30.9 %collective-permute-start.3 = (f32[40,8,256]{2,1,0:T(8,128)S(1)}, f32[40,8,256]{2,1,0:T(8,128)S(1)}, u32[]{:S(2)}, u32[]{:S(2)}) collective-permute-start(f32[40,8,256]{2,1,0:T(8,128)S(1)} %get-tuple-element.23), channel_id=1, source_target_pairs={{1,0},{2,1},{3,2},{4,3},{5,4},{6,5},{7,6},{8,7},{9,8},{10,9},{11,1... | collective-permute-start | bytes 983048 | tf_op jit(solution)/shard_map/ppermute | solution.py:469
  19.8 10.0 %collective-permute-start.4 = (f32[26,8,128]{2,1,0:T(8,128)S(1)}, f32[26,8,128]{2,1,0:T(8,128)S(1)}, u32[]{:S(2)}, u32[]{:S(2)}) collective-permute-start(f32[26,8,128]{2,1,0:T(8,128)S(1)} %get-tuple-element.24), channel_id=1, source_target_pairs={{32,0},{64,32},{96,64},{128,96},{160,128},{192,160},{224,192},{33,... | collective-permute-start | bytes 319496 | tf_op jit(solution)/shard_map/ppermute | solution.py:467
  29.8 1.9 %copy-start.7 = (f32[26,8,128]{2,1,0:T(8,128)}, f32[26,8,128]{2,1,0:T(8,128)S(1)}, u32[]{:S(2)}) copy-start(f32[26,8,128]{2,1,0:T(8,128)S(1)} %collective-permute-done.4.refs_12_) | copy-start | bytes 319492
  29.8 9.0 %collective-permute-start.5 = (f32[26,8,128]{2,1,0:T(8,128)S(1)}, f32[26,8,128]{2,1,0:T(8,128)S(1)}, u32[]{:S(2)}, u32[]{:S(2)}) collective-permute-start(f32[26,8,128]{2,1,0:T(8,128)S(1)} %get-tuple-element.25), channel_id=1, source_target_pairs={{0,32},{32,64},{64,96},{96,128},{128,160},{160,192},{192,224},{1,3... | collective-permute-start | bytes 319496 | tf_op jit(solution)/shard_map/ppermute | solution.py:466
  31.7 7.7 %copy-start.11 = (f32[8]{0:T(128)S(1)}, f32[8]{0:T(128)}, u32[]{:S(2)}) copy-start(f32[8]{0:T(128)} %refs_7_.5) | copy-start | bytes 100
  38.8 0.6 copy-start.9
  46.8 13.3 %slice-start = ((f32[26,8,128]{2,1,0:T(8,128)}), f32[23,8,128]{2,1,0:T(8,128)S(1)}, s32[]{:S(2)}) async-start(f32[26,8,128]{2,1,0:T(8,128)} %copy-done.7), calls=%async_computation | async-start | bytes 188416 | tf_op jit(solution)/shard_map/slice | solution.py:470
  46.9 13.3 %slice-start.1 = ((f32[26,8,128]{2,1,0:T(8,128)}), f32[23,8,128]{2,1,0:T(8,128)S(1)}, s32[]{:S(2)}) async-start(f32[26,8,128]{2,1,0:T(8,128)} %copy-done.9), calls=%async_computation.1 | async-start | bytes 188416 | tf_op jit(solution)/shard_map/slice | solution.py:470
  54.3 42.2 %collective-permute-start.8 = (f32[32,8,256]{2,1,0:T(8,128)S(1)}, f32[32,8,256]{2,1,0:T(8,128)S(1)}, u32[]{:S(2)}, u32[]{:S(2)}) collective-permute-start(f32[32,8,256]{2,1,0:T(8,128)S(1)} %get-tuple-element.34), channel_id=1, source_target_pairs={{1,0},{2,1},{3,2},{4,3},{5,4},{6,5},{7,6},{8,7},{9,8},{10,9},{11,1... | collective-permute-start | bytes 786440 | tf_op jit(solution)/shard_map/ppermute | solution.py:483
  58.2 17.1 %copy-start.8 = (f32[26,8,128]{2,1,0:T(8,128)S(1)}, f32[26,8,128]{2,1,0:T(8,128)}, u32[]{:S(2)}) copy-start(f32[26,8,128]{2,1,0:T(8,128)} %copy-done.7) | copy-start | bytes 319492
  58.2 17.1 %copy-start.10 = (f32[26,8,128]{2,1,0:T(8,128)S(1)}, f32[26,8,128]{2,1,0:T(8,128)}, u32[]{:S(2)}) copy-start(f32[26,8,128]{2,1,0:T(8,128)} %copy-done.9) | copy-start | bytes 319492
  58.2 38.2 %collective-permute-start.9 = (f32[32,8,256]{2,1,0:T(8,128)S(1)}, f32[32,8,256]{2,1,0:T(8,128)S(1)}, u32[]{:S(2)}, u32[]{:S(2)}) collective-permute-start(f32[32,8,256]{2,1,0:T(8,128)S(1)} %get-tuple-element.35), channel_id=1, source_target_pairs={{0,1},{1,2},{2,3},{3,4},{4,5},{5,6},{6,7},{7,8},{8,9},{9,10},{10,1... | collective-permute-start | bytes 786440 | tf_op jit(solution)/shard_map/ppermute | solution.py:484
  60.2 11.1 %collective-permute-start.7 = (f32[46,8,128]{2,1,0:T(8,128)S(1)}, f32[46,8,128]{2,1,0:T(8,128)S(1)}, u32[]{:S(2)}, u32[]{:S(2)}) collective-permute-start(f32[46,8,128]{2,1,0:T(8,128)S(1)} %pad_maximum_fusion), channel_id=1, source_target_pairs={{1,0},{2,1},{3,2},{4,3},{5,4},{6,5},{7,6},{8,7},{9,8},{10,9},{11,1... | collective-permute-start | bytes 565256 | tf_op jit(solution)/shard_map/ppermute | solution.py:472
  68.2 7.1 %collective-permute-start.6 = (f32[46,8,128]{2,1,0:T(8,128)S(1)}, f32[46,8,128]{2,1,0:T(8,128)S(1)}, u32[]{:S(2)}, u32[]{:S(2)}) collective-permute-start(f32[46,8,128]{2,1,0:T(8,128)S(1)} %pad_maximum_fusion), channel_id=1, source_target_pairs={{0,1},{1,2},{2,3},{3,4},{4,5},{5,6},{6,7},{7,8},{8,9},{9,10},{10,1... | collective-permute-start | bytes 565256 | tf_op jit(solution)/shard_map/ppermute | solution.py:471
  90.9 1.7 %collective-permute-start.10 = (f32[8,8,128]{2,1,0:T(8,128)S(1)}, f32[8,8,128]{2,1,0:T(8,128)S(1)}, u32[]{:S(2)}, u32[]{:S(2)}) collective-permute-start(f32[8,8,128]{2,1,0:T(8,128)S(1)} %get-tuple-element.36), channel_id=1, source_target_pairs={{1,0},{2,1},{3,2},{4,3},{5,4},{6,5},{7,6},{8,7},{9,8},{10,9},{11,1... | collective-permute-start | bytes 98312 | tf_op jit(solution)/shard_map/ppermute | solution.py:491
  91.0 5.4 %collective-permute-start.11 = (f32[8,8,128]{2,1,0:T(8,128)S(1)}, f32[8,8,128]{2,1,0:T(8,128)S(1)}, u32[]{:S(2)}, u32[]{:S(2)}) collective-permute-start(f32[8,8,128]{2,1,0:T(8,128)S(1)} %get-tuple-element.37), channel_id=1, source_target_pairs={{0,1},{1,2},{2,3},{3,4},{4,5},{5,6},{6,7},{7,8},{8,9},{9,10},{10,1... | collective-permute-start | bytes 98312 | tf_op jit(solution)/shard_map/ppermute | solution.py:492

commit v2 on v1

--- a/solution.py
+++ b/solution.py
@@ -7,10 +7,11 @@
 
 TRACERS, LEVELS, SUBSTEPS = 4, 8, 4
 PAIR = 2
+TOGETHER = {1: 2, 2: 1}
 COLS, ROWS, EDGE, LANES = 8, 256, 16, 128
 STATE = TRACERS * LEVELS
 HALF = PAIR * LEVELS
-LIMIT = 40 * 1024 * 1024
+LIMIT = 24 * 1024 * 1024
 CORNER = 23
 
 
@@ -23,7 +24,7 @@
 
 
 def pack(*refs):
-    hbm, (right_a, right_b, left_a, left_b, to_north, to_south), own, sems = (refs[:7], refs[7:13], refs[13:20], refs[20])
+    hbm, own, (right_a, right_b, left_a, left_b, to_north, to_south), sems = (refs[:7], refs[7:14], refs[14:20], refs[20])
     copies = [pltpu.make_async_copy(hbm[k], own[k], sems.at[k]) for k in range(7)]
     for copy in copies:
         copy.start()
@@ -57,10 +58,10 @@
         north = jnp.zeros((COLS, LANES), jnp.float32)
         south = north
         for k in range(count):
-            here = (lane >= EDGE * k) & (lane < EDGE * (k + 1))
             whole = read(k)
-            north = jnp.where(here, pltpu.roll(whole[:, LANES:], (EDGE * (k + 1)) % LANES, 1), north)
-            south = jnp.where(here, pltpu.roll(whole[:, :LANES], EDGE * k, 1), south)
+            here = lane // EDGE
+            north = jnp.where(here == (k + 1) % 8, pltpu.roll(whole[:, LANES:], (EDGE * (k + 2)) % LANES, 1), north)
+            south = jnp.where(here == k, pltpu.roll(whole[:, :LANES], EDGE * k, 1), south)
         to_north[place] = north
         to_south[place] = south
 
@@ -123,7 +124,9 @@
         inv, elim, ratio, obs_w, mw_w, force,
     ) = scratch
     lane, col_w = (lane_ids(), col_ids(width))
+    strip_of = lane // EDGE
     count_w = width // LANES
+    together = TOGETHER[count_w]
     tracers = PAIR * len(groups)
     offset = groups[0][0]
     static_left, static_right = groups[0][3:5]
@@ -132,20 +135,17 @@
         if edges is None:
             return value
         north, south = edges[which]
-        n_part = pltpu.roll(north[place], (32 + LANES - EDGE * k) % LANES, 1)
-        s_part = pltpu.roll(south(place), (64 + LANES - EDGE * k) % LANES, 1)
-        top = pltpu.roll(value[:, LANES:], 32, 1)
-        low = pltpu.roll(value[:, :LANES], 80, 1)
-        outer = jnp.where(lane < 48, n_part, jnp.where(lane < 64, 0.0, s_part))
-        inner = jnp.where((lane >= 80) & (lane < 112), low, jnp.where(lane < 112, outer, 0.0))
-        return jnp.where(lane < 32, top, inner)
+        halo = pltpu.roll(jnp.where(strip_of == k, north[place], south(place)), (96 + LANES - EDGE * k) % LANES, 1)
+        top = pltpu.roll(value[:, LANES:], 96, 1)
+        inner = jnp.where(lane < 32, value[:, :LANES], jnp.where(lane < 64, 0.0, top))
+        return jnp.where(lane < 96, inner, halo)
 
     def squeeze(right, left):
         return jnp.where(col_w < 4, right, left)
 
     lane_w = lax.broadcasted_iota(jnp.int32, (COLS, width), 1)
     last = lax.axis_index("lat") == lax.axis_size("lat") - 1
-    pole = (lane_w == (ROWS - 1 if edges is None else 31)) & last
+    pole = (lane_w == (ROWS - 1 if edges is None else 95)) & last
     carry = [None] * 4
     for level in range(LEVELS):
         def blocks(field, k):
@@ -240,88 +240,98 @@
         )
 
     def forward(substep, slots, out_slots):
-        @pl.loop(0, tracers)
-        def _(tracer):
+        @pl.loop(0, tracers // together)
+        def _(batch):
+            members = [batch * together + n for n in range(together)]
             above = {}
             for level in range(LEVELS):
-                row = tracer * LEVELS + level
-                pieces = [
-                    [q[row, k, :, chunk * LANES : (chunk + 1) * LANES] for k in slots] for chunk in range(count_w)
-                ]
-                pieces = lon_sweep(substep, row, level, slots, pieces, False)
-                blocks = {k: jnp.concatenate([piece[n] for piece in pieces], axis=1) for n, k in enumerate(slots)}
-                if substep == 1:
-                    blocks[3] = squeeze(blocks[1], blocks[2])
-                for slot in out_slots:
-                    code_slot = 1 if slot == 3 else slot
-                    first, second = lat_weights(substep, row, level, code_slot, slot)
-                    value = sweep(blocks[slot], cy[level, slot], first, second, 1)
-                    value = value * inv[level, slot]
-                    if level > 0:
-                        value = value + elim[level, slot] * above[slot]
-                    above[slot] = value
-                    temp[row, slot] = value
-            for slot in out_slots:
-                value = above[slot]
-                column = cw[LEVELS - 1] * value
-                for level in range(LEVELS - 1, -1, -1):
+                for n, tracer in enumerate(members):
                     row = tracer * LEVELS + level
-                    if level < LEVELS - 1:
-                        value = temp[row, slot] + ratio[level, slot] * value
-                        column = column + cw[level] * value
-                    if substep == SUBSTEPS - 1:
-                        final[row] = value
-                    else:
-                        q[row, slot] = value
-                if slot == 0:
-                    at = substep * tracers + tracer
-                    force[at] = mw_w[tracer] * (column - obs_w[at])
+                    pieces = [
+                        [q[row, k, :, chunk * LANES : (chunk + 1) * LANES] for k in slots] for chunk in range(count_w)
+                    ]
+                    pieces = lon_sweep(substep, row, level, slots, pieces, False)
+                    blocks = {k: jnp.concatenate([piece[m] for piece in pieces], axis=1) for m, k in enumerate(slots)}
+                    if substep == 1:
+                        blocks[3] = squeeze(blocks[1], blocks[2])
+                    for slot in out_slots:
+                        code_slot = 1 if slot == 3 else slot
+                        first, second = lat_weights(substep, row, level, code_slot, slot)
+                        value = sweep(blocks[slot], cy[level, slot], first, second, 1)
+                        value = value * inv[level, slot]
+                        if level > 0:
+                            value = value + elim[level, slot] * above[n, slot]
+                        above[n, slot] = value
+                        temp[row, slot] = value
+            column = {}
+            for level in range(LEVELS - 1, -1, -1):
+                for n, tracer in enumerate(members):
+                    row = tracer * LEVELS + level
+                    for slot in out_slots:
+                        value = above[n, slot]
+                        if level < LEVELS - 1:
+                            value = temp[row, slot] + ratio[level, slot] * value
+                            above[n, slot] = value
+                        if slot == 0:
+                            part = cw[level] * value
+                            column[n] = part if level == LEVELS - 1 else column[n] + part
+                        if substep == SUBSTEPS - 1:
+                            final[row] = value
+                        else:
+                            q[row, slot] = value
+            for n, tracer in enumerate(members):
+                at = substep * tracers + tracer
+                force[at] = mw_w[tracer] * (column[n] - obs_w[at])
 
     def backward(substep, slots, out_slots):
-        @pl.loop(0, tracers)
-        def _(tracer):
-            for slot in slots:
-                for level in range(LEVELS):
+        @pl.loop(0, tracers // together)
+        def _(batch):
+            members = [batch * together + n for n in range(together)]
+            above = {}
+            for level in range(LEVELS):
+                for n, tracer in enumerate(members):
                     row = tracer * LEVELS + level
-                    if slot == 0:
-                        value = cw[level] * force[substep * tracers + tracer]
-                        if substep < SUBSTEPS - 1:
-                            value = value + q[row, slot]
-                    else:
-                        value = q[row, slot]
-                    value = value * inv[level, slot]
-                    if level > 0:
-                        value = value + elim[level, slot] * above
-                    above = value
-                    temp[row, slot] = value
+                    for slot in slots:
+                        if slot == 0:
+                            value = cw[level] * force[substep * tracers + tracer]
+                            if substep < SUBSTEPS - 1:
+                                value = value + q[row, slot]
+                        else:
+                            value = q[row, slot]
+                        value = value * inv[level, slot]
+                        if level > 0:
+                            value = value + elim[level, slot] * above[n, slot]
+                        above[n, slot] = value
+                        temp[row, slot] = value
             below = {}
             for level in range(LEVELS - 1, -1, -1):
-                row = tracer * LEVELS + level
-                blocks = {}
-                for slot in slots:
-                    code_slot = 1 if slot == 3 else slot
-                    value = temp[row, slot]
-                    if level < LEVELS - 1:
-                        value = value + ratio[level, slot] * below[slot]
-                    below[slot] = value
-                    first, second = lat_weights(substep, row, level, code_slot, slot)
-                    blocks[slot] = sweep_back(value, cy[level, slot], first, second, 1)
-                if substep == SUBSTEPS - 1:
-                    blocks[3] = jnp.zeros_like(blocks[0])
-                if substep == 1:
-                    blocks[1] = jnp.where(col_w < 4, blocks[3], 0.0)
-                    blocks[2] = jnp.where(col_w < 4, 0.0, blocks[3])
-                pieces = [
-                    [blocks[k][:, chunk * LANES : (chunk + 1) * LANES] for k in out_slots] for chunk in range(count_w)
-                ]
-                pieces = lon_sweep(substep, row, level, out_slots, pieces, True)
-                for chunk in range(count_w):
-                    at = slice(chunk * LANES, (chunk + 1) * LANES)
-                    for n, k in enumerate(out_slots):
-                        if substep == 0:
-                            (grad, grad_right, grad_left)[k][row, :, at] = pieces[chunk][n]
-                        else:
-                            q[row, k, :, at] = pieces[chunk][n]
+                for n, tracer in enumerate(members):
+                    row = tracer * LEVELS + level
+                    blocks = {}
+                    for slot in slots:
+                        code_slot = 1 if slot == 3 else slot
+                        value = temp[row, slot]
+                        if level < LEVELS - 1:
+                            value = value + ratio[level, slot] * below[n, slot]
+                        below[n, slot] = value
+                        first, second = lat_weights(substep, row, level, code_slot, slot)
+                        blocks[slot] = sweep_back(value, cy[level, slot], first, second, 1)
+                    if substep == SUBSTEPS - 1:
+                        blocks[3] = jnp.zeros_like(blocks[0])
+                    if substep == 1:
+                        blocks[1] = jnp.where(col_w < 4, blocks[3], 0.0)
+                        blocks[2] = jnp.where(col_w < 4, 0.0, blocks[3])
+                    pieces = [
+                        [blocks[k][:, chunk * LANES : (chunk + 1) * LANES] for k in out_slots] for chunk in range(count_w)
+                    ]
+                    pieces = lon_sweep(substep, row, level, out_slots, pieces, True)
+                    for chunk in range(count_w):
+                        at = slice(chunk * LANES, (chunk + 1) * LANES)
+                        for m, k in enumerate(out_slots):
+                            if substep == 0:
+                                (grad, grad_right, grad_left)[k][row, :, at] = pieces[chunk][m]
+                            else:
+                                q[row, k, :, at] = pieces[chunk][m]
 
     three, two = ((0, 1, 2), (0, 3))
     forward(0, three, three)
@@ -380,9 +390,8 @@
     @pl.loop(0, STATE)
     def _(row):
         for target, source, value in ((final, main_final, outs[0][row]), (grad, main_grad, outs[1][row])):
-            low = pltpu.roll(value, 48, 1)
-            top = pltpu.roll(value, 96, 1)
-            target[row, :, :LANES] = jnp.where(lane < EDGE, low, source[row, :, :LANES])
+            top = pltpu.roll(value, 32, 1)
+            target[row, :, :LANES] = jnp.where(lane < EDGE, value, source[row, :, :LANES])
             target[row, :, LANES:] = jnp.where(lane >= LANES - EDGE, top, source[row, :, LANES:])
 
     for level in range(LEVELS):
@@ -391,8 +400,8 @@
             for tracer in range(TRACERS):
                 value = source[tracer * LEVELS + level]
                 start = 32 * tracer
-                top = pltpu.roll(value, (start + LANES - 16) % LANES, 1)
-                low = pltpu.roll(value, (start + 16 + LANES - 80) % LANES, 1)
+                top = pltpu.roll(value, (start + LANES - 80) % LANES, 1)
+                low = pltpu.roll(value, (start + 16) % LANES, 1)
                 packed = jnp.where(lane >= start, jnp.where(lane < start + 16, top, low), packed)
             target[level] = packed
 
@@ -404,11 +413,10 @@
         for tracer in range(TRACERS):
             row = tracer * LEVELS + level
             start = 32 * tracer
-            top = pltpu.roll(packed, (2 * LANES - 16 - start) % LANES, 1)
-            low = pltpu.roll(packed, (2 * LANES - 16 - start) % LANES, 1)
+            edge = pltpu.roll(packed, (2 * LANES - 16 - start) % LANES, 1)
             total = grad[row] + from_right[row] + from_left[row]
-            out[row, :, :LANES] = total[:, :LANES] + jnp.where(lane < EDGE, low, 0.0)
-            out[row, :, LANES:] = total[:, LANES:] + jnp.where(lane >= LANES - EDGE, top, 0.0)
+            out[row, :, :LANES] = total[:, :LANES] + jnp.where(lane < EDGE, edge, 0.0)
+            out[row, :, LANES:] = total[:, LANES:] + jnp.where(lane >= LANES - EDGE, edge, 0.0)
 
 
 def spec(count, space=pltpu.VMEM):
@@ -452,30 +460,34 @@
         observations.reshape((SUBSTEPS * TRACERS, COLS, ROWS)),
         misfit_weight,
     )
-    copies = [pltpu.VMEM(value.shape, value.dtype) for value in own]
-    right_a, right_b, left_a, left_b, to_north, to_south = call(
+    packed = call(
         pack,
         "pack",
-        (block(72), block(48), block(64), block(40), block(26, LANES), block(26, LANES)),
+        [jax.ShapeDtypeStruct(value.shape, value.dtype) for value in own]
+        + [block(72), block(48), block(64), block(40), block(26, LANES), block(26, LANES)],
         spec(7, pltpu.HBM),
         own,
-        copies + [pltpu.SemaphoreType.DMA((7,))],
-    )
+        [pltpu.SemaphoreType.DMA((7,))],
+    )
+    own, (right_a, right_b, left_a, left_b, to_north, to_south) = (tuple(packed[:7]), packed[7:])
     from_left_a = lax.ppermute(right_a, "lon", east)
     from_right_a = lax.ppermute(left_a, "lon", west)
     south = lax.ppermute(to_north, "lat", up)
     north = lax.ppermute(to_south, "lat", down)
     from_left_b = lax.ppermute(right_b, "lon", east)
+    left_b, from_right_a = lax.optimization_barrier((left_b, from_right_a))
     from_right_b = lax.ppermute(left_b, "lon", west)
-    corner = jnp.concatenate([north[:CORNER], south[:CORNER]], axis=0)
-    corner_l = lax.ppermute(corner, "lon", east)
-    corner_r = lax.ppermute(corner, "lon", west)
     smem = spec(1, pltpu.SMEM)
     owned = own + (column_weights,)
     first = call(
         main_first, "main_first", [block(HALF)] * 4, spec(7) + smem + spec(2),
         owned + (from_left_a, from_right_a), scratch_for(ROWS, PAIR),
     )
+    first, north, south = lax.optimization_barrier((tuple(first), north, south))
+    corner = jnp.concatenate([north[:CORNER], south[:CORNER]], axis=0)
+    first, corner = lax.optimization_barrier((first, corner))
+    corner_l = lax.ppermute(corner, "lon", east)
+    corner_r = lax.ppermute(corner, "lon", west)
     main_final, main_grad, grad_left, grad_right = call(
         main_second, "main_second", [block(STATE)] * 4, spec(7) + smem + spec(8),
         owned + (from_left_a, from_right_a, from_left_b, from_right_b) + tuple(first), scratch_for(ROWS, PAIR),

time: 98.8 us -> 86.3 us (0.87)
  waiting for transfers between devices: 24.4 us -> 19.4 us
  Pallas kernels: 33.7 us -> 29.3 us
  starting transfers between devices: 31.3 us -> 28.7 us
    ppermute x1, waiting for transfers between devices: 7.05 us -> 0.01 us  [shards(): south = lax.ppermute(to_north, 'lat', up)]
    ppermute x1, waiting for transfers between devices: 0.01 us -> 6.74 us  [shards(): from_right_a = lax.ppermute(left_a, 'lon', west)]
    ppermute x1, waiting for transfers between devices: 5.15 us -> 0.01 us  [shards(): north = lax.ppermute(to_south, 'lat', down)]
    pallas_call x5, Pallas kernels: 33.7 us -> 29.3 us  [call(): pl.pallas_call(kernel, out_shape=tuple(outs), in_specs=in_specs, out_spec...]
    ppermute x1, starting transfers between devices: 8.02 us -> 3.85 us  [shards(): corner_r = lax.ppermute(corner, 'lon', west)]
    ppermute x1, starting transfers between devices: 3.93 us -> 6.61 us  [shards(): from_right = lax.ppermute(grad_left, 'lon', west)]
    ppermute x1, starting transfers between devices: 1.93 us -> 0.01 us  [shards(): from_left = lax.ppermute(grad_right, 'lon', east)]
    unnamed x24 -> x16, local copies, waits for them, and re-layouts: 7.01 us -> 7 us
  transfers between devices with their start and end apart: 12 -> 12, of which waited for: 6 -> 5; matrix products, arithmetic and copies ran while one was open for 0% -> 0% of each run, Pallas kernels for 24% -> 22%
where the time goes in v2:
time: 86.3 us; the launch traced here: 85.2 us
  Pallas kernels  29.3 us (34%)
  starting transfers between devices  28.7 us (33%)
  waiting for transfers between devices  19.4 us (22%)
  local copies, waits for them, and re-layouts  7.01 us (8%)
    pallas_call x5, Pallas kernels, call(): pl.pallas_call(kernel, out_shape=tuple(outs), in_specs=in_specs, out_spec...  29.3 us
    unnamed x16, local copies, waits for them, and re-layouts  7 us
    ppermute x1, waiting for transfers between devices, shards(): from_right_a = lax.ppermute(left_a, 'lon', west)  6.74 us
    ppermute x1, starting transfers between devices, shards(): from_right = lax.ppermute(grad_left, 'lon', west)  6.61 us
    ppermute x1, starting transfers between devices, shards(): from_right_a = lax.ppermute(left_a, 'lon', west)  6.3 us
    ppermute x1, starting transfers between devices, shards(): north = lax.ppermute(to_south, 'lat', down)  4.81 us
    ppermute x1, waiting for transfers between devices, shards(): edge_left = lax.ppermute(pack_right, 'lon', east)  4.35 us
    ppermute x1, starting transfers between devices, shards(): from_right_b = lax.ppermute(left_b, 'lon', west)  4.08 us
  transfers between devices with their start and end apart: 12, of which 5 were waited for; matrix products, arithmetic and copies ran while one was open for 0% of the time, Pallas kernels for 22%

profile of v2, /device:TPU:24, one launch (start us, length us, event | category | flops | bytes accessed | tf_op | source)
XLA Modules:
  0.0 85.2 jit_solution(13381071131934503877)
XLA Ops:
  0.6 0.0 copy-start
  0.6 1.2 %copy-done = s32[4,4,8,8,256]{4,3,2,1,0:T(8,128)S(1)} copy-done((s32[4,4,8,8,256]{4,3,2,1,0:T(8,128)S(1)}, s32[4,4,8,8,256]{4,3,2,1,0:T(8,128)}, u32[]{:S(2)}) %copy-start) | copy-done | bytes 1048600
  1.9 0.0 copy-start.1
  1.9 0.9 %copy-done.1 = f32[4,8,8,256]{3,2,1,0:T(8,128)S(1)} copy-done((f32[4,8,8,256]{3,2,1,0:T(8,128)S(1)}, f32[4,8,8,256]{3,2,1,0:T(8,128)}, u32[]{:S(2)}) %copy-start.1) | copy-done | bytes 262168
  2.8 0.0 copy-start.2
  2.8 0.9 %copy-done.2 = f32[4,4,8,256]{3,2,1,0:T(8,128)S(1)} copy-done((f32[4,4,8,256]{3,2,1,0:T(8,128)S(1)}, f32[4,4,8,256]{3,2,1,0:T(8,128)}, u32[]{:S(2)}) %copy-start.2) | copy-done | bytes 131096
  3.7 0.0 copy-start.3
  3.7 0.8 copy-done.3
  4.6 0.0 copy-start.4
  4.6 0.8 copy-done.4
  5.4 0.0 copy-start.5
  5.4 0.8 copy-done.5
  6.2 0.0 copy-start.6
  6.2 0.8 copy-done.6
  7.0 2.6 %pack.1 = (f32[32,8,256]{2,1,0:T(8,128)S(1)}, f32[8,8,256]{2,1,0:T(8,128)S(1)}, f32[8,8,256]{2,1,0:T(8,128)S(1)}, f32[8,8,256]{2,1,0:T(8,128)S(1)}, s32[128,8,25...) custom-call(f32[32,8,256]{2,1,0:T(8,128)S(1)} %bitcast.6, ...), custom_call_target="tpu_custom_call" | custom-call | tf_op jit(solution)/shard_map/pack/pallas_call | solution.py:439
  9.6 6.3 %collective-permute-start.1 = (f32[64,8,256]{2,1,0:T(8,128)S(1)}, f32[64,8,256]{2,1,0:T(8,128)S(1)}, u32[]{:S(2)}, u32[]{:S(2)}) collective-permute-start(f32[64,8,256]{2,1,0:T(8,128)S(1)} %get-tuple-element.49), channel_id=1, source_target_pairs={{1,0},{2,1},{3,2},{4,3},{5,4},{6,5},{7,6},{8,7},{9,8},{10,9},{11,1... | collective-permute-start | bytes 1572872 | tf_op jit(solution)/shard_map/ppermute | solution.py:474
  15.9 0.0 collective-permute-start
  15.9 0.0 collective-permute-start.2
  15.9 6.7 %collective-permute-done.1.refs_9_ = f32[64,8,256]{2,1,0:T(8,128)S(1)} collective-permute-done((f32[64,8,256]{2,1,0:T(8,128)S(1)}, f32[64,8,256]{2,1,0:T(8,128)S(1)}, u32[]{:S(2)}, u32[]{:S(2)}) %collective-permute-start.1) | collective-permute-done | bytes 524320 | tf_op jit(solution)/shard_map/ppermute | solution.py:474
  22.7 4.1 %collective-permute-start.3 = (f32[40,8,256]{2,1,0:T(8,128)S(1)}, f32[40,8,256]{2,1,0:T(8,128)S(1)}, u32[]{:S(2)}, u32[]{:S(2)}) collective-permute-start(f32[40,8,256]{2,1,0:T(8,128)S(1)} %get-tuple-element.52), channel_id=1, source_target_pairs={{1,0},{2,1},{3,2},{4,3},{5,4},{6,5},{7,6},{8,7},{9,8},{10,9},{11,1... | collective-permute-start | bytes 983048 | tf_op jit(solution)/shard_map/ppermute | solution.py:479
  26.7 4.8 %collective-permute-start.4 = (f32[26,8,128]{2,1,0:T(8,128)S(1)}, f32[26,8,128]{2,1,0:T(8,128)S(1)}, u32[]{:S(2)}, u32[]{:S(2)}) collective-permute-start(f32[26,8,128]{2,1,0:T(8,128)S(1)} %get-tuple-element.57), channel_id=1, source_target_pairs={{32,0},{64,32},{96,64},{128,96},{160,128},{192,160},{224,192},{33,... | collective-permute-start | bytes 319496 | tf_op jit(solution)/shard_map/ppermute | solution.py:476
  31.6 2.5 %collective-permute-start.5 = (f32[26,8,128]{2,1,0:T(8,128)S(1)}, f32[26,8,128]{2,1,0:T(8,128)S(1)}, u32[]{:S(2)}, u32[]{:S(2)}) collective-permute-start(f32[26,8,128]{2,1,0:T(8,128)S(1)} %get-tuple-element.58), channel_id=1, source_target_pairs={{0,32},{32,64},{64,96},{96,128},{128,160},{160,192},{192,224},{1,3... | collective-permute-start | bytes 319496 | tf_op jit(solution)/shard_map/ppermute | solution.py:475
  34.1 0.0 collective-permute-done.refs_8_
  34.1 0.0 copy-start.7
  34.1 0.6 copy-done.7
  34.8 7.4 %main_first.1 = (f32[16,8,256]{2,1,0:T(8,128)S(1)}, f32[16,8,256]{2,1,0:T(8,128)S(1)}, f32[16,8,256]{2,1,0:T(8,128)S(1)}, f32[16,8,256]{2,1,0:T(8,128)S(1)}) custom-call(f32[32,8,256]{2,1,0:T(8,128)S(1)} %get-tuple-element.40.refs_0_, f32[8,8,256]{2,1,0:T(8,128)S(1)} %get-tuple-element.41.refs_1_, f32[8,8,256]{2,1,0:T(8,128)S(1)} %get-tuple-element.42.refs_2_, ...), custom_call_target="tpu_custom_call" | custom-call | tf_op jit(solution)/shard_map/main_first/pallas_call | solution.py:439
  42.1 0.0 collective-permute-done.4.refs_12_
  42.2 0.0 collective-permute-done.5.refs_13_
  42.2 0.0 collective-permute-done.2.refs_10_
  42.2 0.0 collective-permute-done.3.refs_11_
  42.2 7.4 %main_second.1 = (f32[32,8,256]{2,1,0:T(8,128)S(1)}, f32[32,8,256]{2,1,0:T(8,128)S(1)}, f32[32,8,256]{2,1,0:T(8,128)S(1)}, f32[32,8,256]{2,1,0:T(8,128)S(1)}) custom-call(f32[32,8,256]{2,1,0:T(8,128)S(1)} %get-tuple-element.40.refs_0_, f32[8,8,256]{2,1,0:T(8,128)S(1)} %get-tuple-element.41.refs_1_, f32[8,8,256]{2,1,0:T(8,128)S(1)} %get-tuple-element.42.refs_2_, ...), custom_call_target="tpu_custom_call" | custom-call | tf_op jit(solution)/shard_map/main_second/pallas_call | solution.py:439
  49.7 6.6 %collective-permute-start.8 = (f32[32,8,256]{2,1,0:T(8,128)S(1)}, f32[32,8,256]{2,1,0:T(8,128)S(1)}, u32[]{:S(2)}, u32[]{:S(2)}) collective-permute-start(f32[32,8,256]{2,1,0:T(8,128)S(1)} %get-tuple-element.74), channel_id=1, source_target_pairs={{1,0},{2,1},{3,2},{4,3},{5,4},{6,5},{7,6},{8,7},{9,8},{10,9},{11,1... | collective-permute-start | bytes 786440 | tf_op jit(solution)/shard_map/ppermute | solution.py:495
  56.3 0.0 collective-permute-start.9
  56.3 3.9 %collective-permute-start.7 = (f32[46,8,128]{2,1,0:T(8,128)S(1)}, f32[46,8,128]{2,1,0:T(8,128)S(1)}, u32[]{:S(2)}, u32[]{:S(2)}) collective-permute-start(f32[46,8,128]{2,1,0:T(8,128)S(1)} %pad_maximum_fusion), channel_id=1, source_target_pairs={{1,0},{2,1},{3,2},{4,3},{5,4},{6,5},{7,6},{8,7},{9,8},{10,9},{11,1... | collective-permute-start | bytes 565256 | tf_op jit(solution)/shard_map/ppermute | solution.py:490
  60.1 0.0 collective-permute-start.6
  60.1 3.1 %collective-permute-done.7.refs_15_ = f32[46,8,128]{2,1,0:T(8,128)S(1)} collective-permute-done((f32[46,8,128]{2,1,0:T(8,128)S(1)}, f32[46,8,128]{2,1,0:T(8,128)S(1)}, u32[]{:S(2)}, u32[]{:S(2)}) %collective-permute-start.7) | collective-permute-done | bytes 188448 | tf_op jit(solution)/shard_map/ppermute | solution.py:490
  63.2 4.0 %collective-permute-done.6.refs_14_ = f32[46,8,128]{2,1,0:T(8,128)S(1)} collective-permute-done((f32[46,8,128]{2,1,0:T(8,128)S(1)}, f32[46,8,128]{2,1,0:T(8,128)S(1)}, u32[]{:S(2)}, u32[]{:S(2)}) %collective-permute-start.6) | collective-permute-done | bytes 188448 | tf_op jit(solution)/shard_map/ppermute | solution.py:489
  67.2 11.1 %strip.1 = (f32[32,8,256]{2,1,0:T(8,128)}, f32[32,8,256]{2,1,0:T(8,128)S(1)}, f32[8,8,128]{2,1,0:T(8,128)S(1)}, f32[8,8,128]{2,1,0:T(8,128)S(1)}) custom-call(f32[32,8,256]{2,1,0:T(8,128)S(1)} %get-tuple-element.40.refs_0_, f32[8,8,256]{2,1,0:T(8,128)S(1)} %get-tuple-element.41.refs_1_, f32[8,8,256]{2,1,0:T(8,128)S(1)} %get-tuple-element.42.refs_2_, ...), custom_call_target="tpu_custom_call" | custom-call | tf_op jit(solution)/shard_map/strip/pallas_call | solution.py:439
  78.3 0.1 collective-permute-start.10
  78.5 0.4 collective-permute-start.11
  78.9 1.2 %collective-permute-done.10.edge_right = f32[8,8,128]{2,1,0:T(8,128)S(1)} collective-permute-done((f32[8,8,128]{2,1,0:T(8,128)S(1)}, f32[8,8,128]{2,1,0:T(8,128)S(1)}, u32[]{:S(2)}, u32[]{:S(2)}) %collective-permute-start.10) | collective-permute-done | bytes 32800 | tf_op jit(solution)/shard_map/ppermute | solution.py:503
  80.1 4.4 %collective-permute-done.11.edge_left = f32[8,8,128]{2,1,0:T(8,128)S(1)} collective-permute-done((f32[8,8,128]{2,1,0:T(8,128)S(1)}, f32[8,8,128]{2,1,0:T(8,128)S(1)}, u32[]{:S(2)}, u32[]{:S(2)}) %collective-permute-start.11) | collective-permute-done | bytes 32800 | tf_op jit(solution)/shard_map/ppermute | solution.py:504
  84.4 0.0 collective-permute-done.8.from_right
  84.4 0.0 collective-permute-done.9.from_left
  84.4 0.8 finish.1
  (3 shorter events, 0.0 us)
Async XLA Ops:
  0.6 1.2 %copy-start = (s32[4,4,8,8,256]{4,3,2,1,0:T(8,128)S(1)}, s32[4,4,8,8,256]{4,3,2,1,0:T(8,128)}, u32[]{:S(2)}) copy-start(s32[4,4,8,8,256]{4,3,2,1,0:T(8,128)} %param.12) | copy-start | bytes 3145732
  1.9 0.9 %copy-start.1 = (f32[4,8,8,256]{3,2,1,0:T(8,128)S(1)}, f32[4,8,8,256]{3,2,1,0:T(8,128)}, u32[]{:S(2)}) copy-start(f32[4,8,8,256]{3,2,1,0:T(8,128)} %param.8) | copy-start | bytes 786436
  2.8 0.9 %copy-start.2 = (f32[4,4,8,256]{3,2,1,0:T(8,128)S(1)}, f32[4,4,8,256]{3,2,1,0:T(8,128)}, u32[]{:S(2)}) copy-start(f32[4,4,8,256]{3,2,1,0:T(8,128)} %param.14) | copy-start | bytes 393220
  3.7 0.8 copy-start.3
  4.6 0.8 copy-start.4
  5.4 0.8 copy-start.5
  6.2 0.8 copy-start.6
  9.6 13.0 %collective-permute-start.1 = (f32[64,8,256]{2,1,0:T(8,128)S(1)}, f32[64,8,256]{2,1,0:T(8,128)S(1)}, u32[]{:S(2)}, u32[]{:S(2)}) collective-permute-start(f32[64,8,256]{2,1,0:T(8,128)S(1)} %get-tuple-element.49), channel_id=1, source_target_pairs={{1,0},{2,1},{3,2},{4,3},{5,4},{6,5},{7,6},{8,7},{9,8},{10,9},{11,1... | collective-permute-start | bytes 1572872 | tf_op jit(solution)/shard_map/ppermute | solution.py:474
  15.9 18.2 %collective-permute-start = (f32[72,8,256]{2,1,0:T(8,128)S(1)}, f32[72,8,256]{2,1,0:T(8,128)S(1)}, u32[]{:S(2)}, u32[]{:S(2)}) collective-permute-start(f32[72,8,256]{2,1,0:T(8,128)S(1)} %get-tuple-element.47), channel_id=1, source_target_pairs={{0,1},{1,2},{2,3},{3,4},{4,5},{5,6},{6,7},{7,8},{8,9},{9,10},{10,1... | collective-permute-start | bytes 1769480 | tf_op jit(solution)/shard_map/ppermute | solution.py:473
  15.9 26.3 %collective-permute-start.2 = (f32[48,8,256]{2,1,0:T(8,128)S(1)}, f32[48,8,256]{2,1,0:T(8,128)S(1)}, u32[]{:S(2)}, u32[]{:S(2)}) collective-permute-start(f32[48,8,256]{2,1,0:T(8,128)S(1)} %get-tuple-element.51), channel_id=1, source_target_pairs={{0,1},{1,2},{2,3},{3,4},{4,5},{5,6},{6,7},{7,8},{8,9},{9,10},{10,1... | collective-permute-start | bytes 1179656 | tf_op jit(solution)/shard_map/ppermute | solution.py:477
  22.7 19.6 %collective-permute-start.3 = (f32[40,8,256]{2,1,0:T(8,128)S(1)}, f32[40,8,256]{2,1,0:T(8,128)S(1)}, u32[]{:S(2)}, u32[]{:S(2)}) collective-permute-start(f32[40,8,256]{2,1,0:T(8,128)S(1)} %get-tuple-element.52), channel_id=1, source_target_pairs={{1,0},{2,1},{3,2},{4,3},{5,4},{6,5},{7,6},{8,7},{9,8},{10,9},{11,1... | collective-permute-start | bytes 983048 | tf_op jit(solution)/shard_map/ppermute | solution.py:479
  26.7 15.4 %collective-permute-start.4 = (f32[26,8,128]{2,1,0:T(8,128)S(1)}, f32[26,8,128]{2,1,0:T(8,128)S(1)}, u32[]{:S(2)}, u32[]{:S(2)}) collective-permute-start(f32[26,8,128]{2,1,0:T(8,128)S(1)} %get-tuple-element.57), channel_id=1, source_target_pairs={{32,0},{64,32},{96,64},{128,96},{160,128},{192,160},{224,192},{33,... | collective-permute-start | bytes 319496 | tf_op jit(solution)/shard_map/ppermute | solution.py:476
  31.6 10.6 %collective-permute-start.5 = (f32[26,8,128]{2,1,0:T(8,128)S(1)}, f32[26,8,128]{2,1,0:T(8,128)S(1)}, u32[]{:S(2)}, u32[]{:S(2)}) collective-permute-start(f32[26,8,128]{2,1,0:T(8,128)S(1)} %get-tuple-element.58), channel_id=1, source_target_pairs={{0,32},{32,64},{64,96},{96,128},{128,160},{160,192},{192,224},{1,3... | collective-permute-start | bytes 319496 | tf_op jit(solution)/shard_map/ppermute | solution.py:475
  34.1 0.7 copy-start.7
  49.7 34.8 %collective-permute-start.8 = (f32[32,8,256]{2,1,0:T(8,128)S(1)}, f32[32,8,256]{2,1,0:T(8,128)S(1)}, u32[]{:S(2)}, u32[]{:S(2)}) collective-permute-start(f32[32,8,256]{2,1,0:T(8,128)S(1)} %get-tuple-element.74), channel_id=1, source_target_pairs={{1,0},{2,1},{3,2},{4,3},{5,4},{6,5},{7,6},{8,7},{9,8},{10,9},{11,1... | collective-permute-start | bytes 786440 | tf_op jit(solution)/shard_map/ppermute | solution.py:495
  56.3 28.1 %collective-permute-start.9 = (f32[32,8,256]{2,1,0:T(8,128)S(1)}, f32[32,8,256]{2,1,0:T(8,128)S(1)}, u32[]{:S(2)}, u32[]{:S(2)}) collective-permute-start(f32[32,8,256]{2,1,0:T(8,128)S(1)} %get-tuple-element.75), channel_id=1, source_target_pairs={{0,1},{1,2},{2,3},{3,4},{4,5},{5,6},{6,7},{7,8},{8,9},{9,10},{10,1... | collective-permute-start | bytes 786440 | tf_op jit(solution)/shard_map/ppermute | solution.py:496
  56.3 7.0 %collective-permute-start.7 = (f32[46,8,128]{2,1,0:T(8,128)S(1)}, f32[46,8,128]{2,1,0:T(8,128)S(1)}, u32[]{:S(2)}, u32[]{:S(2)}) collective-permute-start(f32[46,8,128]{2,1,0:T(8,128)S(1)} %pad_maximum_fusion), channel_id=1, source_target_pairs={{1,0},{2,1},{3,2},{4,3},{5,4},{6,5},{7,6},{8,7},{9,8},{10,9},{11,1... | collective-permute-start | bytes 565256 | tf_op jit(solution)/shard_map/ppermute | solution.py:490
  60.1 7.1 %collective-permute-start.6 = (f32[46,8,128]{2,1,0:T(8,128)S(1)}, f32[46,8,128]{2,1,0:T(8,128)S(1)}, u32[]{:S(2)}, u32[]{:S(2)}) collective-permute-start(f32[46,8,128]{2,1,0:T(8,128)S(1)} %pad_maximum_fusion), channel_id=1, source_target_pairs={{0,1},{1,2},{2,3},{3,4},{4,5},{5,6},{6,7},{7,8},{8,9},{9,10},{10,1... | collective-permute-start | bytes 565256 | tf_op jit(solution)/shard_map/ppermute | solution.py:489
  78.3 1.7 %collective-permute-start.10 = (f32[8,8,128]{2,1,0:T(8,128)S(1)}, f32[8,8,128]{2,1,0:T(8,128)S(1)}, u32[]{:S(2)}, u32[]{:S(2)}) collective-permute-start(f32[8,8,128]{2,1,0:T(8,128)S(1)} %get-tuple-element.76), channel_id=1, source_target_pairs={{1,0},{2,1},{3,2},{4,3},{5,4},{6,5},{7,6},{8,7},{9,8},{10,9},{11,1... | collective-permute-start | bytes 98312 | tf_op jit(solution)/shard_map/ppermute | solution.py:503
  78.5 6.0 %collective-permute-start.11 = (f32[8,8,128]{2,1,0:T(8,128)S(1)}, f32[8,8,128]{2,1,0:T(8,128)S(1)}, u32[]{:S(2)}, u32[]{:S(2)}) collective-permute-start(f32[8,8,128]{2,1,0:T(8,128)S(1)} %get-tuple-element.77), channel_id=1, source_target_pairs={{0,1},{1,2},{2,3},{3,4},{4,5},{5,6},{6,7},{7,8},{8,9},{9,10},{10,1... | collective-permute-start | bytes 98312 | tf_op jit(solution)/shard_map/ppermute | solution.py:504

commit v3 on v2

--- a/solution.py
+++ b/solution.py
@@ -1,3 +1,5 @@
+import functools
+
 import jax
 import jax.numpy as jnp
 from jax import lax
@@ -7,11 +9,11 @@
 
 TRACERS, LEVELS, SUBSTEPS = 4, 8, 4
 PAIR = 2
-TOGETHER = {1: 2, 2: 1}
 COLS, ROWS, EDGE, LANES = 8, 256, 16, 128
 STATE = TRACERS * LEVELS
 HALF = PAIR * LEVELS
 LIMIT = 24 * 1024 * 1024
+PACK_LIMIT = 60 * 1024 * 1024
 CORNER = 23
 
 
@@ -23,15 +25,19 @@
     return lax.broadcasted_iota(jnp.int32, (COLS, lanes), 0)
 
 
-def pack(*refs):
-    hbm, own, (right_a, right_b, left_a, left_b, to_north, to_south), sems = (refs[:7], refs[7:14], refs[14:20], refs[20])
-    copies = [pltpu.make_async_copy(hbm[k], own[k], sems.at[k]) for k in range(7)]
+def fetch(hbm, own, sems):
+    copies = [pltpu.make_async_copy(source, target, sems.at[k]) for k, (source, target) in enumerate(zip(hbm, own))]
     for copy in copies:
         copy.start()
     for copy in copies:
         copy.wait()
-    ck, cl, ct, mx, fl, obs, mw = own
-    lane, col = (lane_ids(), col_ids(ROWS))
+
+
+def pack_lon(*refs):
+    hbm, (right_a, right_b, left_a, left_b), own, sems = (refs[:5], refs[6:10], refs[10:15], refs[15])
+    fetch(hbm, own, sems)
+    ck, cl, ct, mx, fl = own
+    col = col_ids(ROWS)
     for half, (to_right, to_left) in enumerate(((right_a, left_a), (right_b, left_b))):
         to_right[0:HALF] = ck[half * HALF : (half + 1) * HALF]
         to_left[0:HALF] = ck[half * HALF : (half + 1) * HALF]
@@ -54,13 +60,20 @@
         right_a[3 * HALF + 8 * k : 3 * HALF + 8 * k + 8] = field[...]
         left_a[40 + 8 * k : 48 + 8 * k] = field[...]
 
+
+def pack_lat(*refs):
+    hbm, (to_north, to_south), own, sems = (refs[:7], refs[7:9], refs[9:16], refs[16])
+    fetch(hbm, own, sems)
+    ck, cl, ct, mx, fl, obs, mw = own
+    lane = lane_ids()
+
     def strips(place, read, count):
         north = jnp.zeros((COLS, LANES), jnp.float32)
         south = north
         for k in range(count):
             whole = read(k)
             here = lane // EDGE
-            north = jnp.where(here == (k + 1) % 8, pltpu.roll(whole[:, LANES:], (EDGE * (k + 2)) % LANES, 1), north)
+            north = jnp.where(here == (k + 7) % 8, pltpu.roll(whole[:, LANES:], EDGE * k, 1), north)
             south = jnp.where(here == k, pltpu.roll(whole[:, :LANES], EDGE * k, 1), south)
         to_north[place] = north
         to_south[place] = south
@@ -79,6 +92,12 @@
     for half in range(2):
         strips(23 + half, lambda k, half=half: obs[half * 8 + k], 8)
     strips(25, lambda k: mw[k], TRACERS)
+
+
+def join(*refs):
+    north, south, out = (refs[7], refs[8], refs[9])
+    out[0:CORNER] = north[0:CORNER]
+    out[CORNER : 2 * CORNER] = south[0:CORNER]
 
 
 def behind(value, axis):
@@ -116,7 +135,8 @@
     return c_minus, c_minus + slope, slope
 
 
-def window(width, groups, own, edges, outs, scratch):
+def window(groups, own, edges, outs, scratch):
+    width, together = (ROWS + LANES, 1)
     ck, cl, ct, mx, fl, obs, mw, cw = own
     final, grad, grad_left, grad_right = outs
     (
@@ -125,27 +145,23 @@
     ) = scratch
     lane, col_w = (lane_ids(), col_ids(width))
     strip_of = lane // EDGE
+    rim = (lane < EDGE) | (lane >= LANES - EDGE)
     count_w = width // LANES
-    together = TOGETHER[count_w]
     tracers = PAIR * len(groups)
     offset = groups[0][0]
     static_left, static_right = groups[0][3:5]
 
     def spread(value, which, place, k):
-        if edges is None:
-            return value
         north, south = edges[which]
-        halo = pltpu.roll(jnp.where(strip_of == k, north[place], south(place)), (96 + LANES - EDGE * k) % LANES, 1)
-        top = pltpu.roll(value[:, LANES:], 96, 1)
-        inner = jnp.where(lane < 32, value[:, :LANES], jnp.where(lane < 64, 0.0, top))
-        return jnp.where(lane < 96, inner, halo)
+        halo = pltpu.roll(jnp.where(strip_of == k, north[place], south(place)), (LANES - EDGE * k) % LANES, 1)
+        return jnp.concatenate([value, jnp.where(rim, halo, 0.0)], axis=1)
 
     def squeeze(right, left):
         return jnp.where(col_w < 4, right, left)
 
     lane_w = lax.broadcasted_iota(jnp.int32, (COLS, width), 1)
     last = lax.axis_index("lat") == lax.axis_size("lat") - 1
-    pole = (lane_w == (ROWS - 1 if edges is None else 95)) & last
+    pole = (lane_w == ROWS - 1) & last
     carry = [None] * 4
     for level in range(LEVELS):
         def blocks(field, k):
@@ -276,7 +292,7 @@
                             part = cw[level] * value
                             column[n] = part if level == LEVELS - 1 else column[n] + part
                         if substep == SUBSTEPS - 1:
-                            final[row] = value
+                            final[row] = value[:, :ROWS]
                         else:
                             q[row, slot] = value
             for n, tracer in enumerate(members):
@@ -322,10 +338,10 @@
                         blocks[1] = jnp.where(col_w < 4, blocks[3], 0.0)
                         blocks[2] = jnp.where(col_w < 4, 0.0, blocks[3])
                     pieces = [
-                        [blocks[k][:, chunk * LANES : (chunk + 1) * LANES] for k in out_slots] for chunk in range(count_w)
+                        [blocks[k][:, chunk * LANES : (chunk + 1) * LANES] for k in out_slots] for chunk in range(count_w if substep else 2)
                     ]
                     pieces = lon_sweep(substep, row, level, out_slots, pieces, True)
-                    for chunk in range(count_w):
+                    for chunk in range(len(pieces)):
                         at = slice(chunk * LANES, (chunk + 1) * LANES)
                         for m, k in enumerate(out_slots):
                             if substep == 0:
@@ -344,79 +360,34 @@
     backward(0, three, three)
 
 
-def keep_inner(value):
-    lane = lax.broadcasted_iota(jnp.int32, (COLS, ROWS), 1)
-    return jnp.where((lane >= EDGE) & (lane < ROWS - EDGE), value, 0.0)
-
-
-def main_first(*refs):
-    own, (left_a, right_a), outs, scratch = (refs[:8], refs[8:10], refs[10:14], refs[14:])
-    window(ROWS, [(0, left_a, right_a, left_a, right_a)], own, None, outs, scratch)
-    for ref in outs[2:]:
-        @pl.loop(0, HALF)
-        def _(row):
-            ref[row] = keep_inner(ref[row])
-
-
-def main_second(*refs):
-    own, (left_a, right_a, left_b, right_b), before, outs, scratch = (
-        refs[:8], refs[8:12], refs[12:16], refs[16:20], refs[20:]
-    )
-    parts = [ref.at[HALF:STATE] for ref in outs]
-    for ref, old in zip(outs, before):
-        ref[0:HALF] = old[...]
-    window(ROWS, [(PAIR, left_b, right_b, left_a, right_a)], own, None, parts, scratch)
-    for ref in outs[2:]:
-        @pl.loop(HALF, STATE)
-        def _(row):
-            ref[row] = keep_inner(ref[row])
-
-
-def strip(*refs):
-    own, (left_a, right_a, left_b, right_b, north, south, corner_l, corner_r), (main_final, main_grad) = (
-        refs[:8], refs[8:16], refs[16:18]
-    )
-    final, grad, pack_left, pack_right = refs[18:22]
-    outs, scratch = (refs[22:26], refs[26:])
+def halves(half, *refs):
+    own, (left_a, right_a), (north, south, corner_l, corner_r) = (refs[:8], refs[8:10], refs[10:14])
+    refs = refs[14:]
     edges = (
         (north, lambda k: south[k]),
         (corner_l, lambda k: corner_l[CORNER + k]),
         (corner_r, lambda k: corner_r[CORNER + k]),
     )
-    groups = [(0, left_a, right_a, left_a, right_a), (PAIR, left_b, right_b, left_a, right_a)]
-    window(LANES, groups, own, edges, outs, scratch)
-    lane = lane_ids()
-
-    @pl.loop(0, STATE)
-    def _(row):
-        for target, source, value in ((final, main_final, outs[0][row]), (grad, main_grad, outs[1][row])):
-            top = pltpu.roll(value, 32, 1)
-            target[row, :, :LANES] = jnp.where(lane < EDGE, value, source[row, :, :LANES])
-            target[row, :, LANES:] = jnp.where(lane >= LANES - EDGE, top, source[row, :, LANES:])
-
-    for level in range(LEVELS):
-        for target, source in ((pack_left, outs[2]), (pack_right, outs[3])):
-            packed = jnp.zeros((COLS, LANES), jnp.float32)
-            for tracer in range(TRACERS):
-                value = source[tracer * LEVELS + level]
-                start = 32 * tracer
-                top = pltpu.roll(value, (start + LANES - 80) % LANES, 1)
-                low = pltpu.roll(value, (start + 16) % LANES, 1)
-                packed = jnp.where(lane >= start, jnp.where(lane < start + 16, top, low), packed)
-            target[level] = packed
-
-
-def finish(grad, from_right, from_left, edge_right, edge_left, out):
-    lane = lane_ids()
-    for level in range(LEVELS):
-        packed = edge_right[level] + edge_left[level]
-        for tracer in range(TRACERS):
-            row = tracer * LEVELS + level
-            start = 32 * tracer
-            edge = pltpu.roll(packed, (2 * LANES - 16 - start) % LANES, 1)
-            total = grad[row] + from_right[row] + from_left[row]
-            out[row, :, :LANES] = total[:, :LANES] + jnp.where(lane < EDGE, edge, 0.0)
-            out[row, :, LANES:] = total[:, LANES:] + jnp.where(lane >= LANES - EDGE, edge, 0.0)
+    if half == 0:
+        outs, scratch = (refs[:4], refs[4:])
+        groups = [(0, left_a, right_a, left_a, right_a)]
+    else:
+        left_b, right_b, before = refs[:3]
+        final, outs, scratch = (refs[3], refs[4:7], refs[7:])
+        final[0:HALF] = before[...]
+        outs = (final.at[HALF:STATE],) + tuple(outs)
+        groups = [(PAIR, left_b, right_b, left_a, right_a)]
+    window(groups, own, edges, outs, scratch)
+
+
+def finish(*refs):
+    out = refs[6]
+    for half in range(2):
+        own, right, left = refs[3 * half : 3 * half + 3]
+
+        @pl.loop(0, HALF)
+        def _(row):
+            out[half * HALF + row] = own[row] + right[row] + left[row]
 
 
 def spec(count, space=pltpu.VMEM):
@@ -435,14 +406,14 @@
     def block(rows, lanes=ROWS):
         return jax.ShapeDtypeStruct((rows, COLS, lanes), jnp.float32)
 
-    def call(kernel, name, outs, in_specs, operands, scratch=(), cost=0):
+    def call(kernel, name, outs, in_specs, operands, scratch=(), limit=LIMIT):
         return pl.pallas_call(
             kernel,
             out_shape=tuple(outs),
             in_specs=in_specs,
             out_specs=tuple(spec(len(outs))),
             scratch_shapes=list(scratch),
-            compiler_params=pltpu.CompilerParams(vmem_limit_bytes=LIMIT),
+            compiler_params=pltpu.CompilerParams(vmem_limit_bytes=limit),
             name=name,
         )(*operands)
 
@@ -460,49 +431,45 @@
         observations.reshape((SUBSTEPS * TRACERS, COLS, ROWS)),
         misfit_weight,
     )
-    packed = call(
-        pack,
-        "pack",
-        [jax.ShapeDtypeStruct(value.shape, value.dtype) for value in own]
-        + [block(72), block(48), block(64), block(40), block(26, LANES), block(26, LANES)],
-        spec(7, pltpu.HBM),
-        own,
-        [pltpu.SemaphoreType.DMA((7,))],
-    )
-    own, (right_a, right_b, left_a, left_b, to_north, to_south) = (tuple(packed[:7]), packed[7:])
+    hbm = spec(1, pltpu.HBM)
+    held = [pltpu.VMEM(value.shape, value.dtype) for value in own]
+    to_north, to_south = call(
+        pack_lat, "pack_lat", [block(26, LANES)] * 2, hbm * 7, own, held + [pltpu.SemaphoreType.DMA((7,))], limit=PACK_LIMIT
+    )
+    right_a, right_b, left_a, left_b = call(
+        pack_lon, "pack_lon", [block(72), block(48), block(64), block(40)], hbm * 6, own[:5] + (to_north,),
+        held[:5] + [pltpu.SemaphoreType.DMA((5,))], limit=PACK_LIMIT,
+    )
+    south = lax.ppermute(to_north, "lat", up)
+    north = lax.ppermute(to_south, "lat", down)
     from_left_a = lax.ppermute(right_a, "lon", east)
     from_right_a = lax.ppermute(left_a, "lon", west)
-    south = lax.ppermute(to_north, "lat", up)
-    north = lax.ppermute(to_south, "lat", down)
+    (corner,) = call(join, "join", [block(2 * CORNER, LANES)], spec(9), own + (north, south))
+    corner_l = lax.ppermute(corner, "lon", east)
+    corner_r = lax.ppermute(corner, "lon", west)
+    from_left_a, from_right_a, corner_l, corner_r, right_b, left_b = lax.optimization_barrier(
+        (from_left_a, from_right_a, corner_l, corner_r, right_b, left_b)
+    )
     from_left_b = lax.ppermute(right_b, "lon", east)
-    left_b, from_right_a = lax.optimization_barrier((left_b, from_right_a))
     from_right_b = lax.ppermute(left_b, "lon", west)
     smem = spec(1, pltpu.SMEM)
-    owned = own + (column_weights,)
-    first = call(
-        main_first, "main_first", [block(HALF)] * 4, spec(7) + smem + spec(2),
-        owned + (from_left_a, from_right_a), scratch_for(ROWS, PAIR),
-    )
-    first, north, south = lax.optimization_barrier((tuple(first), north, south))
-    corner = jnp.concatenate([north[:CORNER], south[:CORNER]], axis=0)
-    first, corner = lax.optimization_barrier((first, corner))
-    corner_l = lax.ppermute(corner, "lon", east)
-    corner_r = lax.ppermute(corner, "lon", west)
-    main_final, main_grad, grad_left, grad_right = call(
-        main_second, "main_second", [block(STATE)] * 4, spec(7) + smem + spec(8),
-        owned + (from_left_a, from_right_a, from_left_b, from_right_b) + tuple(first), scratch_for(ROWS, PAIR),
-    )
-    from_right = lax.ppermute(grad_left, "lon", west)
-    from_left = lax.ppermute(grad_right, "lon", east)
-    narrow = [pltpu.VMEM((STATE, COLS, LANES), jnp.float32)] * 4
-    final, grad, pack_left, pack_right = call(
-        strip, "strip", [block(STATE)] * 2 + [block(LEVELS, LANES)] * 2, spec(7) + smem + spec(10),
-        owned + (from_left_a, from_right_a, from_left_b, from_right_b, north, south, corner_l, corner_r, main_final, main_grad),
-        narrow + scratch_for(LANES, TRACERS),
-    )
-    edge_right = lax.ppermute(pack_left, "lon", west)
-    edge_left = lax.ppermute(pack_right, "lon", east)
-    (grad,) = call(finish, "finish", [block(STATE)], spec(5), (grad, from_right, from_left, edge_right, edge_left))
+    operands = own + (column_weights, from_left_a, from_right_a, north, south, corner_l, corner_r)
+    final_a, grad_a, gl_a, gr_a = call(
+        functools.partial(halves, 0), "window_first", [block(HALF)] * 4, spec(7) + smem + spec(6), operands,
+        scratch_for(ROWS + LANES, PAIR),
+    )
+    from_right_1 = lax.ppermute(gl_a, "lon", west)
+    from_left_1 = lax.ppermute(gr_a, "lon", east)
+    final, grad_b, gl_b, gr_b = call(
+        functools.partial(halves, 1), "window_second", [block(STATE)] + [block(HALF)] * 3, spec(7) + smem + spec(9),
+        operands + (from_left_b, from_right_b, final_a), scratch_for(ROWS + LANES, PAIR),
+    )
+    from_right_2 = lax.ppermute(gl_b, "lon", west)
+    from_left_2 = lax.ppermute(gr_b, "lon", east)
+    (grad,) = call(
+        finish, "finish", [block(STATE)], spec(6),
+        (grad_a, from_right_1, from_left_1, grad_b, from_right_2, from_left_2),
+    )
     return (final.reshape(checkpoint.shape), grad.reshape(checkpoint.shape))
 
 

time: 86.3 us -> 78.2 us (0.906); the launches traced: 85.2 us -> 78 us
  local copies, waits for them, and re-layouts: 7.01 us -> 0.06 us
  starting transfers between devices: 28.7 us -> 22.8 us
  waiting for transfers between devices: 19.4 us -> 23.9 us
  Pallas kernels: 29.3 us -> 30.5 us
    unnamed x16 -> x20, local copies, waits for them, and re-layouts: 7 us -> 0.06 us
    ppermute x1, waiting for transfers between devices: 6.74 us -> 0.01 us  [shards(): from_right_a = lax.ppermute(left_a, 'lon', west)]
    ppermute x1, waiting for transfers between devices: 0.01 us -> 4.84 us  [shards(): south = lax.ppermute(to_north, 'lat', up)]
    ppermute x1, starting transfers between devices: 3.85 us -> 0.79 us  [shards(): corner_r = lax.ppermute(corner, 'lon', west)]
    ppermute x1, waiting for transfers between devices: 0.01 us -> 3.03 us  [shards(): north = lax.ppermute(to_south, 'lat', down)]
    ppermute x4, starting transfers between devices: 7.12 us -> 4.2 us  [the longest x1 3.62 us: shards(): from_right_2 = lax.ppermute(gl_b, 'lon', west)]
    ppermute x1, waiting for transfers between devices: 4.02 us -> 6.38 us  [shards(): corner_l = lax.ppermute(corner, 'lon', east)]
    pallas_call x5 -> x6, Pallas kernels: 29.3 us -> 30.5 us  [call(): pl.pallas_call(kernel, out_shape=tuple(outs), in_specs=in_specs, out_spec...]
  transfers between devices with their start and end apart: 12 -> 12, of which waited for: 5 -> 6; matrix products, arithmetic and copies ran while one was open for 0% -> 0% of each run, Pallas kernels for 22% -> 29%
where the time goes in v3:
time: 78.2 us; the launch traced here: 78 us
  Pallas kernels  30.5 us (39%)
  waiting for transfers between devices  23.9 us (31%)
  starting transfers between devices  22.8 us (29%)
  between operations  0.82 us (1%)
    pallas_call x6, Pallas kernels, call(): pl.pallas_call(kernel, out_shape=tuple(outs), in_specs=in_specs, out_spec...  30.5 us
    ppermute x1, waiting for transfers between devices, shards(): corner_l = lax.ppermute(corner, 'lon', east)  6.38 us
    ppermute x1, starting transfers between devices, shards(): from_right_a = lax.ppermute(left_a, 'lon', west)  6.3 us
    ppermute x1, starting transfers between devices, shards(): north = lax.ppermute(to_south, 'lat', down)  4.94 us
    ppermute x1, waiting for transfers between devices, shards(): south = lax.ppermute(to_north, 'lat', up)  4.84 us
    ppermute x1, waiting for transfers between devices, shards(): from_left_2 = lax.ppermute(gr_b, 'lon', east)  3.98 us
    ppermute x1, starting transfers between devices, shards(): from_right_b = lax.ppermute(left_b, 'lon', west)  3.83 us
    ppermute x1, starting transfers between devices, shards(): from_right_2 = lax.ppermute(gl_b, 'lon', west)  3.62 us
  transfers between devices with their start and end apart: 12, of which 6 were waited for; matrix products, arithmetic and copies ran while one was open for 0% of the time, Pallas kernels for 29%

profile of v3, /device:TPU:24, one launch (start us, length us, event | category | flops | bytes accessed | tf_op | source)
XLA Modules:
  0.0 78.0 jit_solution(11782868027281451299)
XLA Ops:
  0.6 0.0 copy-start.5
  0.6 4.0 %pack_lat.1 = (f32[26,8,128]{2,1,0:T(8,128)}, f32[26,8,128]{2,1,0:T(8,128)}) custom-call(f32[32,8,256]{2,1,0:T(8,128)} %bitcast.10, f32[8,8,256]{2,1,0:T(8,128)} %refs_1_.9, f32[8,8,256]{2,1,0:T(8,128)} %refs_2_.9, f32[8,8,256]{2,1,0:T(8,128)} %refs_3_.9, s32[128,8,256]{2,1,0:T(8,128)} %bitcast.5, f32[16,8,256]{2,1,0:T(8,128)} %bitcast.15, f32[4,8,256]{2,1,0:T(8,128)} %refs_6_.7), custom_call_target="tpu_custom_call" | custom-call | tf_op jit(solution)/shard_map/pack_lat/pallas_call | solution.py:410
  4.6 0.0 copy-start
  4.6 0.0 copy-start.1
  4.6 0.0 copy-start.2
  4.6 0.0 copy-start.3
  4.7 0.0 copy-start.4
  4.7 0.0 copy-start.6
  4.7 3.0 %pack_lon.1 = (f32[72,8,256]{2,1,0:T(8,128)}, f32[48,8,256]{2,1,0:T(8,128)}, f32[64,8,256]{2,1,0:T(8,128)}, f32[40,8,256]{2,1,0:T(8,128)}) custom-call(f32[32,8,256]{2,1,0:T(8,128)} %bitcast.11, f32[8,8,256]{2,1,0:T(8,128)} %refs_1_.9, f32[8,8,256]{2,1,0:T(8,128)} %refs_2_.9, f32[8,8,256]{2,1,0:T(8,128)} %refs_3_.9, s32[128,8,256]{2,1,0:T(8,128)} %bitcast.6, ...), custom_call_target="tpu_custom_call" | custom-call | tf_op jit(solution)/shard_map/pack_lon/pallas_call | solution.py:410
  7.6 0.1 collective-permute-start
  7.7 6.3 %collective-permute-start.1 = (f32[64,8,256]{2,1,0:T(8,128)}, f32[64,8,256]{2,1,0:T(8,128)S(1)}, u32[]{:S(2)}, u32[]{:S(2)}) collective-permute-start(f32[64,8,256]{2,1,0:T(8,128)} %get-tuple-element.24), channel_id=1, source_target_pairs={{1,0},{2,1},{3,2},{4,3},{5,4},{6,5},{7,6},{8,7},{9,8},{10,9},{11,1... | collective-permute-start | bytes 1572872 | tf_op jit(solution)/shard_map/ppermute | solution.py:446
  14.0 0.0 copy-start.8
  14.0 0.0 copy-start.9
  14.0 4.9 %collective-permute-start.2 = (f32[26,8,128]{2,1,0:T(8,128)}, f32[26,8,128]{2,1,0:T(8,128)S(1)}, u32[]{:S(2)}, u32[]{:S(2)}) collective-permute-start(f32[26,8,128]{2,1,0:T(8,128)} %get-tuple-element.25), channel_id=1, source_target_pairs={{32,0},{64,32},{96,64},{128,96},{160,128},{192,160},{224,192},{33,... | collective-permute-start | bytes 319496 | tf_op jit(solution)/shard_map/ppermute | solution.py:444
  19.0 2.5 %collective-permute-start.3 = (f32[26,8,128]{2,1,0:T(8,128)}, f32[26,8,128]{2,1,0:T(8,128)S(1)}, u32[]{:S(2)}, u32[]{:S(2)}) collective-permute-start(f32[26,8,128]{2,1,0:T(8,128)} %get-tuple-element.22.refs_5_), channel_id=1, source_target_pairs={{0,32},{32,64},{64,96},{96,128},{128,160},{160,192},{192,224},{1,3... | collective-permute-start | bytes 319496 | tf_op jit(solution)/shard_map/ppermute | solution.py:443
  21.5 3.0 %collective-permute-done.2.refs_7_.refs_10_ = f32[26,8,128]{2,1,0:T(8,128)S(1)} collective-permute-done((f32[26,8,128]{2,1,0:T(8,128)}, f32[26,8,128]{2,1,0:T(8,128)S(1)}, u32[]{:S(2)}, u32[]{:S(2)}) %collective-permute-start.2) | collective-permute-done | bytes 106528 | tf_op jit(solution)/shard_map/ppermute | solution.py:444
  24.6 4.8 %collective-permute-done.3.refs_8_.refs_11_ = f32[26,8,128]{2,1,0:T(8,128)S(1)} collective-permute-done((f32[26,8,128]{2,1,0:T(8,128)}, f32[26,8,128]{2,1,0:T(8,128)S(1)}, u32[]{:S(2)}, u32[]{:S(2)}) %collective-permute-start.3) | collective-permute-done | bytes 106528 | tf_op jit(solution)/shard_map/ppermute | solution.py:443
  29.4 0.0 copy-done.5
  29.4 0.0 copy-done
  29.4 0.0 copy-done.1
  29.4 0.0 copy-done.2
  29.4 0.0 copy-done.3
  29.4 0.0 copy-done.4
  29.4 0.0 copy-done.6
  29.5 0.8 %collective-permute-start.5 = (f32[46,8,128]{2,1,0:T(8,128)S(1)}, f32[46,8,128]{2,1,0:T(8,128)S(1)}, u32[]{:S(2)}, u32[]{:S(2)}) collective-permute-start(f32[46,8,128]{2,1,0:T(8,128)S(1)} %join.1), channel_id=1, source_target_pairs={{1,0},{2,1},{3,2},{4,3},{5,4},{6,5},{7,6},{8,7},{9,8},{10,9},{11,1... | collective-permute-start | bytes 565256 | tf_op jit(solution)/shard_map/ppermute | solution.py:449
  30.3 0.0 collective-permute-start.4
  30.3 3.1 %collective-permute-done.5.refs_13_ = f32[46,8,128]{2,1,0:T(8,128)S(1)} collective-permute-done((f32[46,8,128]{2,1,0:T(8,128)S(1)}, f32[46,8,128]{2,1,0:T(8,128)S(1)}, u32[]{:S(2)}, u32[]{:S(2)}) %collective-permute-start.5) | collective-permute-done | bytes 188448 | tf_op jit(solution)/shard_map/ppermute | solution.py:449
  33.4 6.4 %collective-permute-done.4.refs_12_ = f32[46,8,128]{2,1,0:T(8,128)S(1)} collective-permute-done((f32[46,8,128]{2,1,0:T(8,128)S(1)}, f32[46,8,128]{2,1,0:T(8,128)S(1)}, u32[]{:S(2)}, u32[]{:S(2)}) %collective-permute-start.4) | collective-permute-done | bytes 188448 | tf_op jit(solution)/shard_map/ppermute | solution.py:448
  39.7 0.0 collective-permute-done.1.refs_9_
  39.7 0.0 collective-permute-done.refs_8_
  39.7 0.0 copy-start.7
  39.7 0.0 copy-done.8
  39.8 0.1 collective-permute-start.6
  39.9 0.0 copy-done.9
  39.9 3.8 %collective-permute-start.7 = (f32[40,8,256]{2,1,0:T(8,128)S(1)}, f32[40,8,256]{2,1,0:T(8,128)S(1)}, u32[]{:S(2)}, u32[]{:S(2)}) collective-permute-start(f32[40,8,256]{2,1,0:T(8,128)S(1)} %copy-done.9), channel_id=1, source_target_pairs={{1,0},{2,1},{3,2},{4,3},{5,4},{6,5},{7,6},{8,7},{9,8},{10,9},{11,1... | collective-permute-start | bytes 983048 | tf_op jit(solution)/shard_map/ppermute | solution.py:454
  43.7 0.0 copy-done.7
  43.7 11.1 %window_first.1 = (f32[16,8,256]{2,1,0:T(8,128)S(1)}, f32[16,8,256]{2,1,0:T(8,128)S(1)}, f32[16,8,256]{2,1,0:T(8,128)S(1)}, f32[16,8,256]{2,1,0:T(8,128)S(1)}) custom-call(f32[32,8,256]{2,1,0:T(8,128)S(1)} %bitcast.13, f32[8,8,256]{2,1,0:T(8,128)S(1)} %copy-done.3, f32[8,8,256]{2,1,0:T(8,128)S(1)} %copy-done.4, f32[8,8,256]{2,1,0:T(8,128)S(1)} %copy-done.5, ...), custom_call_target="tpu_custom_call" | custom-call | tf_op jit(solution)/shard_map/window_first/pallas_call | solution.py:410
  54.8 0.1 collective-permute-start.8
  54.9 0.5 collective-permute-start.9
  55.4 0.0 collective-permute-done.7.refs_15_
  55.4 0.0 collective-permute-done.6.refs_14_
  55.4 11.6 %window_second.1 = (f32[32,8,256]{2,1,0:T(8,128)}, f32[16,8,256]{2,1,0:T(8,128)S(1)}, f32[16,8,256]{2,1,0:T(8,128)S(1)}, f32[16,8,256]{2,1,0:T(8,128)S(1)}) custom-call(f32[32,8,256]{2,1,0:T(8,128)S(1)} %bitcast.14, f32[8,8,256]{2,1,0:T(8,128)S(1)} %copy-done.3, f32[8,8,256]{2,1,0:T(8,128)S(1)} %copy-done.4, f32[8,8,256]{2,1,0:T(8,128)S(1)} %copy-done.5, ...), custom_call_target="tpu_custom_call" | custom-call | tf_op jit(solution)/shard_map/window_second/pallas_call | solution.py:410
  67.0 3.6 %collective-permute-start.10 = (f32[16,8,256]{2,1,0:T(8,128)S(1)}, f32[16,8,256]{2,1,0:T(8,128)S(1)}, u32[]{:S(2)}, u32[]{:S(2)}) collective-permute-start(f32[16,8,256]{2,1,0:T(8,128)S(1)} %get-tuple-element.40), channel_id=1, source_target_pairs={{1,0},{2,1},{3,2},{4,3},{5,4},{6,5},{7,6},{8,7},{9,8},{10,9},{11,1... | collective-permute-start | bytes 393224 | tf_op jit(solution)/shard_map/ppermute | solution.py:467
  70.6 0.0 collective-permute-start.11
  70.6 0.0 collective-permute-done.8.refs_1_
  70.6 0.0 collective-permute-done.9.refs_2_
  70.6 2.5 %collective-permute-done.10.refs_4_ = f32[16,8,256]{2,1,0:T(8,128)S(1)} collective-permute-done((f32[16,8,256]{2,1,0:T(8,128)S(1)}, f32[16,8,256]{2,1,0:T(8,128)S(1)}, u32[]{:S(2)}, u32[]{:S(2)}) %collective-permute-start.10) | collective-permute-done | bytes 131104 | tf_op jit(solution)/shard_map/ppermute | solution.py:467
  73.1 4.0 %collective-permute-done.11.refs_5_ = f32[16,8,256]{2,1,0:T(8,128)S(1)} collective-permute-done((f32[16,8,256]{2,1,0:T(8,128)S(1)}, f32[16,8,256]{2,1,0:T(8,128)S(1)}, u32[]{:S(2)}, u32[]{:S(2)}) %collective-permute-start.11) | collective-permute-done | bytes 131104 | tf_op jit(solution)/shard_map/ppermute | solution.py:468
  77.1 0.9 %finish.1 = f32[32,8,256]{2,1,0:T(8,128)} custom-call(f32[16,8,256]{2,1,0:T(8,128)S(1)} %get-tuple-element.36.refs_0_, f32[16,8,256]{2,1,0:T(8,128)S(1)} %collective-permute-done.8.refs_1_, f32[16,8,256]{2,1,0:T(8,128)S(1)} %collective-permute-done.9.refs_2_, f32[16,8,256]{2,1,0:T(8,128)S(1)} %get-tuple-element.39.refs_3_, ...), custom_call_target="tpu_custom_call" | custom-call | tf_op jit(solution)/shard_map/finish/pallas_call | solution.py:410
  (1 shorter events, 0.0 us)
Async XLA Ops:
  0.6 28.8 %copy-start.5 = (f32[8,8,256]{2,1,0:T(8,128)S(1)}, f32[8,8,256]{2,1,0:T(8,128)}, u32[]{:S(2)}) copy-start(f32[8,8,256]{2,1,0:T(8,128)} %refs_3_.9) | copy-start | bytes 196612
  4.6 24.8 %copy-start = (s32[4,4,8,8,256]{4,3,2,1,0:T(8,128)S(1)}, s32[4,4,8,8,256]{4,3,2,1,0:T(8,128)}, u32[]{:S(2)}) copy-start(s32[4,4,8,8,256]{4,3,2,1,0:T(8,128)} %param.12) | copy-start | bytes 3145732
  4.6 24.8 %copy-start.1 = (f32[4,8,8,256]{3,2,1,0:T(8,128)S(1)}, f32[4,8,8,256]{3,2,1,0:T(8,128)}, u32[]{:S(2)}) copy-start(f32[4,8,8,256]{3,2,1,0:T(8,128)} %param.8) | copy-start | bytes 786436
  4.6 24.8 %copy-start.2 = (f32[4,4,8,256]{3,2,1,0:T(8,128)S(1)}, f32[4,4,8,256]{3,2,1,0:T(8,128)}, u32[]{:S(2)}) copy-start(f32[4,4,8,256]{3,2,1,0:T(8,128)} %param.14) | copy-start | bytes 393220
  4.6 24.8 %copy-start.3 = (f32[8,8,256]{2,1,0:T(8,128)S(1)}, f32[8,8,256]{2,1,0:T(8,128)}, u32[]{:S(2)}) copy-start(f32[8,8,256]{2,1,0:T(8,128)} %refs_1_.9) | copy-start | bytes 196612
  4.7 24.8 %copy-start.4 = (f32[8,8,256]{2,1,0:T(8,128)S(1)}, f32[8,8,256]{2,1,0:T(8,128)}, u32[]{:S(2)}) copy-start(f32[8,8,256]{2,1,0:T(8,128)} %refs_2_.9) | copy-start | bytes 196612
  4.7 24.8 %copy-start.6 = (f32[4,8,256]{2,1,0:T(8,128)S(1)}, f32[4,8,256]{2,1,0:T(8,128)}, u32[]{:S(2)}) copy-start(f32[4,8,256]{2,1,0:T(8,128)} %refs_6_.7) | copy-start | bytes 98308
  7.6 32.1 %collective-permute-start = (f32[72,8,256]{2,1,0:T(8,128)}, f32[72,8,256]{2,1,0:T(8,128)S(1)}, u32[]{:S(2)}, u32[]{:S(2)}) collective-permute-start(f32[72,8,256]{2,1,0:T(8,128)} %get-tuple-element.23), channel_id=1, source_target_pairs={{0,1},{1,2},{2,3},{3,4},{4,5},{5,6},{6,7},{7,8},{8,9},{9,10},{10,1... | collective-permute-start | bytes 1769480 | tf_op jit(solution)/shard_map/ppermute | solution.py:445
  7.7 32.0 %collective-permute-start.1 = (f32[64,8,256]{2,1,0:T(8,128)}, f32[64,8,256]{2,1,0:T(8,128)S(1)}, u32[]{:S(2)}, u32[]{:S(2)}) collective-permute-start(f32[64,8,256]{2,1,0:T(8,128)} %get-tuple-element.24), channel_id=1, source_target_pairs={{1,0},{2,1},{3,2},{4,3},{5,4},{6,5},{7,6},{8,7},{9,8},{10,9},{11,1... | collective-permute-start | bytes 1572872 | tf_op jit(solution)/shard_map/ppermute | solution.py:446
  14.0 25.7 %copy-start.8 = (f32[48,8,256]{2,1,0:T(8,128)S(1)}, f32[48,8,256]{2,1,0:T(8,128)}, u32[]{:S(2)}) copy-start(f32[48,8,256]{2,1,0:T(8,128)} %get-tuple-element.32) | copy-start | bytes 1179652
  14.0 25.8 %copy-start.9 = (f32[40,8,256]{2,1,0:T(8,128)S(1)}, f32[40,8,256]{2,1,0:T(8,128)}, u32[]{:S(2)}) copy-start(f32[40,8,256]{2,1,0:T(8,128)} %get-tuple-element.33) | copy-start | bytes 983044
  14.0 10.5 %collective-permute-start.2 = (f32[26,8,128]{2,1,0:T(8,128)}, f32[26,8,128]{2,1,0:T(8,128)S(1)}, u32[]{:S(2)}, u32[]{:S(2)}) collective-permute-start(f32[26,8,128]{2,1,0:T(8,128)} %get-tuple-element.25), channel_id=1, source_target_pairs={{32,0},{64,32},{96,64},{128,96},{160,128},{192,160},{224,192},{33,... | collective-permute-start | bytes 319496 | tf_op jit(solution)/shard_map/ppermute | solution.py:444
  19.0 10.4 %collective-permute-start.3 = (f32[26,8,128]{2,1,0:T(8,128)}, f32[26,8,128]{2,1,0:T(8,128)S(1)}, u32[]{:S(2)}, u32[]{:S(2)}) collective-permute-start(f32[26,8,128]{2,1,0:T(8,128)} %get-tuple-element.22.refs_5_), channel_id=1, source_target_pairs={{0,32},{32,64},{64,96},{96,128},{128,160},{160,192},{192,224},{1,3... | collective-permute-start | bytes 319496 | tf_op jit(solution)/shard_map/ppermute | solution.py:443
  29.5 3.9 %collective-permute-start.5 = (f32[46,8,128]{2,1,0:T(8,128)S(1)}, f32[46,8,128]{2,1,0:T(8,128)S(1)}, u32[]{:S(2)}, u32[]{:S(2)}) collective-permute-start(f32[46,8,128]{2,1,0:T(8,128)S(1)} %join.1), channel_id=1, source_target_pairs={{1,0},{2,1},{3,2},{4,3},{5,4},{6,5},{7,6},{8,7},{9,8},{10,9},{11,1... | collective-permute-start | bytes 565256 | tf_op jit(solution)/shard_map/ppermute | solution.py:449
  30.3 9.5 %collective-permute-start.4 = (f32[46,8,128]{2,1,0:T(8,128)S(1)}, f32[46,8,128]{2,1,0:T(8,128)S(1)}, u32[]{:S(2)}, u32[]{:S(2)}) collective-permute-start(f32[46,8,128]{2,1,0:T(8,128)S(1)} %join.1), channel_id=1, source_target_pairs={{0,1},{1,2},{2,3},{3,4},{4,5},{5,6},{6,7},{7,8},{8,9},{9,10},{10,1... | collective-permute-start | bytes 565256 | tf_op jit(solution)/shard_map/ppermute | solution.py:448
  39.7 4.0 %copy-start.7 = (f32[8]{0:T(128)S(1)}, f32[8]{0:T(128)}, u32[]{:S(2)}) copy-start(f32[8]{0:T(128)} %refs_7_.3) | copy-start | bytes 100
  39.8 15.6 %collective-permute-start.6 = (f32[48,8,256]{2,1,0:T(8,128)S(1)}, f32[48,8,256]{2,1,0:T(8,128)S(1)}, u32[]{:S(2)}, u32[]{:S(2)}) collective-permute-start(f32[48,8,256]{2,1,0:T(8,128)S(1)} %copy-done.8), channel_id=1, source_target_pairs={{0,1},{1,2},{2,3},{3,4},{4,5},{5,6},{6,7},{7,8},{8,9},{9,10},{10,1... | collective-permute-start | bytes 1179656 | tf_op jit(solution)/shard_map/ppermute | solution.py:453
  39.9 15.5 %collective-permute-start.7 = (f32[40,8,256]{2,1,0:T(8,128)S(1)}, f32[40,8,256]{2,1,0:T(8,128)S(1)}, u32[]{:S(2)}, u32[]{:S(2)}) collective-permute-start(f32[40,8,256]{2,1,0:T(8,128)S(1)} %copy-done.9), channel_id=1, source_target_pairs={{1,0},{2,1},{3,2},{4,3},{5,4},{6,5},{7,6},{8,7},{9,8},{10,9},{11,1... | collective-permute-start | bytes 983048 | tf_op jit(solution)/shard_map/ppermute | solution.py:454
  54.8 15.8 %collective-permute-start.8 = (f32[16,8,256]{2,1,0:T(8,128)S(1)}, f32[16,8,256]{2,1,0:T(8,128)S(1)}, u32[]{:S(2)}, u32[]{:S(2)}) collective-permute-start(f32[16,8,256]{2,1,0:T(8,128)S(1)} %get-tuple-element.37), channel_id=1, source_target_pairs={{1,0},{2,1},{3,2},{4,3},{5,4},{6,5},{7,6},{8,7},{9,8},{10,9},{11,1... | collective-permute-start | bytes 393224 | tf_op jit(solution)/shard_map/ppermute | solution.py:461
  54.9 15.7 %collective-permute-start.9 = (f32[16,8,256]{2,1,0:T(8,128)S(1)}, f32[16,8,256]{2,1,0:T(8,128)S(1)}, u32[]{:S(2)}, u32[]{:S(2)}) collective-permute-start(f32[16,8,256]{2,1,0:T(8,128)S(1)} %get-tuple-element.38), channel_id=1, source_target_pairs={{0,1},{1,2},{2,3},{3,4},{4,5},{5,6},{6,7},{7,8},{8,9},{9,10},{10,1... | collective-permute-start | bytes 393224 | tf_op jit(solution)/shard_map/ppermute | solution.py:462
  67.0 6.1 %collective-permute-start.10 = (f32[16,8,256]{2,1,0:T(8,128)S(1)}, f32[16,8,256]{2,1,0:T(8,128)S(1)}, u32[]{:S(2)}, u32[]{:S(2)}) collective-permute-start(f32[16,8,256]{2,1,0:T(8,128)S(1)} %get-tuple-element.40), channel_id=1, source_target_pairs={{1,0},{2,1},{3,2},{4,3},{5,4},{6,5},{7,6},{8,7},{9,8},{10,9},{11,1... | collective-permute-start | bytes 393224 | tf_op jit(solution)/shard_map/ppermute | solution.py:467
  70.6 6.5 %collective-permute-start.11 = (f32[16,8,256]{2,1,0:T(8,128)S(1)}, f32[16,8,256]{2,1,0:T(8,128)S(1)}, u32[]{:S(2)}, u32[]{:S(2)}) collective-permute-start(f32[16,8,256]{2,1,0:T(8,128)S(1)} %get-tuple-element.41), channel_id=1, source_target_pairs={{0,1},{1,2},{2,3},{3,4},{4,5},{5,6},{6,7},{7,8},{8,9},{9,10},{10,1... | collective-permute-start | bytes 393224 | tf_op jit(solution)/shard_map/ppermute | solution.py:468

commit v4 on v3

--- a/solution.py
+++ b/solution.py
@@ -33,10 +33,11 @@
         copy.wait()
 
 
-def pack_lon(*refs):
-    hbm, (right_a, right_b, left_a, left_b), own, sems = (refs[:5], refs[6:10], refs[10:15], refs[15])
+def pack(*refs):
+    hbm, (right_a, right_b, left_a, left_b, to_north, to_south), own, sems = (refs[:7], refs[7:13], refs[13:20], refs[20])
     fetch(hbm, own, sems)
-    ck, cl, ct, mx, fl = own
+    ck, cl, ct, mx, fl, obs, mw = own
+    lane = lane_ids()
     col = col_ids(ROWS)
     for half, (to_right, to_left) in enumerate(((right_a, left_a), (right_b, left_b))):
         to_right[0:HALF] = ck[half * HALF : (half + 1) * HALF]
@@ -59,13 +60,6 @@
     for k, field in enumerate((cl, ct, mx)):
         right_a[3 * HALF + 8 * k : 3 * HALF + 8 * k + 8] = field[...]
         left_a[40 + 8 * k : 48 + 8 * k] = field[...]
-
-
-def pack_lat(*refs):
-    hbm, (to_north, to_south), own, sems = (refs[:7], refs[7:9], refs[9:16], refs[16])
-    fetch(hbm, own, sems)
-    ck, cl, ct, mx, fl, obs, mw = own
-    lane = lane_ids()
 
     def strips(place, read, count):
         north = jnp.zeros((COLS, LANES), jnp.float32)
@@ -239,21 +233,20 @@
 
     def lon_sweep(substep, row, level, slots, pieces, back):
         code_slots = slots if len(slots) == 3 else (0, 1)
-        out = []
-        for chunk in range(len(pieces)):
-            at = slice(chunk * LANES, (chunk + 1) * LANES)
-            value = jnp.concatenate(pieces[chunk], axis=0)
-            code = ring(code_slots, lambda k: lon_code[substep, row, k, :, at])
-            c, c_minus, c_both, slope = [ring(slots, lambda k: f[level, k, :, at]) for f in (cx, cx_minus, cx_both, cx_slope)]
-            first, second = weights(code, 1.0, 2.0, c_minus, c_both, slope)
-            value = (sweep_back if back else sweep)(value, c, first, second, 0)
-            out.append([value[n * COLS : (n + 1) * COLS] for n in range(len(slots))])
-        return out
-
-    def lat_weights(substep, row, level, code_slot, slot):
-        return weights(
-            lat_code[substep, row, code_slot], 3.0, 6.0, cy_minus[level, slot], cy_both[level, slot], cy_slope[level, slot]
-        )
+        at = slice(0, len(pieces) * LANES)
+        value = jnp.concatenate([jnp.concatenate(piece, axis=0) for piece in pieces], axis=1)
+        code = ring(code_slots, lambda k: lon_code[substep, row, k, :, at])
+        c, c_minus, c_both, slope = [ring(slots, lambda k: f[level, k, :, at]) for f in (cx, cx_minus, cx_both, cx_slope)]
+        first, second = weights(code, 1.0, 2.0, c_minus, c_both, slope)
+        value = (sweep_back if back else sweep)(value, c, first, second, 0)
+        return [
+            [value[n * COLS : (n + 1) * COLS, chunk * LANES : (chunk + 1) * LANES] for n in range(len(slots))]
+            for chunk in range(len(pieces))
+        ]
+
+    def lat_weights(substep, row, level, slots):
+        code = ring(slots, lambda k: lat_code[substep, row, 1 if k == 3 else k])
+        return weights(code, 3.0, 6.0, *[ring(slots, lambda k: f[level, k]) for f in (cy_minus, cy_both, cy_slope)])
 
     def forward(substep, slots, out_slots):
         @pl.loop(0, tracers // together)
@@ -270,15 +263,15 @@
                     blocks = {k: jnp.concatenate([piece[m] for piece in pieces], axis=1) for m, k in enumerate(slots)}
                     if substep == 1:
                         blocks[3] = squeeze(blocks[1], blocks[2])
-                    for slot in out_slots:
-                        code_slot = 1 if slot == 3 else slot
-                        first, second = lat_weights(substep, row, level, code_slot, slot)
-                        value = sweep(blocks[slot], cy[level, slot], first, second, 1)
-                        value = value * inv[level, slot]
+                    value = jnp.concatenate([blocks[slot] for slot in out_slots], axis=0)
+                    first, second = lat_weights(substep, row, level, out_slots)
+                    value = sweep(value, ring(out_slots, lambda k: cy[level, k]), first, second, 1)
+                    for m, slot in enumerate(out_slots):
+                        part = value[m * COLS : (m + 1) * COLS] * inv[level, slot]
                         if level > 0:
-                            value = value + elim[level, slot] * above[n, slot]
-                        above[n, slot] = value
-                        temp[row, slot] = value
+                            part = part + elim[level, slot] * above[n, slot]
+                        above[n, slot] = part
+                        temp[row, slot] = part
             column = {}
             for level in range(LEVELS - 1, -1, -1):
                 for n, tracer in enumerate(members):
@@ -325,13 +318,15 @@
                     row = tracer * LEVELS + level
                     blocks = {}
                     for slot in slots:
-                        code_slot = 1 if slot == 3 else slot
                         value = temp[row, slot]
                         if level < LEVELS - 1:
                             value = value + ratio[level, slot] * below[n, slot]
                         below[n, slot] = value
-                        first, second = lat_weights(substep, row, level, code_slot, slot)
-                        blocks[slot] = sweep_back(value, cy[level, slot], first, second, 1)
+                    first, second = lat_weights(substep, row, level, slots)
+                    value = jnp.concatenate([below[n, slot] for slot in slots], axis=0)
+                    value = sweep_back(value, ring(slots, lambda k: cy[level, k]), first, second, 1)
+                    for m, slot in enumerate(slots):
+                        blocks[slot] = value[m * COLS : (m + 1) * COLS]
                     if substep == SUBSTEPS - 1:
                         blocks[3] = jnp.zeros_like(blocks[0])
                     if substep == 1:
@@ -433,12 +428,14 @@
     )
     hbm = spec(1, pltpu.HBM)
     held = [pltpu.VMEM(value.shape, value.dtype) for value in own]
-    to_north, to_south = call(
-        pack_lat, "pack_lat", [block(26, LANES)] * 2, hbm * 7, own, held + [pltpu.SemaphoreType.DMA((7,))], limit=PACK_LIMIT
-    )
-    right_a, right_b, left_a, left_b = call(
-        pack_lon, "pack_lon", [block(72), block(48), block(64), block(40)], hbm * 6, own[:5] + (to_north,),
-        held[:5] + [pltpu.SemaphoreType.DMA((5,))], limit=PACK_LIMIT,
+    right_a, right_b, left_a, left_b, to_north, to_south = call(
+        pack,
+        "pack",
+        [block(72), block(48), block(64), block(40), block(26, LANES), block(26, LANES)],
+        hbm * 7,
+        own,
+        held + [pltpu.SemaphoreType.DMA((7,))],
+        limit=PACK_LIMIT,
     )
     south = lax.ppermute(to_north, "lat", up)
     north = lax.ppermute(to_south, "lat", down)

time: 78.2 us -> 73.4 us (0.939)
  Pallas kernels: 30.5 us -> 25.7 us
    pallas_call x6 -> x5, Pallas kernels: 30.5 us -> 25.7 us  [call(): pl.pallas_call(kernel, out_shape=tuple(outs), in_specs=in_specs, out_spec...]
  transfers between devices with their start and end apart: 12 -> 12, of which waited for: 6 -> 6; matrix products, arithmetic and copies ran while one was open for 0% -> 0% of each run, Pallas kernels for 29% -> 28%
where the time goes in v4:
time: 73.4 us; the launch traced here: 73.2 us
  Pallas kernels  25.7 us (35%)
  waiting for transfers between devices  23.9 us (33%)
  starting transfers between devices  22.7 us (31%)
  between operations  0.83 us (1%)
    pallas_call x5, Pallas kernels, call(): pl.pallas_call(kernel, out_shape=tuple(outs), in_specs=in_specs, out_spec...  25.7 us
    ppermute x1, waiting for transfers between devices, shards(): corner_l = lax.ppermute(corner, 'lon', east)  6.38 us
    ppermute x1, starting transfers between devices, shards(): from_right_a = lax.ppermute(left_a, 'lon', west)  6.3 us
    ppermute x1, waiting for transfers between devices, shards(): south = lax.ppermute(to_north, 'lat', up)  4.86 us
    ppermute x1, starting transfers between devices, shards(): north = lax.ppermute(to_south, 'lat', down)  4.81 us
    ppermute x1, waiting for transfers between devices, shards(): from_left_2 = lax.ppermute(gr_b, 'lon', east)  3.98 us
    ppermute x1, starting transfers between devices, shards(): from_right_b = lax.ppermute(left_b, 'lon', west)  3.83 us
    ppermute x1, starting transfers between devices, shards(): from_right_2 = lax.ppermute(gl_b, 'lon', west)  3.62 us
  transfers between devices with their start and end apart: 12, of which 6 were waited for; matrix products, arithmetic and copies ran while one was open for 0% of the time, Pallas kernels for 28%

profile of v4, /device:TPU:24, one launch (start us, length us, event | category | flops | bytes accessed | tf_op | source)
XLA Modules:
  0.0 73.2 jit_solution(6464685161139588709)
XLA Ops:
  0.6 0.0 copy-start
  0.6 0.0 copy-start.1
  0.7 0.0 copy-start.2
  0.7 0.0 copy-start.3
  0.7 0.0 copy-start.4
  0.7 0.0 copy-start.5
  0.7 0.0 copy-start.6
  0.7 4.7 %pack.1 = (f32[72,8,256]{2,1,0:T(8,128)}, f32[48,8,256]{2,1,0:T(8,128)}, f32[64,8,256]{2,1,0:T(8,128)}, f32[40,8,256]{2,1,0:T(8,128)}, f32[26,8,128]{2,1,0:T(8,128)}, /*index=5*/f32[26,8,128]{2,1,0:T(8,128)}) custom-call(f32[32,8,256]{2,1,0:T(8,128)} %bitcast.9, f32[8,8,256]{2,1,0:T(8,128)} %refs_1_.7, f32[8,8,256]{2,1,0:T(8,128)} %refs_2_.7, ...), custom_call_target="tpu_custom_call" | custom-call | tf_op jit(solution)/shard_map/pack/pallas_call | solution.py:405
  5.4 0.1 collective-permute-start
  5.5 6.3 %collective-permute-start.1 = (f32[64,8,256]{2,1,0:T(8,128)}, f32[64,8,256]{2,1,0:T(8,128)S(1)}, u32[]{:S(2)}, u32[]{:S(2)}) collective-permute-start(f32[64,8,256]{2,1,0:T(8,128)} %get-tuple-element.23), channel_id=1, source_target_pairs={{1,0},{2,1},{3,2},{4,3},{5,4},{6,5},{7,6},{8,7},{9,8},{10,9},{11,1... | collective-permute-start | bytes 1572872 | tf_op jit(solution)/shard_map/ppermute | solution.py:443
  11.8 4.8 %collective-permute-start.2 = (f32[26,8,128]{2,1,0:T(8,128)}, f32[26,8,128]{2,1,0:T(8,128)S(1)}, u32[]{:S(2)}, u32[]{:S(2)}) collective-permute-start(f32[26,8,128]{2,1,0:T(8,128)} %get-tuple-element.24), channel_id=1, source_target_pairs={{32,0},{64,32},{96,64},{128,96},{160,128},{192,160},{224,192},{33,... | collective-permute-start | bytes 319496 | tf_op jit(solution)/shard_map/ppermute | solution.py:441
  16.6 0.0 copy-start.8
  16.6 0.0 copy-start.9
  16.6 2.7 %collective-permute-start.3 = (f32[26,8,128]{2,1,0:T(8,128)}, f32[26,8,128]{2,1,0:T(8,128)S(1)}, u32[]{:S(2)}, u32[]{:S(2)}) collective-permute-start(f32[26,8,128]{2,1,0:T(8,128)} %get-tuple-element.25), channel_id=1, source_target_pairs={{0,32},{32,64},{64,96},{96,128},{128,160},{160,192},{192,224},{1,3... | collective-permute-start | bytes 319496 | tf_op jit(solution)/shard_map/ppermute | solution.py:440
  19.3 3.0 %collective-permute-done.2.refs_7_.refs_10_ = f32[26,8,128]{2,1,0:T(8,128)S(1)} collective-permute-done((f32[26,8,128]{2,1,0:T(8,128)}, f32[26,8,128]{2,1,0:T(8,128)S(1)}, u32[]{:S(2)}, u32[]{:S(2)}) %collective-permute-start.2) | collective-permute-done | bytes 106528 | tf_op jit(solution)/shard_map/ppermute | solution.py:441
  22.3 4.9 %collective-permute-done.3.refs_8_.refs_11_ = f32[26,8,128]{2,1,0:T(8,128)S(1)} collective-permute-done((f32[26,8,128]{2,1,0:T(8,128)}, f32[26,8,128]{2,1,0:T(8,128)S(1)}, u32[]{:S(2)}, u32[]{:S(2)}) %collective-permute-start.3) | collective-permute-done | bytes 106528 | tf_op jit(solution)/shard_map/ppermute | solution.py:440
  27.2 0.0 copy-done
  27.2 0.0 copy-done.1
  27.2 0.0 copy-done.2
  27.2 0.0 copy-done.3
  27.2 0.0 copy-done.4
  27.2 0.0 copy-done.5
  27.2 0.0 copy-done.6
  27.2 0.8 %collective-permute-start.5 = (f32[46,8,128]{2,1,0:T(8,128)S(1)}, f32[46,8,128]{2,1,0:T(8,128)S(1)}, u32[]{:S(2)}, u32[]{:S(2)}) collective-permute-start(f32[46,8,128]{2,1,0:T(8,128)S(1)} %join.1), channel_id=1, source_target_pairs={{1,0},{2,1},{3,2},{4,3},{5,4},{6,5},{7,6},{8,7},{9,8},{10,9},{11,1... | collective-permute-start | bytes 565256 | tf_op jit(solution)/shard_map/ppermute | solution.py:446
  28.0 0.0 collective-permute-start.4
  28.0 3.1 %collective-permute-done.5.refs_13_ = f32[46,8,128]{2,1,0:T(8,128)S(1)} collective-permute-done((f32[46,8,128]{2,1,0:T(8,128)S(1)}, f32[46,8,128]{2,1,0:T(8,128)S(1)}, u32[]{:S(2)}, u32[]{:S(2)}) %collective-permute-start.5) | collective-permute-done | bytes 188448 | tf_op jit(solution)/shard_map/ppermute | solution.py:446
  31.1 6.4 %collective-permute-done.4.refs_12_ = f32[46,8,128]{2,1,0:T(8,128)S(1)} collective-permute-done((f32[46,8,128]{2,1,0:T(8,128)S(1)}, f32[46,8,128]{2,1,0:T(8,128)S(1)}, u32[]{:S(2)}, u32[]{:S(2)}) %collective-permute-start.4) | collective-permute-done | bytes 188448 | tf_op jit(solution)/shard_map/ppermute | solution.py:445
  37.5 0.0 collective-permute-done.1.refs_9_
  37.5 0.0 collective-permute-done.refs_8_
  37.5 0.0 copy-start.7
  37.5 0.0 copy-done.8
  37.5 0.1 collective-permute-start.6
  37.6 0.0 copy-done.9
  37.6 3.8 %collective-permute-start.7 = (f32[40,8,256]{2,1,0:T(8,128)S(1)}, f32[40,8,256]{2,1,0:T(8,128)S(1)}, u32[]{:S(2)}, u32[]{:S(2)}) collective-permute-start(f32[40,8,256]{2,1,0:T(8,128)S(1)} %copy-done.9), channel_id=1, source_target_pairs={{1,0},{2,1},{3,2},{4,3},{5,4},{6,5},{7,6},{8,7},{9,8},{10,9},{11,1... | collective-permute-start | bytes 983048 | tf_op jit(solution)/shard_map/ppermute | solution.py:451
  41.4 0.0 copy-done.7
  41.4 9.9 %window_first.1 = (f32[16,8,256]{2,1,0:T(8,128)S(1)}, f32[16,8,256]{2,1,0:T(8,128)S(1)}, f32[16,8,256]{2,1,0:T(8,128)S(1)}, f32[16,8,256]{2,1,0:T(8,128)S(1)}) custom-call(f32[32,8,256]{2,1,0:T(8,128)S(1)} %bitcast.11, f32[8,8,256]{2,1,0:T(8,128)S(1)} %copy-done.3, f32[8,8,256]{2,1,0:T(8,128)S(1)} %copy-done.4, f32[8,8,256]{2,1,0:T(8,128)S(1)} %copy-done.5, ...), custom_call_target="tpu_custom_call" | custom-call | tf_op jit(solution)/shard_map/window_first/pallas_call | solution.py:405
  51.3 0.1 collective-permute-start.8
  51.4 0.5 collective-permute-start.9
  51.9 0.0 collective-permute-done.7.refs_15_
  51.9 0.0 collective-permute-done.6.refs_14_
  51.9 10.3 %window_second.1 = (f32[32,8,256]{2,1,0:T(8,128)}, f32[16,8,256]{2,1,0:T(8,128)S(1)}, f32[16,8,256]{2,1,0:T(8,128)S(1)}, f32[16,8,256]{2,1,0:T(8,128)S(1)}) custom-call(f32[32,8,256]{2,1,0:T(8,128)S(1)} %bitcast.12, f32[8,8,256]{2,1,0:T(8,128)S(1)} %copy-done.3, f32[8,8,256]{2,1,0:T(8,128)S(1)} %copy-done.4, f32[8,8,256]{2,1,0:T(8,128)S(1)} %copy-done.5, ...), custom_call_target="tpu_custom_call" | custom-call | tf_op jit(solution)/shard_map/window_second/pallas_call | solution.py:405
  62.2 3.6 %collective-permute-start.10 = (f32[16,8,256]{2,1,0:T(8,128)S(1)}, f32[16,8,256]{2,1,0:T(8,128)S(1)}, u32[]{:S(2)}, u32[]{:S(2)}) collective-permute-start(f32[16,8,256]{2,1,0:T(8,128)S(1)} %get-tuple-element.40), channel_id=1, source_target_pairs={{1,0},{2,1},{3,2},{4,3},{5,4},{6,5},{7,6},{8,7},{9,8},{10,9},{11,1... | collective-permute-start | bytes 393224 | tf_op jit(solution)/shard_map/ppermute | solution.py:464
  65.8 0.0 collective-permute-start.11
  65.8 0.0 collective-permute-done.8.refs_1_
  65.8 0.0 collective-permute-done.9.refs_2_
  65.8 2.5 %collective-permute-done.10.refs_4_ = f32[16,8,256]{2,1,0:T(8,128)S(1)} collective-permute-done((f32[16,8,256]{2,1,0:T(8,128)S(1)}, f32[16,8,256]{2,1,0:T(8,128)S(1)}, u32[]{:S(2)}, u32[]{:S(2)}) %collective-permute-start.10) | collective-permute-done | bytes 131104 | tf_op jit(solution)/shard_map/ppermute | solution.py:464
  68.3 4.0 %collective-permute-done.11.refs_5_ = f32[16,8,256]{2,1,0:T(8,128)S(1)} collective-permute-done((f32[16,8,256]{2,1,0:T(8,128)S(1)}, f32[16,8,256]{2,1,0:T(8,128)S(1)}, u32[]{:S(2)}, u32[]{:S(2)}) %collective-permute-start.11) | collective-permute-done | bytes 131104 | tf_op jit(solution)/shard_map/ppermute | solution.py:465
  72.3 0.9 %finish.1 = f32[32,8,256]{2,1,0:T(8,128)} custom-call(f32[16,8,256]{2,1,0:T(8,128)S(1)} %get-tuple-element.36.refs_0_, f32[16,8,256]{2,1,0:T(8,128)S(1)} %collective-permute-done.8.refs_1_, f32[16,8,256]{2,1,0:T(8,128)S(1)} %collective-permute-done.9.refs_2_, f32[16,8,256]{2,1,0:T(8,128)S(1)} %get-tuple-element.39.refs_3_, ...), custom_call_target="tpu_custom_call" | custom-call | tf_op jit(solution)/shard_map/finish/pallas_call | solution.py:405
  (1 shorter events, 0.0 us)
Async XLA Ops:
  0.6 26.5 %copy-start = (s32[4,4,8,8,256]{4,3,2,1,0:T(8,128)S(1)}, s32[4,4,8,8,256]{4,3,2,1,0:T(8,128)}, u32[]{:S(2)}) copy-start(s32[4,4,8,8,256]{4,3,2,1,0:T(8,128)} %param.12) | copy-start | bytes 3145732
  0.6 26.5 %copy-start.1 = (f32[4,8,8,256]{3,2,1,0:T(8,128)S(1)}, f32[4,8,8,256]{3,2,1,0:T(8,128)}, u32[]{:S(2)}) copy-start(f32[4,8,8,256]{3,2,1,0:T(8,128)} %param.8) | copy-start | bytes 786436
  0.7 26.5 %copy-start.2 = (f32[4,4,8,256]{3,2,1,0:T(8,128)S(1)}, f32[4,4,8,256]{3,2,1,0:T(8,128)}, u32[]{:S(2)}) copy-start(f32[4,4,8,256]{3,2,1,0:T(8,128)} %param.14) | copy-start | bytes 393220
  0.7 26.5 %copy-start.3 = (f32[8,8,256]{2,1,0:T(8,128)S(1)}, f32[8,8,256]{2,1,0:T(8,128)}, u32[]{:S(2)}) copy-start(f32[8,8,256]{2,1,0:T(8,128)} %refs_1_.7) | copy-start | bytes 196612
  0.7 26.5 %copy-start.4 = (f32[8,8,256]{2,1,0:T(8,128)S(1)}, f32[8,8,256]{2,1,0:T(8,128)}, u32[]{:S(2)}) copy-start(f32[8,8,256]{2,1,0:T(8,128)} %refs_2_.7) | copy-start | bytes 196612
  0.7 26.5 %copy-start.5 = (f32[8,8,256]{2,1,0:T(8,128)S(1)}, f32[8,8,256]{2,1,0:T(8,128)}, u32[]{:S(2)}) copy-start(f32[8,8,256]{2,1,0:T(8,128)} %refs_3_.7) | copy-start | bytes 196612
  0.7 26.5 %copy-start.6 = (f32[4,8,256]{2,1,0:T(8,128)S(1)}, f32[4,8,256]{2,1,0:T(8,128)}, u32[]{:S(2)}) copy-start(f32[4,8,256]{2,1,0:T(8,128)} %refs_6_.7) | copy-start | bytes 98308
  5.4 32.1 %collective-permute-start = (f32[72,8,256]{2,1,0:T(8,128)}, f32[72,8,256]{2,1,0:T(8,128)S(1)}, u32[]{:S(2)}, u32[]{:S(2)}) collective-permute-start(f32[72,8,256]{2,1,0:T(8,128)} %get-tuple-element.22), channel_id=1, source_target_pairs={{0,1},{1,2},{2,3},{3,4},{4,5},{5,6},{6,7},{7,8},{8,9},{9,10},{10,1... | collective-permute-start | bytes 1769480 | tf_op jit(solution)/shard_map/ppermute | solution.py:442
  5.5 32.0 %collective-permute-start.1 = (f32[64,8,256]{2,1,0:T(8,128)}, f32[64,8,256]{2,1,0:T(8,128)S(1)}, u32[]{:S(2)}, u32[]{:S(2)}) collective-permute-start(f32[64,8,256]{2,1,0:T(8,128)} %get-tuple-element.23), channel_id=1, source_target_pairs={{1,0},{2,1},{3,2},{4,3},{5,4},{6,5},{7,6},{8,7},{9,8},{10,9},{11,1... | collective-permute-start | bytes 1572872 | tf_op jit(solution)/shard_map/ppermute | solution.py:443
  11.8 10.5 %collective-permute-start.2 = (f32[26,8,128]{2,1,0:T(8,128)}, f32[26,8,128]{2,1,0:T(8,128)S(1)}, u32[]{:S(2)}, u32[]{:S(2)}) collective-permute-start(f32[26,8,128]{2,1,0:T(8,128)} %get-tuple-element.24), channel_id=1, source_target_pairs={{32,0},{64,32},{96,64},{128,96},{160,128},{192,160},{224,192},{33,... | collective-permute-start | bytes 319496 | tf_op jit(solution)/shard_map/ppermute | solution.py:441
  16.6 20.9 %copy-start.8 = (f32[48,8,256]{2,1,0:T(8,128)S(1)}, f32[48,8,256]{2,1,0:T(8,128)}, u32[]{:S(2)}) copy-start(f32[48,8,256]{2,1,0:T(8,128)} %get-tuple-element.32) | copy-start | bytes 1179652
  16.6 21.0 %copy-start.9 = (f32[40,8,256]{2,1,0:T(8,128)S(1)}, f32[40,8,256]{2,1,0:T(8,128)}, u32[]{:S(2)}) copy-start(f32[40,8,256]{2,1,0:T(8,128)} %get-tuple-element.33) | copy-start | bytes 983044
  16.6 10.5 %collective-permute-start.3 = (f32[26,8,128]{2,1,0:T(8,128)}, f32[26,8,128]{2,1,0:T(8,128)S(1)}, u32[]{:S(2)}, u32[]{:S(2)}) collective-permute-start(f32[26,8,128]{2,1,0:T(8,128)} %get-tuple-element.25), channel_id=1, source_target_pairs={{0,32},{32,64},{64,96},{96,128},{128,160},{160,192},{192,224},{1,3... | collective-permute-start | bytes 319496 | tf_op jit(solution)/shard_map/ppermute | solution.py:440
  27.2 3.9 %collective-permute-start.5 = (f32[46,8,128]{2,1,0:T(8,128)S(1)}, f32[46,8,128]{2,1,0:T(8,128)S(1)}, u32[]{:S(2)}, u32[]{:S(2)}) collective-permute-start(f32[46,8,128]{2,1,0:T(8,128)S(1)} %join.1), channel_id=1, source_target_pairs={{1,0},{2,1},{3,2},{4,3},{5,4},{6,5},{7,6},{8,7},{9,8},{10,9},{11,1... | collective-permute-start | bytes 565256 | tf_op jit(solution)/shard_map/ppermute | solution.py:446
  28.0 9.5 %collective-permute-start.4 = (f32[46,8,128]{2,1,0:T(8,128)S(1)}, f32[46,8,128]{2,1,0:T(8,128)S(1)}, u32[]{:S(2)}, u32[]{:S(2)}) collective-permute-start(f32[46,8,128]{2,1,0:T(8,128)S(1)} %join.1), channel_id=1, source_target_pairs={{0,1},{1,2},{2,3},{3,4},{4,5},{5,6},{6,7},{7,8},{8,9},{9,10},{10,1... | collective-permute-start | bytes 565256 | tf_op jit(solution)/shard_map/ppermute | solution.py:445
  37.5 4.0 %copy-start.7 = (f32[8]{0:T(128)S(1)}, f32[8]{0:T(128)}, u32[]{:S(2)}) copy-start(f32[8]{0:T(128)} %refs_7_.3) | copy-start | bytes 100
  37.5 14.4 %collective-permute-start.6 = (f32[48,8,256]{2,1,0:T(8,128)S(1)}, f32[48,8,256]{2,1,0:T(8,128)S(1)}, u32[]{:S(2)}, u32[]{:S(2)}) collective-permute-start(f32[48,8,256]{2,1,0:T(8,128)S(1)} %copy-done.8), channel_id=1, source_target_pairs={{0,1},{1,2},{2,3},{3,4},{4,5},{5,6},{6,7},{7,8},{8,9},{9,10},{10,1... | collective-permute-start | bytes 1179656 | tf_op jit(solution)/shard_map/ppermute | solution.py:450
  37.6 14.3 %collective-permute-start.7 = (f32[40,8,256]{2,1,0:T(8,128)S(1)}, f32[40,8,256]{2,1,0:T(8,128)S(1)}, u32[]{:S(2)}, u32[]{:S(2)}) collective-permute-start(f32[40,8,256]{2,1,0:T(8,128)S(1)} %copy-done.9), channel_id=1, source_target_pairs={{1,0},{2,1},{3,2},{4,3},{5,4},{6,5},{7,6},{8,7},{9,8},{10,9},{11,1... | collective-permute-start | bytes 983048 | tf_op jit(solution)/shard_map/ppermute | solution.py:451
  51.3 14.5 %collective-permute-start.8 = (f32[16,8,256]{2,1,0:T(8,128)S(1)}, f32[16,8,256]{2,1,0:T(8,128)S(1)}, u32[]{:S(2)}, u32[]{:S(2)}) collective-permute-start(f32[16,8,256]{2,1,0:T(8,128)S(1)} %get-tuple-element.37), channel_id=1, source_target_pairs={{1,0},{2,1},{3,2},{4,3},{5,4},{6,5},{7,6},{8,7},{9,8},{10,9},{11,1... | collective-permute-start | bytes 393224 | tf_op jit(solution)/shard_map/ppermute | solution.py:458
  51.4 14.4 %collective-permute-start.9 = (f32[16,8,256]{2,1,0:T(8,128)S(1)}, f32[16,8,256]{2,1,0:T(8,128)S(1)}, u32[]{:S(2)}, u32[]{:S(2)}) collective-permute-start(f32[16,8,256]{2,1,0:T(8,128)S(1)} %get-tuple-element.38), channel_id=1, source_target_pairs={{0,1},{1,2},{2,3},{3,4},{4,5},{5,6},{6,7},{7,8},{8,9},{9,10},{10,1... | collective-permute-start | bytes 393224 | tf_op jit(solution)/shard_map/ppermute | solution.py:459
  62.2 6.1 %collective-permute-start.10 = (f32[16,8,256]{2,1,0:T(8,128)S(1)}, f32[16,8,256]{2,1,0:T(8,128)S(1)}, u32[]{:S(2)}, u32[]{:S(2)}) collective-permute-start(f32[16,8,256]{2,1,0:T(8,128)S(1)} %get-tuple-element.40), channel_id=1, source_target_pairs={{1,0},{2,1},{3,2},{4,3},{5,4},{6,5},{7,6},{8,7},{9,8},{10,9},{11,1... | collective-permute-start | bytes 393224 | tf_op jit(solution)/shard_map/ppermute | solution.py:464
  65.8 6.5 %collective-permute-start.11 = (f32[16,8,256]{2,1,0:T(8,128)S(1)}, f32[16,8,256]{2,1,0:T(8,128)S(1)}, u32[]{:S(2)}, u32[]{:S(2)}) collective-permute-start(f32[16,8,256]{2,1,0:T(8,128)S(1)} %get-tuple-element.41), channel_id=1, source_target_pairs={{0,1},{1,2},{2,3},{3,4},{4,5},{5,6},{6,7},{7,8},{8,9},{9,10},{10,1... | collective-permute-start | bytes 393224 | tf_op jit(solution)/shard_map/ppermute | solution.py:465

commit v5 on v4

--- a/solution.py
+++ b/solution.py
@@ -444,9 +444,7 @@
     (corner,) = call(join, "join", [block(2 * CORNER, LANES)], spec(9), own + (north, south))
     corner_l = lax.ppermute(corner, "lon", east)
     corner_r = lax.ppermute(corner, "lon", west)
-    from_left_a, from_right_a, corner_l, corner_r, right_b, left_b = lax.optimization_barrier(
-        (from_left_a, from_right_a, corner_l, corner_r, right_b, left_b)
-    )
+    corner_l, corner_r, right_b, left_b = lax.optimization_barrier((corner_l, corner_r, right_b, left_b))
     from_left_b = lax.ppermute(right_b, "lon", east)
     from_right_b = lax.ppermute(left_b, "lon", west)
     smem = spec(1, pltpu.SMEM)

time: 73.4 us -> 74.9 us (1.020)
  the two profiles are of different devices: /device:TPU:24 before, /device:TPU:4 now
where the time goes in v5:
time: 74.9 us; the launch traced here: 74.7 us
  starting transfers between devices  33.1 us (44%)
  Pallas kernels  25.7 us (34%)
  waiting for transfers between devices  15.1 us (20%)
  between operations  0.83 us (1%)
    pallas_call x5, Pallas kernels, call(): pl.pallas_call(kernel, out_shape=tuple(outs), in_specs=in_specs, out_spec...  25.7 us
    ppermute x1, starting transfers between devices, shards(): from_right_a = lax.ppermute(left_a, 'lon', west)  10.4 us
    ppermute x1, waiting for transfers between devices, shards(): south = lax.ppermute(to_north, 'lat', up)  4.34 us
    ppermute x1, starting transfers between devices, shards(): north = lax.ppermute(to_south, 'lat', down)  4.15 us
    ppermute x1, starting transfers between devices, shards(): from_right_2 = lax.ppermute(gl_b, 'lon', west)  4.13 us
    ppermute x1, starting transfers between devices, shards(): south = lax.ppermute(to_north, 'lat', up)  4.09 us
    ppermute x1, waiting for transfers between devices, shards(): from_left_2 = lax.ppermute(gr_b, 'lon', east)  3.98 us
    ppermute x1, starting transfers between devices, shards(): from_right_b = lax.ppermute(left_b, 'lon', west)  3.84 us
  transfers between devices with their start and end apart: 12, of which 5 were waited for; matrix products, arithmetic and copies ran while one was open for 0% of the time, Pallas kernels for 27%

profile of v5, /device:TPU:4, one launch (start us, length us, event | category | flops | bytes accessed | tf_op | source)
XLA Modules:
  0.0 74.7 jit_solution(14748416303602402962)
XLA Ops:
  0.6 0.0 copy-start
  0.6 0.0 copy-start.1
  0.7 0.0 copy-start.2
  0.7 0.0 copy-start.3
  0.7 0.0 copy-start.4
  0.7 0.0 copy-start.5
  0.7 0.0 copy-start.6
  0.7 4.7 %pack.1 = (f32[72,8,256]{2,1,0:T(8,128)}, f32[48,8,256]{2,1,0:T(8,128)}, f32[64,8,256]{2,1,0:T(8,128)}, f32[40,8,256]{2,1,0:T(8,128)}, f32[26,8,128]{2,1,0:T(8,128)}, /*index=5*/f32[26,8,128]{2,1,0:T(8,128)}) custom-call(f32[32,8,256]{2,1,0:T(8,128)} %bitcast.9, f32[8,8,256]{2,1,0:T(8,128)} %refs_1_.7, f32[8,8,256]{2,1,0:T(8,128)} %refs_2_.7, ...), custom_call_target="tpu_custom_call" | custom-call | tf_op jit(solution)/shard_map/pack/pallas_call | solution.py:405
  5.4 4.2 %collective-permute-start.2 = (f32[26,8,128]{2,1,0:T(8,128)}, f32[26,8,128]{2,1,0:T(8,128)S(1)}, u32[]{:S(2)}, u32[]{:S(2)}) collective-permute-start(f32[26,8,128]{2,1,0:T(8,128)} %get-tuple-element.22), channel_id=1, source_target_pairs={{32,0},{64,32},{96,64},{128,96},{160,128},{192,160},{224,192},{33,... | collective-permute-start | bytes 319496 | tf_op jit(solution)/shard_map/ppermute | solution.py:441
  9.5 4.1 %collective-permute-start.3 = (f32[26,8,128]{2,1,0:T(8,128)}, f32[26,8,128]{2,1,0:T(8,128)S(1)}, u32[]{:S(2)}, u32[]{:S(2)}) collective-permute-start(f32[26,8,128]{2,1,0:T(8,128)} %get-tuple-element.23), channel_id=1, source_target_pairs={{0,32},{32,64},{64,96},{96,128},{128,160},{160,192},{192,224},{1,3... | collective-permute-start | bytes 319496 | tf_op jit(solution)/shard_map/ppermute | solution.py:440
  13.6 0.0 copy-start.8
  13.6 0.0 copy-start.9
  13.6 0.0 copy-start.10
  13.7 0.1 collective-permute-start
  13.8 0.8 %collective-permute-done.2.refs_7_.refs_10_ = f32[26,8,128]{2,1,0:T(8,128)S(1)} collective-permute-done((f32[26,8,128]{2,1,0:T(8,128)}, f32[26,8,128]{2,1,0:T(8,128)S(1)}, u32[]{:S(2)}, u32[]{:S(2)}) %collective-permute-start.2) | collective-permute-done | bytes 106528 | tf_op jit(solution)/shard_map/ppermute | solution.py:441
  14.6 4.3 %collective-permute-done.3.refs_8_.refs_11_ = f32[26,8,128]{2,1,0:T(8,128)S(1)} collective-permute-done((f32[26,8,128]{2,1,0:T(8,128)}, f32[26,8,128]{2,1,0:T(8,128)S(1)}, u32[]{:S(2)}, u32[]{:S(2)}) %collective-permute-start.3) | collective-permute-done | bytes 106528 | tf_op jit(solution)/shard_map/ppermute | solution.py:440
  18.9 0.0 copy-done
  18.9 0.0 copy-done.1
  18.9 0.0 copy-done.2
  18.9 0.0 copy-done.3
  19.0 0.0 copy-done.4
  19.0 0.0 copy-done.5
  19.0 0.0 copy-done.6
  19.0 2.6 %collective-permute-start.5 = (f32[46,8,128]{2,1,0:T(8,128)S(1)}, f32[46,8,128]{2,1,0:T(8,128)S(1)}, u32[]{:S(2)}, u32[]{:S(2)}) collective-permute-start(f32[46,8,128]{2,1,0:T(8,128)S(1)} %join.1), channel_id=1, source_target_pairs={{1,0},{2,1},{3,2},{4,3},{5,4},{6,5},{7,6},{8,7},{9,8},{10,9},{11,1... | collective-permute-start | bytes 565256 | tf_op jit(solution)/shard_map/ppermute | solution.py:446
  21.7 0.0 collective-permute-start.4
  21.7 0.0 copy-done.8
  21.7 10.4 %collective-permute-start.1 = (f32[64,8,256]{2,1,0:T(8,128)S(1)}, f32[64,8,256]{2,1,0:T(8,128)S(1)}, u32[]{:S(2)}, u32[]{:S(2)}) collective-permute-start(f32[64,8,256]{2,1,0:T(8,128)S(1)} %copy-done.8), channel_id=1, source_target_pairs={{1,0},{2,1},{3,2},{4,3},{5,4},{6,5},{7,6},{8,7},{9,8},{10,9},{11,1... | collective-permute-start | bytes 1572872 | tf_op jit(solution)/shard_map/ppermute | solution.py:443
  32.1 0.0 collective-permute-done.5.refs_13_
  32.1 3.4 %collective-permute-done.4.refs_12_ = f32[46,8,128]{2,1,0:T(8,128)S(1)} collective-permute-done((f32[46,8,128]{2,1,0:T(8,128)S(1)}, f32[46,8,128]{2,1,0:T(8,128)S(1)}, u32[]{:S(2)}, u32[]{:S(2)}) %collective-permute-start.4) | collective-permute-done | bytes 188448 | tf_op jit(solution)/shard_map/ppermute | solution.py:445
  35.5 0.0 copy-start.7
  35.5 0.0 copy-done.9
  35.5 0.0 collective-permute-start.6
  35.5 0.0 copy-done.10
  35.5 3.8 %collective-permute-start.7 = (f32[40,8,256]{2,1,0:T(8,128)S(1)}, f32[40,8,256]{2,1,0:T(8,128)S(1)}, u32[]{:S(2)}, u32[]{:S(2)}) collective-permute-start(f32[40,8,256]{2,1,0:T(8,128)S(1)} %copy-done.10), channel_id=1, source_target_pairs={{1,0},{2,1},{3,2},{4,3},{5,4},{6,5},{7,6},{8,7},{9,8},{10,9},{11,1... | collective-permute-start | bytes 983048 | tf_op jit(solution)/shard_map/ppermute | solution.py:449
  39.3 0.0 collective-permute-done.1.refs_9_
  39.3 0.0 collective-permute-done.refs_8_
  39.3 0.0 copy-done.7
  39.3 9.9 %window_first.1 = (f32[16,8,256]{2,1,0:T(8,128)S(1)}, f32[16,8,256]{2,1,0:T(8,128)S(1)}, f32[16,8,256]{2,1,0:T(8,128)S(1)}, f32[16,8,256]{2,1,0:T(8,128)S(1)}) custom-call(f32[32,8,256]{2,1,0:T(8,128)S(1)} %bitcast.11, f32[8,8,256]{2,1,0:T(8,128)S(1)} %copy-done.3, f32[8,8,256]{2,1,0:T(8,128)S(1)} %copy-done.4, f32[8,8,256]{2,1,0:T(8,128)S(1)} %copy-done.5, ...), custom_call_target="tpu_custom_call" | custom-call | tf_op jit(solution)/shard_map/window_first/pallas_call | solution.py:405
  49.2 3.7 %collective-permute-start.8 = (f32[16,8,256]{2,1,0:T(8,128)S(1)}, f32[16,8,256]{2,1,0:T(8,128)S(1)}, u32[]{:S(2)}, u32[]{:S(2)}) collective-permute-start(f32[16,8,256]{2,1,0:T(8,128)S(1)} %get-tuple-element.33), channel_id=1, source_target_pairs={{1,0},{2,1},{3,2},{4,3},{5,4},{6,5},{7,6},{8,7},{9,8},{10,9},{11,1... | collective-permute-start | bytes 393224 | tf_op jit(solution)/shard_map/ppermute | solution.py:456
  52.9 0.0 collective-permute-start.9
  52.9 0.0 collective-permute-done.7.refs_15_
  52.9 0.0 collective-permute-done.6.refs_14_
  52.9 10.3 %window_second.1 = (f32[32,8,256]{2,1,0:T(8,128)}, f32[16,8,256]{2,1,0:T(8,128)S(1)}, f32[16,8,256]{2,1,0:T(8,128)S(1)}, f32[16,8,256]{2,1,0:T(8,128)S(1)}) custom-call(f32[32,8,256]{2,1,0:T(8,128)S(1)} %bitcast.12, f32[8,8,256]{2,1,0:T(8,128)S(1)} %copy-done.3, f32[8,8,256]{2,1,0:T(8,128)S(1)} %copy-done.4, f32[8,8,256]{2,1,0:T(8,128)S(1)} %copy-done.5, ...), custom_call_target="tpu_custom_call" | custom-call | tf_op jit(solution)/shard_map/window_second/pallas_call | solution.py:405
  63.2 4.1 %collective-permute-start.10 = (f32[16,8,256]{2,1,0:T(8,128)S(1)}, f32[16,8,256]{2,1,0:T(8,128)S(1)}, u32[]{:S(2)}, u32[]{:S(2)}) collective-permute-start(f32[16,8,256]{2,1,0:T(8,128)S(1)} %get-tuple-element.36), channel_id=1, source_target_pairs={{1,0},{2,1},{3,2},{4,3},{5,4},{6,5},{7,6},{8,7},{9,8},{10,9},{11,1... | collective-permute-start | bytes 393224 | tf_op jit(solution)/shard_map/ppermute | solution.py:462
  67.3 0.0 collective-permute-start.11
  67.3 0.0 collective-permute-done.8.refs_1_
  67.3 0.0 collective-permute-done.9.refs_2_
  67.3 2.5 %collective-permute-done.10.refs_4_ = f32[16,8,256]{2,1,0:T(8,128)S(1)} collective-permute-done((f32[16,8,256]{2,1,0:T(8,128)S(1)}, f32[16,8,256]{2,1,0:T(8,128)S(1)}, u32[]{:S(2)}, u32[]{:S(2)}) %collective-permute-start.10) | collective-permute-done | bytes 131104 | tf_op jit(solution)/shard_map/ppermute | solution.py:462
  69.8 4.0 %collective-permute-done.11.refs_5_ = f32[16,8,256]{2,1,0:T(8,128)S(1)} collective-permute-done((f32[16,8,256]{2,1,0:T(8,128)S(1)}, f32[16,8,256]{2,1,0:T(8,128)S(1)}, u32[]{:S(2)}, u32[]{:S(2)}) %collective-permute-start.11) | collective-permute-done | bytes 131104 | tf_op jit(solution)/shard_map/ppermute | solution.py:463
  73.8 0.9 %finish.1 = f32[32,8,256]{2,1,0:T(8,128)} custom-call(f32[16,8,256]{2,1,0:T(8,128)S(1)} %get-tuple-element.32.refs_0_, f32[16,8,256]{2,1,0:T(8,128)S(1)} %collective-permute-done.8.refs_1_, f32[16,8,256]{2,1,0:T(8,128)S(1)} %collective-permute-done.9.refs_2_, f32[16,8,256]{2,1,0:T(8,128)S(1)} %get-tuple-element.35.refs_3_, ...), custom_call_target="tpu_custom_call" | custom-call | tf_op jit(solution)/shard_map/finish/pallas_call | solution.py:405
  (1 shorter events, 0.0 us)
Async XLA Ops:
  0.6 18.3 %copy-start = (s32[4,4,8,8,256]{4,3,2,1,0:T(8,128)S(1)}, s32[4,4,8,8,256]{4,3,2,1,0:T(8,128)}, u32[]{:S(2)}) copy-start(s32[4,4,8,8,256]{4,3,2,1,0:T(8,128)} %param.12) | copy-start | bytes 3145732
  0.6 18.3 %copy-start.1 = (f32[4,8,8,256]{3,2,1,0:T(8,128)S(1)}, f32[4,8,8,256]{3,2,1,0:T(8,128)}, u32[]{:S(2)}) copy-start(f32[4,8,8,256]{3,2,1,0:T(8,128)} %param.8) | copy-start | bytes 786436
  0.7 18.3 %copy-start.2 = (f32[4,4,8,256]{3,2,1,0:T(8,128)S(1)}, f32[4,4,8,256]{3,2,1,0:T(8,128)}, u32[]{:S(2)}) copy-start(f32[4,4,8,256]{3,2,1,0:T(8,128)} %param.14) | copy-start | bytes 393220
  0.7 18.3 %copy-start.3 = (f32[8,8,256]{2,1,0:T(8,128)S(1)}, f32[8,8,256]{2,1,0:T(8,128)}, u32[]{:S(2)}) copy-start(f32[8,8,256]{2,1,0:T(8,128)} %refs_1_.7) | copy-start | bytes 196612
  0.7 18.3 %copy-start.4 = (f32[8,8,256]{2,1,0:T(8,128)S(1)}, f32[8,8,256]{2,1,0:T(8,128)}, u32[]{:S(2)}) copy-start(f32[8,8,256]{2,1,0:T(8,128)} %refs_2_.7) | copy-start | bytes 196612
  0.7 18.3 %copy-start.5 = (f32[8,8,256]{2,1,0:T(8,128)S(1)}, f32[8,8,256]{2,1,0:T(8,128)}, u32[]{:S(2)}) copy-start(f32[8,8,256]{2,1,0:T(8,128)} %refs_3_.7) | copy-start | bytes 196612
  0.7 18.3 %copy-start.6 = (f32[4,8,256]{2,1,0:T(8,128)S(1)}, f32[4,8,256]{2,1,0:T(8,128)}, u32[]{:S(2)}) copy-start(f32[4,8,256]{2,1,0:T(8,128)} %refs_6_.7) | copy-start | bytes 98308
  5.4 9.2 %collective-permute-start.2 = (f32[26,8,128]{2,1,0:T(8,128)}, f32[26,8,128]{2,1,0:T(8,128)S(1)}, u32[]{:S(2)}, u32[]{:S(2)}) collective-permute-start(f32[26,8,128]{2,1,0:T(8,128)} %get-tuple-element.22), channel_id=1, source_target_pairs={{32,0},{64,32},{96,64},{128,96},{160,128},{192,160},{224,192},{33,... | collective-permute-start | bytes 319496 | tf_op jit(solution)/shard_map/ppermute | solution.py:441
  9.5 9.4 %collective-permute-start.3 = (f32[26,8,128]{2,1,0:T(8,128)}, f32[26,8,128]{2,1,0:T(8,128)S(1)}, u32[]{:S(2)}, u32[]{:S(2)}) collective-permute-start(f32[26,8,128]{2,1,0:T(8,128)} %get-tuple-element.23), channel_id=1, source_target_pairs={{0,32},{32,64},{64,96},{96,128},{128,160},{160,192},{192,224},{1,3... | collective-permute-start | bytes 319496 | tf_op jit(solution)/shard_map/ppermute | solution.py:440
  13.6 8.0 %copy-start.8 = (f32[64,8,256]{2,1,0:T(8,128)S(1)}, f32[64,8,256]{2,1,0:T(8,128)}, u32[]{:S(2)}) copy-start(f32[64,8,256]{2,1,0:T(8,128)} %get-tuple-element.21) | copy-start | bytes 1572868
  13.6 21.8 %copy-start.9 = (f32[48,8,256]{2,1,0:T(8,128)S(1)}, f32[48,8,256]{2,1,0:T(8,128)}, u32[]{:S(2)}) copy-start(f32[48,8,256]{2,1,0:T(8,128)} %get-tuple-element.28) | copy-start | bytes 1179652
  13.6 21.8 %copy-start.10 = (f32[40,8,256]{2,1,0:T(8,128)S(1)}, f32[40,8,256]{2,1,0:T(8,128)}, u32[]{:S(2)}) copy-start(f32[40,8,256]{2,1,0:T(8,128)} %get-tuple-element.29) | copy-start | bytes 983044
  13.7 25.7 %collective-permute-start = (f32[72,8,256]{2,1,0:T(8,128)}, f32[72,8,256]{2,1,0:T(8,128)S(1)}, u32[]{:S(2)}, u32[]{:S(2)}) collective-permute-start(f32[72,8,256]{2,1,0:T(8,128)} %get-tuple-element.20), channel_id=1, source_target_pairs={{0,1},{1,2},{2,3},{3,4},{4,5},{5,6},{6,7},{7,8},{8,9},{9,10},{10,1... | collective-permute-start | bytes 1769480 | tf_op jit(solution)/shard_map/ppermute | solution.py:442
  19.0 13.1 %collective-permute-start.5 = (f32[46,8,128]{2,1,0:T(8,128)S(1)}, f32[46,8,128]{2,1,0:T(8,128)S(1)}, u32[]{:S(2)}, u32[]{:S(2)}) collective-permute-start(f32[46,8,128]{2,1,0:T(8,128)S(1)} %join.1), channel_id=1, source_target_pairs={{1,0},{2,1},{3,2},{4,3},{5,4},{6,5},{7,6},{8,7},{9,8},{10,9},{11,1... | collective-permute-start | bytes 565256 | tf_op jit(solution)/shard_map/ppermute | solution.py:446
  21.7 13.8 %collective-permute-start.4 = (f32[46,8,128]{2,1,0:T(8,128)S(1)}, f32[46,8,128]{2,1,0:T(8,128)S(1)}, u32[]{:S(2)}, u32[]{:S(2)}) collective-permute-start(f32[46,8,128]{2,1,0:T(8,128)S(1)} %join.1), channel_id=1, source_target_pairs={{0,1},{1,2},{2,3},{3,4},{4,5},{5,6},{6,7},{7,8},{8,9},{9,10},{10,1... | collective-permute-start | bytes 565256 | tf_op jit(solution)/shard_map/ppermute | solution.py:445
  21.7 17.7 %collective-permute-start.1 = (f32[64,8,256]{2,1,0:T(8,128)S(1)}, f32[64,8,256]{2,1,0:T(8,128)S(1)}, u32[]{:S(2)}, u32[]{:S(2)}) collective-permute-start(f32[64,8,256]{2,1,0:T(8,128)S(1)} %copy-done.8), channel_id=1, source_target_pairs={{1,0},{2,1},{3,2},{4,3},{5,4},{6,5},{7,6},{8,7},{9,8},{10,9},{11,1... | collective-permute-start | bytes 1572872 | tf_op jit(solution)/shard_map/ppermute | solution.py:443
  35.5 3.9 %copy-start.7 = (f32[8]{0:T(128)S(1)}, f32[8]{0:T(128)}, u32[]{:S(2)}) copy-start(f32[8]{0:T(128)} %refs_7_.3) | copy-start | bytes 100
  35.5 17.4 %collective-permute-start.6 = (f32[48,8,256]{2,1,0:T(8,128)S(1)}, f32[48,8,256]{2,1,0:T(8,128)S(1)}, u32[]{:S(2)}, u32[]{:S(2)}) collective-permute-start(f32[48,8,256]{2,1,0:T(8,128)S(1)} %copy-done.9), channel_id=1, source_target_pairs={{0,1},{1,2},{2,3},{3,4},{4,5},{5,6},{6,7},{7,8},{8,9},{9,10},{10,1... | collective-permute-start | bytes 1179656 | tf_op jit(solution)/shard_map/ppermute | solution.py:448
  35.5 17.4 %collective-permute-start.7 = (f32[40,8,256]{2,1,0:T(8,128)S(1)}, f32[40,8,256]{2,1,0:T(8,128)S(1)}, u32[]{:S(2)}, u32[]{:S(2)}) collective-permute-start(f32[40,8,256]{2,1,0:T(8,128)S(1)} %copy-done.10), channel_id=1, source_target_pairs={{1,0},{2,1},{3,2},{4,3},{5,4},{6,5},{7,6},{8,7},{9,8},{10,9},{11,1... | collective-permute-start | bytes 983048 | tf_op jit(solution)/shard_map/ppermute | solution.py:449
  49.2 18.1 %collective-permute-start.8 = (f32[16,8,256]{2,1,0:T(8,128)S(1)}, f32[16,8,256]{2,1,0:T(8,128)S(1)}, u32[]{:S(2)}, u32[]{:S(2)}) collective-permute-start(f32[16,8,256]{2,1,0:T(8,128)S(1)} %get-tuple-element.33), channel_id=1, source_target_pairs={{1,0},{2,1},{3,2},{4,3},{5,4},{6,5},{7,6},{8,7},{9,8},{10,9},{11,1... | collective-permute-start | bytes 393224 | tf_op jit(solution)/shard_map/ppermute | solution.py:456
  52.9 14.4 %collective-permute-start.9 = (f32[16,8,256]{2,1,0:T(8,128)S(1)}, f32[16,8,256]{2,1,0:T(8,128)S(1)}, u32[]{:S(2)}, u32[]{:S(2)}) collective-permute-start(f32[16,8,256]{2,1,0:T(8,128)S(1)} %get-tuple-element.34), channel_id=1, source_target_pairs={{0,1},{1,2},{2,3},{3,4},{4,5},{5,6},{6,7},{7,8},{8,9},{9,10},{10,1... | collective-permute-start | bytes 393224 | tf_op jit(solution)/shard_map/ppermute | solution.py:457
  63.2 6.7 %collective-permute-start.10 = (f32[16,8,256]{2,1,0:T(8,128)S(1)}, f32[16,8,256]{2,1,0:T(8,128)S(1)}, u32[]{:S(2)}, u32[]{:S(2)}) collective-permute-start(f32[16,8,256]{2,1,0:T(8,128)S(1)} %get-tuple-element.36), channel_id=1, source_target_pairs={{1,0},{2,1},{3,2},{4,3},{5,4},{6,5},{7,6},{8,7},{9,8},{10,9},{11,1... | collective-permute-start | bytes 393224 | tf_op jit(solution)/shard_map/ppermute | solution.py:462
  67.3 6.5 %collective-permute-start.11 = (f32[16,8,256]{2,1,0:T(8,128)S(1)}, f32[16,8,256]{2,1,0:T(8,128)S(1)}, u32[]{:S(2)}, u32[]{:S(2)}) collective-permute-start(f32[16,8,256]{2,1,0:T(8,128)S(1)} %get-tuple-element.37), channel_id=1, source_target_pairs={{0,1},{1,2},{2,3},{3,4},{4,5},{5,6},{6,7},{7,8},{8,9},{9,10},{10,1... | collective-permute-start | bytes 393224 | tf_op jit(solution)/shard_map/ppermute | solution.py:463

commit v6 on v5

--- a/solution.py
+++ b/solution.py
@@ -444,7 +444,9 @@
     (corner,) = call(join, "join", [block(2 * CORNER, LANES)], spec(9), own + (north, south))
     corner_l = lax.ppermute(corner, "lon", east)
     corner_r = lax.ppermute(corner, "lon", west)
-    corner_l, corner_r, right_b, left_b = lax.optimization_barrier((corner_l, corner_r, right_b, left_b))
+    from_right_a, corner_l, corner_r, right_b, left_b = lax.optimization_barrier(
+        (from_right_a, corner_l, corner_r, right_b, left_b)
+    )
     from_left_b = lax.ppermute(right_b, "lon", east)
     from_right_b = lax.ppermute(left_b, "lon", west)
     smem = spec(1, pltpu.SMEM)

time: 74.9 us -> 72.2 us (0.964)
  the two profiles are of different devices: /device:TPU:4 before, /device:TPU:24 now
where the time goes in v6:
time: 72.2 us; the launch traced here: 72 us
  Pallas kernels  25.7 us (36%)
  waiting for transfers between devices  23 us (32%)
  starting transfers between devices  22.4 us (31%)
  between operations  0.83 us (1%)
    pallas_call x5, Pallas kernels, call(): pl.pallas_call(kernel, out_shape=tuple(outs), in_specs=in_specs, out_spec...  25.7 us
    ppermute x1, waiting for transfers between devices, shards(): south = lax.ppermute(to_north, 'lat', up)  7.74 us
    ppermute x1, starting transfers between devices, shards(): from_right_a = lax.ppermute(left_a, 'lon', west)  6.3 us
    ppermute x1, starting transfers between devices, shards(): north = lax.ppermute(to_south, 'lat', down)  4.81 us
    ppermute x1, waiting for transfers between devices, shards(): corner_l = lax.ppermute(corner, 'lon', east)  4.1 us
    ppermute x1, waiting for transfers between devices, shards(): from_left_2 = lax.ppermute(gr_b, 'lon', east)  3.98 us
    ppermute x1, starting transfers between devices, shards(): from_right_b = lax.ppermute(left_b, 'lon', west)  3.83 us
    ppermute x1, starting transfers between devices, shards(): from_right_2 = lax.ppermute(gl_b, 'lon', west)  3.62 us
  transfers between devices with their start and end apart: 12, of which 6 were waited for; matrix products, arithmetic and copies ran while one was open for 0% of the time, Pallas kernels for 28%

profile of v6, /device:TPU:24, one launch (start us, length us, event | category | flops | bytes accessed | tf_op | source)
XLA Modules:
  0.0 72.0 jit_solution(1625970443111536148)
XLA Ops:
  0.6 0.0 copy-start
  0.6 0.0 copy-start.1
  0.7 0.0 copy-start.2
  0.7 0.0 copy-start.3
  0.7 0.0 copy-start.4
  0.7 0.0 copy-start.5
  0.7 0.0 copy-start.6
  0.7 4.7 %pack.1 = (f32[72,8,256]{2,1,0:T(8,128)}, f32[48,8,256]{2,1,0:T(8,128)}, f32[64,8,256]{2,1,0:T(8,128)}, f32[40,8,256]{2,1,0:T(8,128)}, f32[26,8,128]{2,1,0:T(8,128)}, /*index=5*/f32[26,8,128]{2,1,0:T(8,128)}) custom-call(f32[32,8,256]{2,1,0:T(8,128)} %bitcast.9, f32[8,8,256]{2,1,0:T(8,128)} %refs_1_.7, f32[8,8,256]{2,1,0:T(8,128)} %refs_2_.7, ...), custom_call_target="tpu_custom_call" | custom-call | tf_op jit(solution)/shard_map/pack/pallas_call | solution.py:405
  5.4 6.3 %collective-permute-start.1 = (f32[64,8,256]{2,1,0:T(8,128)}, f32[64,8,256]{2,1,0:T(8,128)S(1)}, u32[]{:S(2)}, u32[]{:S(2)}) collective-permute-start(f32[64,8,256]{2,1,0:T(8,128)} %get-tuple-element.22), channel_id=1, source_target_pairs={{1,0},{2,1},{3,2},{4,3},{5,4},{6,5},{7,6},{8,7},{9,8},{10,9},{11,1... | collective-permute-start | bytes 1572872 | tf_op jit(solution)/shard_map/ppermute | solution.py:443
  11.7 4.8 %collective-permute-start.2 = (f32[26,8,128]{2,1,0:T(8,128)}, f32[26,8,128]{2,1,0:T(8,128)S(1)}, u32[]{:S(2)}, u32[]{:S(2)}) collective-permute-start(f32[26,8,128]{2,1,0:T(8,128)} %get-tuple-element.23), channel_id=1, source_target_pairs={{32,0},{64,32},{96,64},{128,96},{160,128},{192,160},{224,192},{33,... | collective-permute-start | bytes 319496 | tf_op jit(solution)/shard_map/ppermute | solution.py:441
  16.5 2.5 %collective-permute-start.3 = (f32[26,8,128]{2,1,0:T(8,128)}, f32[26,8,128]{2,1,0:T(8,128)S(1)}, u32[]{:S(2)}, u32[]{:S(2)}) collective-permute-start(f32[26,8,128]{2,1,0:T(8,128)} %get-tuple-element.24), channel_id=1, source_target_pairs={{0,32},{32,64},{64,96},{96,128},{128,160},{160,192},{192,224},{1,3... | collective-permute-start | bytes 319496 | tf_op jit(solution)/shard_map/ppermute | solution.py:440
  19.0 0.0 copy-start.8
  19.0 0.0 copy-start.9
  19.1 0.1 collective-permute-start
  19.1 2.0 %collective-permute-done.2.refs_7_.refs_10_ = f32[26,8,128]{2,1,0:T(8,128)S(1)} collective-permute-done((f32[26,8,128]{2,1,0:T(8,128)}, f32[26,8,128]{2,1,0:T(8,128)S(1)}, u32[]{:S(2)}, u32[]{:S(2)}) %collective-permute-start.2) | collective-permute-done | bytes 106528 | tf_op jit(solution)/shard_map/ppermute | solution.py:441
  21.2 7.7 %collective-permute-done.3.refs_8_.refs_11_ = f32[26,8,128]{2,1,0:T(8,128)S(1)} collective-permute-done((f32[26,8,128]{2,1,0:T(8,128)}, f32[26,8,128]{2,1,0:T(8,128)S(1)}, u32[]{:S(2)}, u32[]{:S(2)}) %collective-permute-start.3) | collective-permute-done | bytes 106528 | tf_op jit(solution)/shard_map/ppermute | solution.py:440
  28.9 0.0 copy-done
  28.9 0.0 copy-done.1
  28.9 0.0 copy-done.2
  28.9 0.0 copy-done.3
  29.0 0.0 copy-done.4
  29.0 0.0 copy-done.5
  29.0 0.0 copy-done.6
  29.0 0.1 collective-permute-start.5
  29.1 0.5 collective-permute-start.4
  29.6 2.6 %collective-permute-done.5.refs_13_ = f32[46,8,128]{2,1,0:T(8,128)S(1)} collective-permute-done((f32[46,8,128]{2,1,0:T(8,128)S(1)}, f32[46,8,128]{2,1,0:T(8,128)S(1)}, u32[]{:S(2)}, u32[]{:S(2)}) %collective-permute-start.5) | collective-permute-done | bytes 188448 | tf_op jit(solution)/shard_map/ppermute | solution.py:446
  32.2 4.1 %collective-permute-done.4.refs_12_ = f32[46,8,128]{2,1,0:T(8,128)S(1)} collective-permute-done((f32[46,8,128]{2,1,0:T(8,128)S(1)}, f32[46,8,128]{2,1,0:T(8,128)S(1)}, u32[]{:S(2)}, u32[]{:S(2)}) %collective-permute-start.4) | collective-permute-done | bytes 188448 | tf_op jit(solution)/shard_map/ppermute | solution.py:445
  36.3 0.0 collective-permute-done.1.refs_9_
  36.3 0.0 copy-start.7
  36.3 0.0 copy-done.8
  36.3 0.1 collective-permute-start.6
  36.4 0.0 copy-done.9
  36.4 3.8 %collective-permute-start.7 = (f32[40,8,256]{2,1,0:T(8,128)S(1)}, f32[40,8,256]{2,1,0:T(8,128)S(1)}, u32[]{:S(2)}, u32[]{:S(2)}) collective-permute-start(f32[40,8,256]{2,1,0:T(8,128)S(1)} %copy-done.9), channel_id=1, source_target_pairs={{1,0},{2,1},{3,2},{4,3},{5,4},{6,5},{7,6},{8,7},{9,8},{10,9},{11,1... | collective-permute-start | bytes 983048 | tf_op jit(solution)/shard_map/ppermute | solution.py:451
  40.2 0.0 collective-permute-done.refs_8_
  40.2 0.0 copy-done.7
  40.2 9.9 %window_first.1 = (f32[16,8,256]{2,1,0:T(8,128)S(1)}, f32[16,8,256]{2,1,0:T(8,128)S(1)}, f32[16,8,256]{2,1,0:T(8,128)S(1)}, f32[16,8,256]{2,1,0:T(8,128)S(1)}) custom-call(f32[32,8,256]{2,1,0:T(8,128)S(1)} %bitcast.11, f32[8,8,256]{2,1,0:T(8,128)S(1)} %copy-done.3, f32[8,8,256]{2,1,0:T(8,128)S(1)} %copy-done.4, f32[8,8,256]{2,1,0:T(8,128)S(1)} %copy-done.5, ...), custom_call_target="tpu_custom_call" | custom-call | tf_op jit(solution)/shard_map/window_first/pallas_call | solution.py:405
  50.1 0.1 collective-permute-start.8
  50.2 0.5 collective-permute-start.9
  50.7 0.0 collective-permute-done.7.refs_15_
  50.7 0.0 collective-permute-done.6.refs_14_
  50.7 10.3 %window_second.1 = (f32[32,8,256]{2,1,0:T(8,128)}, f32[16,8,256]{2,1,0:T(8,128)S(1)}, f32[16,8,256]{2,1,0:T(8,128)S(1)}, f32[16,8,256]{2,1,0:T(8,128)S(1)}) custom-call(f32[32,8,256]{2,1,0:T(8,128)S(1)} %bitcast.12, f32[8,8,256]{2,1,0:T(8,128)S(1)} %copy-done.3, f32[8,8,256]{2,1,0:T(8,128)S(1)} %copy-done.4, f32[8,8,256]{2,1,0:T(8,128)S(1)} %copy-done.5, ...), custom_call_target="tpu_custom_call" | custom-call | tf_op jit(solution)/shard_map/window_second/pallas_call | solution.py:405
  61.0 3.6 %collective-permute-start.10 = (f32[16,8,256]{2,1,0:T(8,128)S(1)}, f32[16,8,256]{2,1,0:T(8,128)S(1)}, u32[]{:S(2)}, u32[]{:S(2)}) collective-permute-start(f32[16,8,256]{2,1,0:T(8,128)S(1)} %get-tuple-element.38), channel_id=1, source_target_pairs={{1,0},{2,1},{3,2},{4,3},{5,4},{6,5},{7,6},{8,7},{9,8},{10,9},{11,1... | collective-permute-start | bytes 393224 | tf_op jit(solution)/shard_map/ppermute | solution.py:464
  64.6 0.0 collective-permute-start.11
  64.6 0.0 collective-permute-done.8.refs_1_
  64.6 0.0 collective-permute-done.9.refs_2_
  64.6 2.5 %collective-permute-done.10.refs_4_ = f32[16,8,256]{2,1,0:T(8,128)S(1)} collective-permute-done((f32[16,8,256]{2,1,0:T(8,128)S(1)}, f32[16,8,256]{2,1,0:T(8,128)S(1)}, u32[]{:S(2)}, u32[]{:S(2)}) %collective-permute-start.10) | collective-permute-done | bytes 131104 | tf_op jit(solution)/shard_map/ppermute | solution.py:464
  67.1 4.0 %collective-permute-done.11.refs_5_ = f32[16,8,256]{2,1,0:T(8,128)S(1)} collective-permute-done((f32[16,8,256]{2,1,0:T(8,128)S(1)}, f32[16,8,256]{2,1,0:T(8,128)S(1)}, u32[]{:S(2)}, u32[]{:S(2)}) %collective-permute-start.11) | collective-permute-done | bytes 131104 | tf_op jit(solution)/shard_map/ppermute | solution.py:465
  71.1 0.9 %finish.1 = f32[32,8,256]{2,1,0:T(8,128)} custom-call(f32[16,8,256]{2,1,0:T(8,128)S(1)} %get-tuple-element.34.refs_0_, f32[16,8,256]{2,1,0:T(8,128)S(1)} %collective-permute-done.8.refs_1_, f32[16,8,256]{2,1,0:T(8,128)S(1)} %collective-permute-done.9.refs_2_, f32[16,8,256]{2,1,0:T(8,128)S(1)} %get-tuple-element.37.refs_3_, ...), custom_call_target="tpu_custom_call" | custom-call | tf_op jit(solution)/shard_map/finish/pallas_call | solution.py:405
  (1 shorter events, 0.0 us)
Async XLA Ops:
  0.6 28.3 %copy-start = (s32[4,4,8,8,256]{4,3,2,1,0:T(8,128)S(1)}, s32[4,4,8,8,256]{4,3,2,1,0:T(8,128)}, u32[]{:S(2)}) copy-start(s32[4,4,8,8,256]{4,3,2,1,0:T(8,128)} %param.12) | copy-start | bytes 3145732
  0.6 28.3 %copy-start.1 = (f32[4,8,8,256]{3,2,1,0:T(8,128)S(1)}, f32[4,8,8,256]{3,2,1,0:T(8,128)}, u32[]{:S(2)}) copy-start(f32[4,8,8,256]{3,2,1,0:T(8,128)} %param.8) | copy-start | bytes 786436
  0.7 28.3 %copy-start.2 = (f32[4,4,8,256]{3,2,1,0:T(8,128)S(1)}, f32[4,4,8,256]{3,2,1,0:T(8,128)}, u32[]{:S(2)}) copy-start(f32[4,4,8,256]{3,2,1,0:T(8,128)} %param.14) | copy-start | bytes 393220
  0.7 28.3 %copy-start.3 = (f32[8,8,256]{2,1,0:T(8,128)S(1)}, f32[8,8,256]{2,1,0:T(8,128)}, u32[]{:S(2)}) copy-start(f32[8,8,256]{2,1,0:T(8,128)} %refs_1_.7) | copy-start | bytes 196612
  0.7 28.3 %copy-start.4 = (f32[8,8,256]{2,1,0:T(8,128)S(1)}, f32[8,8,256]{2,1,0:T(8,128)}, u32[]{:S(2)}) copy-start(f32[8,8,256]{2,1,0:T(8,128)} %refs_2_.7) | copy-start | bytes 196612
  0.7 28.3 %copy-start.5 = (f32[8,8,256]{2,1,0:T(8,128)S(1)}, f32[8,8,256]{2,1,0:T(8,128)}, u32[]{:S(2)}) copy-start(f32[8,8,256]{2,1,0:T(8,128)} %refs_3_.7) | copy-start | bytes 196612
  0.7 28.3 %copy-start.6 = (f32[4,8,256]{2,1,0:T(8,128)S(1)}, f32[4,8,256]{2,1,0:T(8,128)}, u32[]{:S(2)}) copy-start(f32[4,8,256]{2,1,0:T(8,128)} %refs_6_.7) | copy-start | bytes 98308
  5.4 30.9 %collective-permute-start.1 = (f32[64,8,256]{2,1,0:T(8,128)}, f32[64,8,256]{2,1,0:T(8,128)S(1)}, u32[]{:S(2)}, u32[]{:S(2)}) collective-permute-start(f32[64,8,256]{2,1,0:T(8,128)} %get-tuple-element.22), channel_id=1, source_target_pairs={{1,0},{2,1},{3,2},{4,3},{5,4},{6,5},{7,6},{8,7},{9,8},{10,9},{11,1... | collective-permute-start | bytes 1572872 | tf_op jit(solution)/shard_map/ppermute | solution.py:443
  11.7 9.5 %collective-permute-start.2 = (f32[26,8,128]{2,1,0:T(8,128)}, f32[26,8,128]{2,1,0:T(8,128)S(1)}, u32[]{:S(2)}, u32[]{:S(2)}) collective-permute-start(f32[26,8,128]{2,1,0:T(8,128)} %get-tuple-element.23), channel_id=1, source_target_pairs={{32,0},{64,32},{96,64},{128,96},{160,128},{192,160},{224,192},{33,... | collective-permute-start | bytes 319496 | tf_op jit(solution)/shard_map/ppermute | solution.py:441
  16.5 12.4 %collective-permute-start.3 = (f32[26,8,128]{2,1,0:T(8,128)}, f32[26,8,128]{2,1,0:T(8,128)S(1)}, u32[]{:S(2)}, u32[]{:S(2)}) collective-permute-start(f32[26,8,128]{2,1,0:T(8,128)} %get-tuple-element.24), channel_id=1, source_target_pairs={{0,32},{32,64},{64,96},{96,128},{128,160},{160,192},{192,224},{1,3... | collective-permute-start | bytes 319496 | tf_op jit(solution)/shard_map/ppermute | solution.py:440
  19.0 17.3 %copy-start.8 = (f32[48,8,256]{2,1,0:T(8,128)S(1)}, f32[48,8,256]{2,1,0:T(8,128)}, u32[]{:S(2)}) copy-start(f32[48,8,256]{2,1,0:T(8,128)} %get-tuple-element.30) | copy-start | bytes 1179652
  19.0 17.4 %copy-start.9 = (f32[40,8,256]{2,1,0:T(8,128)S(1)}, f32[40,8,256]{2,1,0:T(8,128)}, u32[]{:S(2)}) copy-start(f32[40,8,256]{2,1,0:T(8,128)} %get-tuple-element.31) | copy-start | bytes 983044
  19.1 21.2 %collective-permute-start = (f32[72,8,256]{2,1,0:T(8,128)}, f32[72,8,256]{2,1,0:T(8,128)S(1)}, u32[]{:S(2)}, u32[]{:S(2)}) collective-permute-start(f32[72,8,256]{2,1,0:T(8,128)} %get-tuple-element.21), channel_id=1, source_target_pairs={{0,1},{1,2},{2,3},{3,4},{4,5},{5,6},{6,7},{7,8},{8,9},{9,10},{10,1... | collective-permute-start | bytes 1769480 | tf_op jit(solution)/shard_map/ppermute | solution.py:442
  29.0 3.2 %collective-permute-start.5 = (f32[46,8,128]{2,1,0:T(8,128)S(1)}, f32[46,8,128]{2,1,0:T(8,128)S(1)}, u32[]{:S(2)}, u32[]{:S(2)}) collective-permute-start(f32[46,8,128]{2,1,0:T(8,128)S(1)} %join.1), channel_id=1, source_target_pairs={{1,0},{2,1},{3,2},{4,3},{5,4},{6,5},{7,6},{8,7},{9,8},{10,9},{11,1... | collective-permute-start | bytes 565256 | tf_op jit(solution)/shard_map/ppermute | solution.py:446
  29.1 7.2 %collective-permute-start.4 = (f32[46,8,128]{2,1,0:T(8,128)S(1)}, f32[46,8,128]{2,1,0:T(8,128)S(1)}, u32[]{:S(2)}, u32[]{:S(2)}) collective-permute-start(f32[46,8,128]{2,1,0:T(8,128)S(1)} %join.1), channel_id=1, source_target_pairs={{0,1},{1,2},{2,3},{3,4},{4,5},{5,6},{6,7},{7,8},{8,9},{9,10},{10,1... | collective-permute-start | bytes 565256 | tf_op jit(solution)/shard_map/ppermute | solution.py:445
  36.3 3.9 %copy-start.7 = (f32[8]{0:T(128)S(1)}, f32[8]{0:T(128)}, u32[]{:S(2)}) copy-start(f32[8]{0:T(128)} %refs_7_.3) | copy-start | bytes 100
  36.3 14.4 %collective-permute-start.6 = (f32[48,8,256]{2,1,0:T(8,128)S(1)}, f32[48,8,256]{2,1,0:T(8,128)S(1)}, u32[]{:S(2)}, u32[]{:S(2)}) collective-permute-start(f32[48,8,256]{2,1,0:T(8,128)S(1)} %copy-done.8), channel_id=1, source_target_pairs={{0,1},{1,2},{2,3},{3,4},{4,5},{5,6},{6,7},{7,8},{8,9},{9,10},{10,1... | collective-permute-start | bytes 1179656 | tf_op jit(solution)/shard_map/ppermute | solution.py:450
  36.4 14.3 %collective-permute-start.7 = (f32[40,8,256]{2,1,0:T(8,128)S(1)}, f32[40,8,256]{2,1,0:T(8,128)S(1)}, u32[]{:S(2)}, u32[]{:S(2)}) collective-permute-start(f32[40,8,256]{2,1,0:T(8,128)S(1)} %copy-done.9), channel_id=1, source_target_pairs={{1,0},{2,1},{3,2},{4,3},{5,4},{6,5},{7,6},{8,7},{9,8},{10,9},{11,1... | collective-permute-start | bytes 983048 | tf_op jit(solution)/shard_map/ppermute | solution.py:451
  50.1 14.5 %collective-permute-start.8 = (f32[16,8,256]{2,1,0:T(8,128)S(1)}, f32[16,8,256]{2,1,0:T(8,128)S(1)}, u32[]{:S(2)}, u32[]{:S(2)}) collective-permute-start(f32[16,8,256]{2,1,0:T(8,128)S(1)} %get-tuple-element.35), channel_id=1, source_target_pairs={{1,0},{2,1},{3,2},{4,3},{5,4},{6,5},{7,6},{8,7},{9,8},{10,9},{11,1... | collective-permute-start | bytes 393224 | tf_op jit(solution)/shard_map/ppermute | solution.py:458
  50.2 14.4 %collective-permute-start.9 = (f32[16,8,256]{2,1,0:T(8,128)S(1)}, f32[16,8,256]{2,1,0:T(8,128)S(1)}, u32[]{:S(2)}, u32[]{:S(2)}) collective-permute-start(f32[16,8,256]{2,1,0:T(8,128)S(1)} %get-tuple-element.36), channel_id=1, source_target_pairs={{0,1},{1,2},{2,3},{3,4},{4,5},{5,6},{6,7},{7,8},{8,9},{9,10},{10,1... | collective-permute-start | bytes 393224 | tf_op jit(solution)/shard_map/ppermute | solution.py:459
  61.0 6.1 %collective-permute-start.10 = (f32[16,8,256]{2,1,0:T(8,128)S(1)}, f32[16,8,256]{2,1,0:T(8,128)S(1)}, u32[]{:S(2)}, u32[]{:S(2)}) collective-permute-start(f32[16,8,256]{2,1,0:T(8,128)S(1)} %get-tuple-element.38), channel_id=1, source_target_pairs={{1,0},{2,1},{3,2},{4,3},{5,4},{6,5},{7,6},{8,7},{9,8},{10,9},{11,1... | collective-permute-start | bytes 393224 | tf_op jit(solution)/shard_map/ppermute | solution.py:464
  64.6 6.5 %collective-permute-start.11 = (f32[16,8,256]{2,1,0:T(8,128)S(1)}, f32[16,8,256]{2,1,0:T(8,128)S(1)}, u32[]{:S(2)}, u32[]{:S(2)}) collective-permute-start(f32[16,8,256]{2,1,0:T(8,128)S(1)} %get-tuple-element.39), channel_id=1, source_target_pairs={{0,1},{1,2},{2,3},{3,4},{4,5},{5,6},{6,7},{7,8},{8,9},{9,10},{10,1... | collective-permute-start | bytes 393224 | tf_op jit(solution)/shard_map/ppermute | solution.py:465

commit v7 on v6

--- a/solution.py
+++ b/solution.py
@@ -9,6 +9,7 @@
 
 TRACERS, LEVELS, SUBSTEPS = 4, 8, 4
 PAIR = 2
+BATCH = 2
 COLS, ROWS, EDGE, LANES = 8, 256, 16, 128
 STATE = TRACERS * LEVELS
 HALF = PAIR * LEVELS
@@ -253,6 +254,7 @@
         def _(batch):
             members = [batch * together + n for n in range(together)]
             above = {}
+            stacked = []
             for level in range(LEVELS):
                 for n, tracer in enumerate(members):
                     row = tracer * LEVELS + level
@@ -263,15 +265,24 @@
                     blocks = {k: jnp.concatenate([piece[m] for piece in pieces], axis=1) for m, k in enumerate(slots)}
                     if substep == 1:
                         blocks[3] = squeeze(blocks[1], blocks[2])
-                    value = jnp.concatenate([blocks[slot] for slot in out_slots], axis=0)
-                    first, second = lat_weights(substep, row, level, out_slots)
-                    value = sweep(value, ring(out_slots, lambda k: cy[level, k]), first, second, 1)
-                    for m, slot in enumerate(out_slots):
-                        part = value[m * COLS : (m + 1) * COLS] * inv[level, slot]
-                        if level > 0:
-                            part = part + elim[level, slot] * above[n, slot]
-                        above[n, slot] = part
-                        temp[row, slot] = part
+                    stacked.append((n, row, level, blocks))
+                    if len(stacked) < BATCH:
+                        continue
+                    value = jnp.concatenate([b[slot] for _, _, _, b in stacked for slot in out_slots], axis=0)
+                    both = [lat_weights(substep, r, z, out_slots) for _, r, z, _ in stacked]
+                    first, second = [jnp.concatenate([w[e] for w in both], axis=0) for e in range(2)]
+                    c = jnp.concatenate([ring(out_slots, lambda k: cy[z, k]) for _, _, z, _ in stacked], axis=0)
+                    value = sweep(value, c, first, second, 1)
+                    m = 0
+                    for n_, r, z, _ in stacked:
+                        for slot in out_slots:
+                            part = value[m * COLS : (m + 1) * COLS] * inv[z, slot]
+                            m += 1
+                            if z > 0:
+                                part = part + elim[z, slot] * above[n_, slot]
+                            above[n_, slot] = part
+                            temp[r, slot] = part
+                    stacked = []
             column = {}
             for level in range(LEVELS - 1, -1, -1):
                 for n, tracer in enumerate(members):

time: 72.2 us -> 71.8 us (level)
  no operation moved by 1% of the time
where the time goes in v7:
time: 71.8 us; the launch traced here: 71.7 us
  Pallas kernels  25.4 us (35%)
  waiting for transfers between devices  23 us (32%)
  starting transfers between devices  22.4 us (31%)
  between operations  0.83 us (1%)
    pallas_call x5, Pallas kernels, call(): pl.pallas_call(kernel, out_shape=tuple(outs), in_specs=in_specs, out_spec...  25.4 us
    ppermute x1, waiting for transfers between devices, shards(): south = lax.ppermute(to_north, 'lat', up)  7.74 us
    ppermute x1, starting transfers between devices, shards(): from_right_a = lax.ppermute(left_a, 'lon', west)  6.3 us
    ppermute x1, starting transfers between devices, shards(): north = lax.ppermute(to_south, 'lat', down)  4.81 us
    ppermute x1, waiting for transfers between devices, shards(): corner_l = lax.ppermute(corner, 'lon', east)  4.1 us
    ppermute x1, waiting for transfers between devices, shards(): from_left_2 = lax.ppermute(gr_b, 'lon', east)  3.98 us
    ppermute x1, starting transfers between devices, shards(): from_right_b = lax.ppermute(left_b, 'lon', west)  3.83 us
    ppermute x1, starting transfers between devices, shards(): from_right_2 = lax.ppermute(gl_b, 'lon', west)  3.62 us
  transfers between devices with their start and end apart: 12, of which 6 were waited for; matrix products, arithmetic and copies ran while one was open for 0% of the time, Pallas kernels for 28%

profile of v7, /device:TPU:24, one launch (start us, length us, event | category | flops | bytes accessed | tf_op | source)
XLA Modules:
  0.0 71.7 jit_solution(15368317162560700815)
XLA Ops:
  0.6 0.0 copy-start
  0.6 0.0 copy-start.1
  0.7 0.0 copy-start.2
  0.7 0.0 copy-start.3
  0.7 0.0 copy-start.4
  0.7 0.0 copy-start.5
  0.7 0.0 copy-start.6
  0.7 4.7 %pack.1 = (f32[72,8,256]{2,1,0:T(8,128)}, f32[48,8,256]{2,1,0:T(8,128)}, f32[64,8,256]{2,1,0:T(8,128)}, f32[40,8,256]{2,1,0:T(8,128)}, f32[26,8,128]{2,1,0:T(8,128)}, /*index=5*/f32[26,8,128]{2,1,0:T(8,128)}) custom-call(f32[32,8,256]{2,1,0:T(8,128)} %bitcast.9, f32[8,8,256]{2,1,0:T(8,128)} %refs_1_.7, f32[8,8,256]{2,1,0:T(8,128)} %refs_2_.7, ...), custom_call_target="tpu_custom_call" | custom-call | tf_op jit(solution)/shard_map/pack/pallas_call | solution.py:416
  5.4 6.3 %collective-permute-start.1 = (f32[64,8,256]{2,1,0:T(8,128)}, f32[64,8,256]{2,1,0:T(8,128)S(1)}, u32[]{:S(2)}, u32[]{:S(2)}) collective-permute-start(f32[64,8,256]{2,1,0:T(8,128)} %get-tuple-element.22), channel_id=1, source_target_pairs={{1,0},{2,1},{3,2},{4,3},{5,4},{6,5},{7,6},{8,7},{9,8},{10,9},{11,1... | collective-permute-start | bytes 1572872 | tf_op jit(solution)/shard_map/ppermute | solution.py:454
  11.7 4.8 %collective-permute-start.2 = (f32[26,8,128]{2,1,0:T(8,128)}, f32[26,8,128]{2,1,0:T(8,128)S(1)}, u32[]{:S(2)}, u32[]{:S(2)}) collective-permute-start(f32[26,8,128]{2,1,0:T(8,128)} %get-tuple-element.23), channel_id=1, source_target_pairs={{32,0},{64,32},{96,64},{128,96},{160,128},{192,160},{224,192},{33,... | collective-permute-start | bytes 319496 | tf_op jit(solution)/shard_map/ppermute | solution.py:452
  16.5 2.5 %collective-permute-start.3 = (f32[26,8,128]{2,1,0:T(8,128)}, f32[26,8,128]{2,1,0:T(8,128)S(1)}, u32[]{:S(2)}, u32[]{:S(2)}) collective-permute-start(f32[26,8,128]{2,1,0:T(8,128)} %get-tuple-element.24), channel_id=1, source_target_pairs={{0,32},{32,64},{64,96},{96,128},{128,160},{160,192},{192,224},{1,3... | collective-permute-start | bytes 319496 | tf_op jit(solution)/shard_map/ppermute | solution.py:451
  19.0 0.0 copy-start.8
  19.0 0.0 copy-start.9
  19.1 0.1 collective-permute-start
  19.1 2.0 %collective-permute-done.2.refs_7_.refs_10_ = f32[26,8,128]{2,1,0:T(8,128)S(1)} collective-permute-done((f32[26,8,128]{2,1,0:T(8,128)}, f32[26,8,128]{2,1,0:T(8,128)S(1)}, u32[]{:S(2)}, u32[]{:S(2)}) %collective-permute-start.2) | collective-permute-done | bytes 106528 | tf_op jit(solution)/shard_map/ppermute | solution.py:452
  21.2 7.7 %collective-permute-done.3.refs_8_.refs_11_ = f32[26,8,128]{2,1,0:T(8,128)S(1)} collective-permute-done((f32[26,8,128]{2,1,0:T(8,128)}, f32[26,8,128]{2,1,0:T(8,128)S(1)}, u32[]{:S(2)}, u32[]{:S(2)}) %collective-permute-start.3) | collective-permute-done | bytes 106528 | tf_op jit(solution)/shard_map/ppermute | solution.py:451
  28.9 0.0 copy-done
  28.9 0.0 copy-done.1
  28.9 0.0 copy-done.2
  28.9 0.0 copy-done.3
  29.0 0.0 copy-done.4
  29.0 0.0 copy-done.5
  29.0 0.0 copy-done.6
  29.0 0.1 collective-permute-start.5
  29.1 0.5 collective-permute-start.4
  29.6 2.6 %collective-permute-done.5.refs_13_ = f32[46,8,128]{2,1,0:T(8,128)S(1)} collective-permute-done((f32[46,8,128]{2,1,0:T(8,128)S(1)}, f32[46,8,128]{2,1,0:T(8,128)S(1)}, u32[]{:S(2)}, u32[]{:S(2)}) %collective-permute-start.5) | collective-permute-done | bytes 188448 | tf_op jit(solution)/shard_map/ppermute | solution.py:457
  32.2 4.1 %collective-permute-done.4.refs_12_ = f32[46,8,128]{2,1,0:T(8,128)S(1)} collective-permute-done((f32[46,8,128]{2,1,0:T(8,128)S(1)}, f32[46,8,128]{2,1,0:T(8,128)S(1)}, u32[]{:S(2)}, u32[]{:S(2)}) %collective-permute-start.4) | collective-permute-done | bytes 188448 | tf_op jit(solution)/shard_map/ppermute | solution.py:456
  36.3 0.0 collective-permute-done.1.refs_9_
  36.3 0.0 copy-start.7
  36.3 0.0 copy-done.8
  36.3 0.1 collective-permute-start.6
  36.4 0.0 copy-done.9
  36.4 3.8 %collective-permute-start.7 = (f32[40,8,256]{2,1,0:T(8,128)S(1)}, f32[40,8,256]{2,1,0:T(8,128)S(1)}, u32[]{:S(2)}, u32[]{:S(2)}) collective-permute-start(f32[40,8,256]{2,1,0:T(8,128)S(1)} %copy-done.9), channel_id=1, source_target_pairs={{1,0},{2,1},{3,2},{4,3},{5,4},{6,5},{7,6},{8,7},{9,8},{10,9},{11,1... | collective-permute-start | bytes 983048 | tf_op jit(solution)/shard_map/ppermute | solution.py:462
  40.2 0.0 collective-permute-done.refs_8_
  40.2 0.0 copy-done.7
  40.2 9.7 %window_first.1 = (f32[16,8,256]{2,1,0:T(8,128)S(1)}, f32[16,8,256]{2,1,0:T(8,128)S(1)}, f32[16,8,256]{2,1,0:T(8,128)S(1)}, f32[16,8,256]{2,1,0:T(8,128)S(1)}) custom-call(f32[32,8,256]{2,1,0:T(8,128)S(1)} %bitcast.11, f32[8,8,256]{2,1,0:T(8,128)S(1)} %copy-done.3, f32[8,8,256]{2,1,0:T(8,128)S(1)} %copy-done.4, f32[8,8,256]{2,1,0:T(8,128)S(1)} %copy-done.5, ...), custom_call_target="tpu_custom_call" | custom-call | tf_op jit(solution)/shard_map/window_first/pallas_call | solution.py:416
  49.9 0.1 collective-permute-start.8
  50.0 0.5 collective-permute-start.9
  50.5 0.0 collective-permute-done.7.refs_15_
  50.5 0.0 collective-permute-done.6.refs_14_
  50.5 10.1 %window_second.1 = (f32[32,8,256]{2,1,0:T(8,128)}, f32[16,8,256]{2,1,0:T(8,128)S(1)}, f32[16,8,256]{2,1,0:T(8,128)S(1)}, f32[16,8,256]{2,1,0:T(8,128)S(1)}) custom-call(f32[32,8,256]{2,1,0:T(8,128)S(1)} %bitcast.12, f32[8,8,256]{2,1,0:T(8,128)S(1)} %copy-done.3, f32[8,8,256]{2,1,0:T(8,128)S(1)} %copy-done.4, f32[8,8,256]{2,1,0:T(8,128)S(1)} %copy-done.5, ...), custom_call_target="tpu_custom_call" | custom-call | tf_op jit(solution)/shard_map/window_second/pallas_call | solution.py:416
  60.7 3.6 %collective-permute-start.10 = (f32[16,8,256]{2,1,0:T(8,128)S(1)}, f32[16,8,256]{2,1,0:T(8,128)S(1)}, u32[]{:S(2)}, u32[]{:S(2)}) collective-permute-start(f32[16,8,256]{2,1,0:T(8,128)S(1)} %get-tuple-element.38), channel_id=1, source_target_pairs={{1,0},{2,1},{3,2},{4,3},{5,4},{6,5},{7,6},{8,7},{9,8},{10,9},{11,1... | collective-permute-start | bytes 393224 | tf_op jit(solution)/shard_map/ppermute | solution.py:475
  64.3 0.0 collective-permute-start.11
  64.3 0.0 collective-permute-done.8.refs_1_
  64.3 0.0 collective-permute-done.9.refs_2_
  64.3 2.5 %collective-permute-done.10.refs_4_ = f32[16,8,256]{2,1,0:T(8,128)S(1)} collective-permute-done((f32[16,8,256]{2,1,0:T(8,128)S(1)}, f32[16,8,256]{2,1,0:T(8,128)S(1)}, u32[]{:S(2)}, u32[]{:S(2)}) %collective-permute-start.10) | collective-permute-done | bytes 131104 | tf_op jit(solution)/shard_map/ppermute | solution.py:475
  66.8 4.0 %collective-permute-done.11.refs_5_ = f32[16,8,256]{2,1,0:T(8,128)S(1)} collective-permute-done((f32[16,8,256]{2,1,0:T(8,128)S(1)}, f32[16,8,256]{2,1,0:T(8,128)S(1)}, u32[]{:S(2)}, u32[]{:S(2)}) %collective-permute-start.11) | collective-permute-done | bytes 131104 | tf_op jit(solution)/shard_map/ppermute | solution.py:476
  70.8 0.9 %finish.1 = f32[32,8,256]{2,1,0:T(8,128)} custom-call(f32[16,8,256]{2,1,0:T(8,128)S(1)} %get-tuple-element.34.refs_0_, f32[16,8,256]{2,1,0:T(8,128)S(1)} %collective-permute-done.8.refs_1_, f32[16,8,256]{2,1,0:T(8,128)S(1)} %collective-permute-done.9.refs_2_, f32[16,8,256]{2,1,0:T(8,128)S(1)} %get-tuple-element.37.refs_3_, ...), custom_call_target="tpu_custom_call" | custom-call | tf_op jit(solution)/shard_map/finish/pallas_call | solution.py:416
  (1 shorter events, 0.0 us)
Async XLA Ops:
  0.6 28.3 %copy-start = (s32[4,4,8,8,256]{4,3,2,1,0:T(8,128)S(1)}, s32[4,4,8,8,256]{4,3,2,1,0:T(8,128)}, u32[]{:S(2)}) copy-start(s32[4,4,8,8,256]{4,3,2,1,0:T(8,128)} %param.12) | copy-start | bytes 3145732
  0.6 28.3 %copy-start.1 = (f32[4,8,8,256]{3,2,1,0:T(8,128)S(1)}, f32[4,8,8,256]{3,2,1,0:T(8,128)}, u32[]{:S(2)}) copy-start(f32[4,8,8,256]{3,2,1,0:T(8,128)} %param.8) | copy-start | bytes 786436
  0.7 28.3 %copy-start.2 = (f32[4,4,8,256]{3,2,1,0:T(8,128)S(1)}, f32[4,4,8,256]{3,2,1,0:T(8,128)}, u32[]{:S(2)}) copy-start(f32[4,4,8,256]{3,2,1,0:T(8,128)} %param.14) | copy-start | bytes 393220
  0.7 28.3 %copy-start.3 = (f32[8,8,256]{2,1,0:T(8,128)S(1)}, f32[8,8,256]{2,1,0:T(8,128)}, u32[]{:S(2)}) copy-start(f32[8,8,256]{2,1,0:T(8,128)} %refs_1_.7) | copy-start | bytes 196612
  0.7 28.3 %copy-start.4 = (f32[8,8,256]{2,1,0:T(8,128)S(1)}, f32[8,8,256]{2,1,0:T(8,128)}, u32[]{:S(2)}) copy-start(f32[8,8,256]{2,1,0:T(8,128)} %refs_2_.7) | copy-start | bytes 196612
  0.7 28.3 %copy-start.5 = (f32[8,8,256]{2,1,0:T(8,128)S(1)}, f32[8,8,256]{2,1,0:T(8,128)}, u32[]{:S(2)}) copy-start(f32[8,8,256]{2,1,0:T(8,128)} %refs_3_.7) | copy-start | bytes 196612
  0.7 28.3 %copy-start.6 = (f32[4,8,256]{2,1,0:T(8,128)S(1)}, f32[4,8,256]{2,1,0:T(8,128)}, u32[]{:S(2)}) copy-start(f32[4,8,256]{2,1,0:T(8,128)} %refs_6_.7) | copy-start | bytes 98308
  5.4 30.9 %collective-permute-start.1 = (f32[64,8,256]{2,1,0:T(8,128)}, f32[64,8,256]{2,1,0:T(8,128)S(1)}, u32[]{:S(2)}, u32[]{:S(2)}) collective-permute-start(f32[64,8,256]{2,1,0:T(8,128)} %get-tuple-element.22), channel_id=1, source_target_pairs={{1,0},{2,1},{3,2},{4,3},{5,4},{6,5},{7,6},{8,7},{9,8},{10,9},{11,1... | collective-permute-start | bytes 1572872 | tf_op jit(solution)/shard_map/ppermute | solution.py:454
  11.7 9.5 %collective-permute-start.2 = (f32[26,8,128]{2,1,0:T(8,128)}, f32[26,8,128]{2,1,0:T(8,128)S(1)}, u32[]{:S(2)}, u32[]{:S(2)}) collective-permute-start(f32[26,8,128]{2,1,0:T(8,128)} %get-tuple-element.23), channel_id=1, source_target_pairs={{32,0},{64,32},{96,64},{128,96},{160,128},{192,160},{224,192},{33,... | collective-permute-start | bytes 319496 | tf_op jit(solution)/shard_map/ppermute | solution.py:452
  16.5 12.4 %collective-permute-start.3 = (f32[26,8,128]{2,1,0:T(8,128)}, f32[26,8,128]{2,1,0:T(8,128)S(1)}, u32[]{:S(2)}, u32[]{:S(2)}) collective-permute-start(f32[26,8,128]{2,1,0:T(8,128)} %get-tuple-element.24), channel_id=1, source_target_pairs={{0,32},{32,64},{64,96},{96,128},{128,160},{160,192},{192,224},{1,3... | collective-permute-start | bytes 319496 | tf_op jit(solution)/shard_map/ppermute | solution.py:451
  19.0 17.3 %copy-start.8 = (f32[48,8,256]{2,1,0:T(8,128)S(1)}, f32[48,8,256]{2,1,0:T(8,128)}, u32[]{:S(2)}) copy-start(f32[48,8,256]{2,1,0:T(8,128)} %get-tuple-element.30) | copy-start | bytes 1179652
  19.0 17.4 %copy-start.9 = (f32[40,8,256]{2,1,0:T(8,128)S(1)}, f32[40,8,256]{2,1,0:T(8,128)}, u32[]{:S(2)}) copy-start(f32[40,8,256]{2,1,0:T(8,128)} %get-tuple-element.31) | copy-start | bytes 983044
  19.1 21.2 %collective-permute-start = (f32[72,8,256]{2,1,0:T(8,128)}, f32[72,8,256]{2,1,0:T(8,128)S(1)}, u32[]{:S(2)}, u32[]{:S(2)}) collective-permute-start(f32[72,8,256]{2,1,0:T(8,128)} %get-tuple-element.21), channel_id=1, source_target_pairs={{0,1},{1,2},{2,3},{3,4},{4,5},{5,6},{6,7},{7,8},{8,9},{9,10},{10,1... | collective-permute-start | bytes 1769480 | tf_op jit(solution)/shard_map/ppermute | solution.py:453
  29.0 3.2 %collective-permute-start.5 = (f32[46,8,128]{2,1,0:T(8,128)S(1)}, f32[46,8,128]{2,1,0:T(8,128)S(1)}, u32[]{:S(2)}, u32[]{:S(2)}) collective-permute-start(f32[46,8,128]{2,1,0:T(8,128)S(1)} %join.1), channel_id=1, source_target_pairs={{1,0},{2,1},{3,2},{4,3},{5,4},{6,5},{7,6},{8,7},{9,8},{10,9},{11,1... | collective-permute-start | bytes 565256 | tf_op jit(solution)/shard_map/ppermute | solution.py:457
  29.1 7.2 %collective-permute-start.4 = (f32[46,8,128]{2,1,0:T(8,128)S(1)}, f32[46,8,128]{2,1,0:T(8,128)S(1)}, u32[]{:S(2)}, u32[]{:S(2)}) collective-permute-start(f32[46,8,128]{2,1,0:T(8,128)S(1)} %join.1), channel_id=1, source_target_pairs={{0,1},{1,2},{2,3},{3,4},{4,5},{5,6},{6,7},{7,8},{8,9},{9,10},{10,1... | collective-permute-start | bytes 565256 | tf_op jit(solution)/shard_map/ppermute | solution.py:456
  36.3 3.9 %copy-start.7 = (f32[8]{0:T(128)S(1)}, f32[8]{0:T(128)}, u32[]{:S(2)}) copy-start(f32[8]{0:T(128)} %refs_7_.3) | copy-start | bytes 100
  36.3 14.2 %collective-permute-start.6 = (f32[48,8,256]{2,1,0:T(8,128)S(1)}, f32[48,8,256]{2,1,0:T(8,128)S(1)}, u32[]{:S(2)}, u32[]{:S(2)}) collective-permute-start(f32[48,8,256]{2,1,0:T(8,128)S(1)} %copy-done.8), channel_id=1, source_target_pairs={{0,1},{1,2},{2,3},{3,4},{4,5},{5,6},{6,7},{7,8},{8,9},{9,10},{10,1... | collective-permute-start | bytes 1179656 | tf_op jit(solution)/shard_map/ppermute | solution.py:461
  36.4 14.1 %collective-permute-start.7 = (f32[40,8,256]{2,1,0:T(8,128)S(1)}, f32[40,8,256]{2,1,0:T(8,128)S(1)}, u32[]{:S(2)}, u32[]{:S(2)}) collective-permute-start(f32[40,8,256]{2,1,0:T(8,128)S(1)} %copy-done.9), channel_id=1, source_target_pairs={{1,0},{2,1},{3,2},{4,3},{5,4},{6,5},{7,6},{8,7},{9,8},{10,9},{11,1... | collective-permute-start | bytes 983048 | tf_op jit(solution)/shard_map/ppermute | solution.py:462
  49.9 14.3 %collective-permute-start.8 = (f32[16,8,256]{2,1,0:T(8,128)S(1)}, f32[16,8,256]{2,1,0:T(8,128)S(1)}, u32[]{:S(2)}, u32[]{:S(2)}) collective-permute-start(f32[16,8,256]{2,1,0:T(8,128)S(1)} %get-tuple-element.35), channel_id=1, source_target_pairs={{1,0},{2,1},{3,2},{4,3},{5,4},{6,5},{7,6},{8,7},{9,8},{10,9},{11,1... | collective-permute-start | bytes 393224 | tf_op jit(solution)/shard_map/ppermute | solution.py:469
  50.0 14.2 %collective-permute-start.9 = (f32[16,8,256]{2,1,0:T(8,128)S(1)}, f32[16,8,256]{2,1,0:T(8,128)S(1)}, u32[]{:S(2)}, u32[]{:S(2)}) collective-permute-start(f32[16,8,256]{2,1,0:T(8,128)S(1)} %get-tuple-element.36), channel_id=1, source_target_pairs={{0,1},{1,2},{2,3},{3,4},{4,5},{5,6},{6,7},{7,8},{8,9},{9,10},{10,1... | collective-permute-start | bytes 393224 | tf_op jit(solution)/shard_map/ppermute | solution.py:470
  60.7 6.1 %collective-permute-start.10 = (f32[16,8,256]{2,1,0:T(8,128)S(1)}, f32[16,8,256]{2,1,0:T(8,128)S(1)}, u32[]{:S(2)}, u32[]{:S(2)}) collective-permute-start(f32[16,8,256]{2,1,0:T(8,128)S(1)} %get-tuple-element.38), channel_id=1, source_target_pairs={{1,0},{2,1},{3,2},{4,3},{5,4},{6,5},{7,6},{8,7},{9,8},{10,9},{11,1... | collective-permute-start | bytes 393224 | tf_op jit(solution)/shard_map/ppermute | solution.py:475
  64.3 6.5 %collective-permute-start.11 = (f32[16,8,256]{2,1,0:T(8,128)S(1)}, f32[16,8,256]{2,1,0:T(8,128)S(1)}, u32[]{:S(2)}, u32[]{:S(2)}) collective-permute-start(f32[16,8,256]{2,1,0:T(8,128)S(1)} %get-tuple-element.39), channel_id=1, source_target_pairs={{0,1},{1,2},{2,3},{3,4},{4,5},{5,6},{6,7},{7,8},{8,9},{9,10},{10,1... | collective-permute-start | bytes 393224 | tf_op jit(solution)/shard_map/ppermute | solution.py:476
